TPU v7x, 256 devices: a whole 4x4x8 slice. The times are simulated.
256 devices in a mesh: dp: 4 (over x), expert: 8 (over z), tensor: 8 (over y, core).
Axes of the slice: x: 4, y: 4, z: 8, core: 2. Of those that a mesh axis runs over, the one named last changes fastest.
Arguments:
- tokens: bfloat16 [4096, 6144], P(('dp', 'expert')), may hold values from -6 to 6
- routes: int32 [4096, 2], P(('dp', 'expert')), may hold values from 0 to 7, as said below
- logits: float32 [4096, 2], P(('dp', 'expert')), may hold values from -6.5 to 6.5
- w_gate: bfloat16 [8, 6144, 8192], P('expert', None, ('dp', 'tensor')), may hold values from -0.078125 to 0.078125
- w_up: bfloat16 [8, 6144, 8192], P('expert', None, ('dp', 'tensor')), may hold values from -0.078125 to 0.078125
- w_down: bfloat16 [8, 8192, 6144], P('expert', ('dp', 'tensor')), may hold values from -0.0625 to 0.0625
Outputs:
- mixed: bfloat16 [4096, 6144], P(('dp', 'expert'), 'tensor')
Inputs may be any that keep to these rules, and one draw needn't show every extreme that they name: `routes`: each row names two different experts. In each aligned block of 128 rows (the rows of one data shard) every expert is named, none more than 40 times, and five or six experts exactly 40 times.
All inputs are finite; a program needn't handle non-finite values.
Results may differ from a plain program's by a relative error of at most 0.025.
Values may be sent and summed in bfloat16 or wider, within the bound.
No kernel may reach another device: no remote copies, remote signals or barrier semaphores. Data moves between devices by JAX's collectives and lax.ppermute only.
A program may use at most 128 MiB of HBM per device.

v0:
```python
import jax
import jax.numpy as jnp
from jax import lax
from jax.sharding import PartitionSpec as P

E = 8
CAP = 40


def body(tokens, routes, logits, w_gate, w_up, w_down):
    token_rows = tokens.shape[0]
    model_width = tokens.shape[1]
    local_experts = w_gate.shape[0]
    expert_devices = lax.axis_size("expert")
    expert_ids = routes.reshape(-1)
    onehot = (expert_ids[:, None] == jnp.arange(E, dtype=jnp.int32)[None, :]).astype(jnp.int32)
    before = jnp.cumsum(onehot, axis=0) - onehot
    slot_index = jnp.sum(before * onehot, axis=1)
    target = slot_index * E + expert_ids
    placing = (jnp.arange(CAP * E, dtype=jnp.int32)[:, None] == target[None, :]).astype(jnp.int32)
    placing = jnp.sum(placing.reshape(CAP * E, token_rows, 2), axis=2).astype(jnp.bfloat16)
    outgoing = jnp.dot(placing, tokens, preferred_element_type=jnp.float32).astype(jnp.bfloat16)
    outgoing = outgoing.reshape(CAP, expert_devices, local_experts, model_width)
    arrived = lax.all_to_all(outgoing, "expert", split_axis=1, concat_axis=1, tiled=True)
    piece = lax.all_gather(arrived, "dp", axis=0, tiled=True)
    gate = jnp.einsum("rsed,edf->rsef", piece, w_gate, preferred_element_type=jnp.float32)
    upper = jnp.einsum("rsed,edf->rsef", piece, w_up, preferred_element_type=jnp.float32)
    hidden = (jax.nn.silu(gate) * upper).astype(jnp.bfloat16)
    summed = lax.psum_scatter(
        jnp.einsum("rsef,efd->rsed", hidden, w_down, preferred_element_type=jnp.float32).astype(
            jnp.bfloat16
        ),
        ("dp", "tensor"),
        scatter_dimension=0,
        tiled=True,
    )
    gathered = lax.all_to_all(
        lax.all_to_all(summed, "expert", split_axis=1, concat_axis=1, tiled=True),
        "tensor",
        split_axis=3,
        concat_axis=0,
        tiled=True,
    )
    table = gathered.reshape(CAP * E, gathered.shape[3])
    picked = (
        jnp.take(table, target, axis=0)
        .astype(jnp.float32)
        .reshape(token_rows, 2, gathered.shape[3])
    )
    share = jax.nn.sigmoid(logits - logits[:, ::-1])
    return jnp.sum(picked * share[:, :, None], axis=1).astype(jnp.bfloat16)


def solution(mesh):
    placed = (
        P(("dp", "expert"), None),
        P(("dp", "expert"), None),
        P(("dp", "expert"), None),
        P("expert", None, ("dp", "tensor")),
        P("expert", None, ("dp", "tensor")),
        P("expert", ("dp", "tensor"), None),
    )
    return jax.shard_map(
        body, mesh=mesh, in_specs=placed, out_specs=P(("dp", "expert"), "tensor"), check_vma=False
    )
```

profile of v0, /device:TPU:24, one launch (start us, length us, event | category | flops | bytes accessed | tf_op | source)
XLA Modules:
  0.0 515.4 jit_solution(17498324330411987440)
XLA Ops:
  6.5 0.0 copy-start
  6.5 0.0 all-gather.2.cloned.1.call-start
  6.5 0.9 copy.38
  7.5 0.1 eq.43
  7.6 0.1 eq.39
  7.8 0.6 reduce-window.6
  8.4 0.2 slice_reduce_fusion
  8.6 0.1 fusion.35
  8.7 0.1 mul.47
  8.9 0.1 copy.40
  8.9 0.7 compare_and_fusion
  9.7 2.6 fusion.4
  12.3 2.2 copy.42
  14.4 98.8 %all_to_all.25 = bf16[40,8,1,6144]{3,0,2,1:T(8,128)(2,1)S(1)} all-to-all(bf16[40,8,1,6144]{3,0,2,1:T(8,128)(2,1)S(1)} %copy.42), channel_id=1, replica_groups=mesh['dp'=4,'expert'=8,'tensor'=8] {'expert'}, dimensions={1} | all-to-all | bytes 7864320 | tf_op jit(solution)/shard_map/all_to_all | solution.py:24
  113.2 4.0 copy.43
  117.3 0.0 all-gather.2.cloned.1.call-update
  117.3 0.2 reduce-scatter.2.cloned.1.call-start
  117.5 143.8 %all-gather.2.cloned.1.call-done = bf16[160,8,1,6144]{3,1,2,0:T(8,128)(2,1)} async-done(((bf16[40,8,1,6144]{3,1,2,0:T(8,128)(2,1)}), bf16[160,8,1,6144]{3,1,2,0:T(8,128)(2,1)}) %all-gather.2.cloned.1.call-update) | async-done | bytes 15728656 | tf_op jit(solution)/shard_map/all_gather | solution.py:25
  261.3 11.7 %fusion.8 = f32[160,8,1,256]{3,1,0,2:T(8,128)} fusion(bf16[1,6144,256]{2,1,0:T(8,128)(2,1)} %param.9, bf16[160,8,1,6144]{3,1,2,0:T(8,128)(2,1)} %all-gather.2.cloned.1.call-done), kind=kOutput, calls=%fused_computation.11 | convolution fusion | flops 4026531840 | bytes 20185088 | tf_op jit(solution)/shard_map/rsed,edf->rsef/dot_general | solution.py:26
  273.0 12.0 %fusion.28 = bf16[160,8,256]{2,1,0:T(8,128)(2,1)} fusion(bf16[1,6144,256]{2,1,0:T(8,128)(2,1)} %param.10, bf16[160,8,1,6144]{3,1,2,0:T(8,128)(2,1)} %all-gather.2.cloned.1.call-done, f32[160,8,1,256]{3,1,0,2:T(8,128)} %fusion.8), kind=kOutput, calls=%fused_computation.15 | convolution fusion | flops 4028497920 | bytes 20840448 | tf_op jit(solution)/shard_map/rsed,edf->rsef/dot_general | solution.py:27
  285.0 0.0 copy-done
  285.0 8.8 %convert_bitcast_fusion = bf16[160,8,1,6144]{3,1,0,2:T(8,128)(2,1)} fusion(bf16[160,8,256]{2,1,0:T(8,128)(2,1)} %fusion.28, bf16[1,256,6144]{2,1,0:T(8,128)(2,1)S(1)} %copy-done), kind=kOutput, calls=%fused_computation.5 | convolution fusion | flops 4034396160 | bytes 19529728 | tf_op jit(solution)/shard_map/rsef,efd->rsed/dot_general | solution.py:30
  293.7 0.0 copy-start.2
  293.7 0.0 reduce-scatter.2.cloned.1.call-update
  293.8 121.4 %reduce-scatter.2.cloned.1.call-done = bf16[5,8,1,6144]{3,1,0,2:T(8,128)(2,1)} async-done(((bf16[160,8,1,6144]{3,1,0,2:T(8,128)(2,1)}), bf16[5,8,1,6144]{3,1,0,2:T(8,128)(2,1)}) %reduce-scatter.2.cloned.1.call-update) | async-done | bytes 491536 | tf_op jit(solution)/shard_map/reduce_scatter | solution.py:29
  415.2 2.2 copy.44
  417.4 7.0 %all-to-all-start.1 = ((bf16[5,8,1,6144]{3,0,2,1:T(8,128)(2,1)}), bf16[5,8,1,6144]{3,0,2,1:T(8,128)(2,1)S(1)}, u32[]{:S(2)}, u32[]{:S(2)}) async-start(bf16[5,8,1,6144]{3,0,2,1:T(8,128)(2,1)} %copy.44), calls=%async_computation.2 | async-start | bytes 1572864 | tf_op jit(solution)/shard_map/all_to_all | solution.py:38
  424.4 0.0 copy-done.2
  424.5 21.6 %all-to-all-done.1 = bf16[5,8,1,6144]{3,0,2,1:T(8,128)(2,1)S(1)} async-done(((bf16[5,8,1,6144]{3,0,2,1:T(8,128)(2,1)}), bf16[5,8,1,6144]{3,0,2,1:T(8,128)(2,1)S(1)}, u32[]{:S(2)}, u32[]{:S(2)}) %all-to-all-start.1) | async-done | bytes 491552 | tf_op jit(solution)/shard_map/all_to_all | solution.py:38
  446.0 10.0 %copy.45 = bf16[5,8,1,6144]{1,0,2,3:T(8,128)(2,1)} copy(bf16[5,8,1,6144]{3,0,2,1:T(8,128)(2,1)S(1)} %all-to-all-done.1) | data formatting | bytes 983040 | tf_op jit(solution)/shard_map/all_to_all | solution.py:38
  456.1 11.8 %reshape.130 = bf16[8,2,15360]{2,1,0:T(2,128)(2,1)} reshape(bf16[6144,1,5,8]{3,2,1,0:T(8,128)(2,1)} %bitcast.83) | data formatting | bytes 983040
  467.9 4.7 all-to-all-start.2
  472.5 0.1 reshape.117
  472.7 0.1 copy.41
  472.8 0.7 copy.48
  473.6 6.9 %all-to-all-done.2 = bf16[8,2,15360]{2,1,0:T(2,128)(2,1)S(1)} async-done(((bf16[8,2,15360]{2,1,0:T(2,128)(2,1)}), bf16[8,2,15360]{2,1,0:T(2,128)(2,1)S(1)}, u32[]{:S(2)}, u32[]{:S(2)}) %all-to-all-start.2) | async-done | bytes 491552 | tf_op jit(solution)/shard_map/all_to_all | solution.py:37
  480.4 9.6 %reshape.131 = bf16[6144,1,5,8]{3,2,1,0:T(8,128)(2,1)} reshape(bf16[8,2,15360]{2,1,0:T(2,128)(2,1)S(1)} %all-to-all-done.2) | data formatting | bytes 983040
  490.0 0.0 copy-start.1
  490.0 11.3 %copy.46 = bf16[5,8,1,8,768]{4,1,0,3,2:T(8,128)(2,1)} copy(bf16[5,8,1,8,768]{1,0,4,3,2:T(8,128)(2,1)} %bitcast.84) | data formatting | bytes 983040 | tf_op jit(solution)/shard_map/all_to_all | solution.py:37
  501.4 3.2 gather_fusion
  504.6 1.1 gather.7
  505.7 2.8 multiply_reduce_fusion
  508.5 0.0 copy-done.1
  (9 shorter events, 0.1 us)
Async XLA Ops:
  6.5 278.4 %copy-start = (bf16[1,256,6144]{2,1,0:T(8,128)(2,1)S(1)}, bf16[1,256,6144]{2,1,0:T(8,128)(2,1)}, u32[]{:S(2)}) copy-start(bf16[1,256,6144]{2,1,0:T(8,128)(2,1)} %param.11) | copy-start | bytes 9437188
  6.5 254.7 %all-gather.2.cloned.1.call-start = ((), (), s32[]{:S(2)}) async-start(), calls=%async_computation.4 | async-start | bytes 19660800 | tf_op jit(solution)/shard_map/all_gather | solution.py:25
  117.3 297.9 %reduce-scatter.2.cloned.1.call-start = ((), (), s32[]{:S(2)}) async-start(), calls=%async_computation.5 | async-start | bytes 16220160 | tf_op jit(solution)/shard_map/reduce_scatter | solution.py:29
  293.7 130.7 %copy-start.2 = (f32[128,2]{0,1:T(2,128)S(1)}, f32[128,2]{0,1:T(2,128)}, u32[]{:S(2)}) copy-start(f32[128,2]{0,1:T(2,128)} %param.8) | copy-start | bytes 3076
  417.4 28.6 %all-to-all-start.1 = ((bf16[5,8,1,6144]{3,0,2,1:T(8,128)(2,1)}), bf16[5,8,1,6144]{3,0,2,1:T(8,128)(2,1)S(1)}, u32[]{:S(2)}, u32[]{:S(2)}) async-start(bf16[5,8,1,6144]{3,0,2,1:T(8,128)(2,1)} %copy.44), calls=%async_computation.2 | async-start | bytes 1572864 | tf_op jit(solution)/shard_map/all_to_all | solution.py:38
  467.9 12.6 %all-to-all-start.2 = ((bf16[8,2,15360]{2,1,0:T(2,128)(2,1)}), bf16[8,2,15360]{2,1,0:T(2,128)(2,1)S(1)}, u32[]{:S(2)}, u32[]{:S(2)}) async-start(bf16[8,2,15360]{2,1,0:T(2,128)(2,1)} %reshape.130), calls=%async_computation.3 | async-start | bytes 983040 | tf_op jit(solution)/shard_map/all_to_all | solution.py:37
  490.0 18.5 %copy-start.1 = (bf16[1,256,6144]{2,1,0:T(8,128)(2,1)S(1)}, bf16[1,256,6144]{2,1,0:T(8,128)(2,1)}, u32[]{:S(2)}) copy-start(bf16[1,256,6144]{2,1,0:T(8,128)(2,1)} %param.11) | copy-start | bytes 9437188
Sparse Core Ops, SparseCore 0:
  117.4 143.8 all-gather.1
  293.9 121.2 reduce-scatter.1
where the time goes:
time: 519 us; the launch traced here: 515 us
  waiting for transfers between devices  294 us (57%)
  blocking collectives  98.8 us (19%)
  local copies, waits for them, and re-layouts  58.2 us (11%)
  matrix products  35 us (7%)
  between operations  13.5 us (3%)
  starting transfers between devices  11.9 us (2%)
    all_gather x1, waiting for transfers between devices, body(): piece = lax.all_gather(arrived, 'dp', axis=0, tiled=True)  144 us
    reduce_scatter x1, waiting for transfers between devices, body(): lax.psum_scatter(jnp.einsum('rsef,efd->rsed', hidden, w_down, preferred_e...  121 us
    all_to_all x1, blocking collectives, body(): lax.all_to_all(outgoing, 'expert', split_axis=1, concat_axis=1, tiled=True)  98.8 us
    unnamed x9, local copies, waits for them, and re-layouts  22.3 us
    all_to_all x1, waiting for transfers between devices, body(): lax.all_to_all(summed, 'expert', split_axis=1, concat_axis=1, tiled=True)  21.6 us
    dot_general x1, matrix products, body(): jnp.einsum('rsed,edf->rsef', piece, w_up, preferred_element_type=jnp.floa...  12 us
    dot_general x1, matrix products, body(): jnp.einsum('rsed,edf->rsef', piece, w_gate, preferred_element_type=jnp.fl...  11.7 us
    all_to_all x1, local copies, waits for them, and re-layouts, body(): lax.all_to_all(lax.all_to_all(summed, 'expert', split_axis=1, concat_axis...  11.3 us
  transfers between devices with their start and end apart: 4, of which 4 were waited for; matrix products, arithmetic and copies ran while one was open for 0% of the time, Pallas kernels for 0%

commit v1 on v0

v1 whole, which is shorter than its diff:
```python
import functools

import jax
import jax.numpy as jnp
import numpy as np
from jax import lax
from jax.experimental import pallas as pl
from jax.experimental.pallas import tpu as pltpu
from jax.sharding import Mesh, PartitionSpec as P

E = 8
CAP = 40
BF = jnp.bfloat16
F32 = jnp.float32
OFFSETS = (0, -1, 1, 2)
ROUTES = ((0, 4), (1, -1), (2, -2), (3, -3))
MIB = 2**20
VMEM = pl.BlockSpec(memory_space=pltpu.VMEM)
SMEM = pl.BlockSpec(memory_space=pltpu.SMEM)
ANY = pl.BlockSpec(memory_space=pl.ANY)
HBM = pl.BlockSpec(memory_space=pltpu.HBM)
COST = pl.CostEstimate(flops=MIB, bytes_accessed=MIB, transcendentals=0)


def dot(p, q):
    return jnp.dot(p, q, preferred_element_type=F32)


def add(*values):
    return sum(v.astype(F32) for v in values).astype(BF)


def plane(value, phase, step):
    pairs = []
    for x in range(4):
        for y in range(4):
            for c in range(2):
                along_x = (c == 0) == (phase == 0)
                to = ((x + step) % 4, y) if along_x else (x, (y + step) % 4)
                pairs.append(((x * 4 + y) * 2 + c, (to[0] * 4 + to[1]) * 2 + c))
    return lax.ppermute(value, ("dp", "ty", "core"), pairs)


def along_z(value, j):
    pairs = [(z * 4 + y, (z + ROUTES[y][j]) % 8 * 4 + y) for z in range(8) for y in range(4)]
    return lax.ppermute(value, ("expert", "ty"), pairs)


def swap(value):
    return lax.ppermute(value, "core", [(0, 1), (1, 0)])


def after(value, *others):
    return pl.pallas_call(
        lambda *refs: None,
        in_specs=[ANY] * (1 + len(others)),
        out_specs=ANY,
        out_shape=jax.ShapeDtypeStruct(value.shape, value.dtype),
        input_output_aliases={0: 0},
        compiler_params=pltpu.CompilerParams(vmem_limit_bytes=MIB),
        cost_estimate=COST,
    )(value, *others)


def gate_up_kernel(pieces, scalars, *refs):
    rows, weights = refs[:pieces], refs[pieces : pieces + 4]
    out, held, weight, row_sems, sems = refs[-5:]
    depth, step = weight.shape[1:]
    at, row_copies = 0, []
    for i, ref in enumerate(rows):
        count = ref.shape[0]
        row_copies.append(pltpu.make_async_copy(ref, held.at[pl.ds(at, count)], row_sems.at[i]))
        at += count
    start = pl.multiple_of(scalars[20] * depth, depth)
    copies = [
        pltpu.make_async_copy(ref.at[pl.ds(start, depth)], weight.at[i], sems.at[i])
        for i, ref in enumerate(weights)
    ]
    for copy in row_copies + copies:
        copy.start()
    for copy in row_copies:
        copy.wait()

    @pl.loop(0, 4)
    def _(n):
        pltpu.make_async_copy(weights[0].at[pl.ds(start, depth)], weight.at[n], sems.at[n]).wait()
        value = dot(held[...], weight[n])
        column = pl.multiple_of(n * step, step)
        for i in range(out.shape[0]):
            block = value[i * out.shape[1] : (i + 1) * out.shape[1]]
            out[i, :, pl.ds(column, step)] = block.astype(BF)


def gate_up(rows, weights, scalars):
    count = sum(r.shape[0] for r in rows)
    depth, step = weights[0].shape
    depth //= 2
    block = 2 * CAP
    return pl.pallas_call(
        functools.partial(gate_up_kernel, len(rows)),
        in_specs=[SMEM] + [ANY] * len(rows) + [HBM] * 4,
        out_specs=VMEM,
        out_shape=jax.ShapeDtypeStruct((count // block, block, 4 * step), BF),
        scratch_shapes=[
            pltpu.VMEM((count, depth), BF),
            pltpu.VMEM((4, depth, step), BF),
            pltpu.SemaphoreType.DMA((len(rows),)),
            pltpu.SemaphoreType.DMA((4,)),
        ],
        compiler_params=pltpu.CompilerParams(vmem_limit_bytes=24 * MIB),
        cost_estimate=COST,
    )(scalars, *rows, *weights)


def down_copies(scalars, mine, theirs, down, sems, count=4):
    units, part = mine.shape[0], down.shape[2]
    copies = []
    for k in range(count):
        start = pl.multiple_of((2 * scalars[16 + k] + scalars[20]) * part, part)
        for side, ref in enumerate((mine, theirs)):
            copies.append(
                pltpu.make_async_copy(
                    ref.at[:, pl.ds(start, part)],
                    down.at[k, pl.ds(side * units, units)],
                    sems.at[2 * k + side],
                )
            )
    return copies


def hidden_kernel(
    scalars, sums, got, mine, theirs, hidden, far_a, far_b, down, sems
):
    copies = down_copies(scalars, mine, theirs, down, sems)
    for copy in copies:
        copy.start()
    units = hidden.shape[1] // 2
    rows = hidden.shape[0] // 4
    block = rows // 4
    for i in range(4):
        for j in range(4):
            start = pl.multiple_of(scalars[4 * i + j] * block, 16)
            here, there = sums[4 * i + j].astype(F32), got[4 * j + i].astype(F32)
            for side in range(2):
                at, other = 2 * units * side, 2 * units * (1 - side)
                gate = here[:, at : at + units] + there[:, other : other + units]
                upper = here[:, at + units : at + 2 * units]
                upper = upper + there[:, other + units : other + 2 * units]
                value = gate / (1.0 + jnp.exp(-gate)) * upper
                hidden[pl.ds(start, block), side * units : (side + 1) * units] = value.astype(BF)
    outs = (far_a.at[0], far_a.at[1], far_b.at[0], far_b.at[1])
    for copy in copies:
        copy.wait()

    @pl.when(scalars[20] == 0)
    def _():
        for k in range(4):
            outs[k][...] = dot(hidden[3 * rows :, :], down[k]).astype(BF)

    @pl.when(scalars[20] == 1)
    def _():
        value = dot(hidden[...], down[3]).astype(BF)
        for r in range(4):
            outs[r][...] = value[r * rows : (r + 1) * rows]


def hidden_of(sums, got, mine, theirs, scalars):
    rows, units = sums.shape[0] * sums.shape[1], 2 * mine.shape[0]
    part = mine.shape[1] // 8
    piece = jax.ShapeDtypeStruct((2, rows // 4, part), BF)
    return pl.pallas_call(
        hidden_kernel,
        in_specs=[SMEM] + [VMEM] * 2 + [HBM] * 2,
        out_specs=[VMEM] * 3,
        out_shape=[jax.ShapeDtypeStruct((rows, units), BF), piece, piece],
        scratch_shapes=[pltpu.VMEM((4, units, part), BF), pltpu.SemaphoreType.DMA((8,))],
        compiler_params=pltpu.CompilerParams(vmem_limit_bytes=20 * MIB),
        cost_estimate=COST,
    )(scalars, sums, got, mine, theirs)


def down_kernel(
    scalars, hidden, mine, theirs, below_a, below_b, above_a, above_b, own, down, sems
):
    copies = down_copies(scalars, mine, theirs, down, sems)
    for copy in copies:
        copy.start()
    for copy in copies:
        copy.wait()
    rows = hidden.shape[0] // 4
    outs = (
        (own.at[0], own.at[1], own.at[2], own.at[3]),
        (below_a.at[0], below_a.at[1], below_b.at[0], below_b.at[1]),
        (above_a.at[0], above_a.at[1], above_b.at[0], above_b.at[1]),
    )

    @pl.when(scalars[20] == 0)
    def _():
        for k in range(4):
            value = dot(hidden[: 3 * rows, :], down[k]).astype(BF)
            for r in range(3):
                outs[r][k][...] = value[r * rows : (r + 1) * rows]

    @pl.when(scalars[20] == 1)
    def _():
        for k in range(3):
            value = dot(hidden[...], down[k]).astype(BF)
            for r in range(4):
                outs[k][r][...] = value[r * rows : (r + 1) * rows]


def down_of(hidden, mine, theirs, scalars):
    rows, units = hidden.shape
    part = mine.shape[1] // 8
    return pl.pallas_call(
        down_kernel,
        in_specs=[SMEM, VMEM, HBM, HBM],
        out_specs=[VMEM] * 5,
        out_shape=[jax.ShapeDtypeStruct((s, rows // 4, part), BF) for s in (2, 2, 2, 2, 4)],
        scratch_shapes=[pltpu.VMEM((4, units, part), BF), pltpu.SemaphoreType.DMA((8,))],
        compiler_params=pltpu.CompilerParams(vmem_limit_bytes=20 * MIB),
        cost_estimate=COST,
    )(scalars, hidden, mine, theirs)


def body(tokens, routes, logits, w_gate, w_up, w_down):
    rows, width = tokens.shape
    half = width // 2
    part = half // 4
    y, c, z = lax.axis_index("ty"), lax.axis_index("core"), lax.axis_index("expert")

    expert_ids = routes.reshape(-1)
    onehot = (expert_ids[:, None] == jnp.arange(E, dtype=jnp.int32)[None, :]).astype(jnp.int32)
    before = jnp.cumsum(onehot, axis=0) - onehot
    slot_index = jnp.sum(before * onehot, axis=1)
    target = (expert_ids * CAP + slot_index).reshape(rows, 2)
    columns = lax.dynamic_slice_in_dim(tokens, c * half, half, 1)
    slots = jnp.arange(CAP, dtype=jnp.int32)

    def outgoing(j):
        step = jnp.int32(ROUTES[0][j])
        for line in range(1, 4):
            step = jnp.where(y == line, ROUTES[line][j], step)
        places = (z + step + 8) % 8 * CAP + slots
        hit = places[:, None, None] == target[None, :, :]
        return dot(jnp.any(hit, axis=2).astype(BF), columns).astype(BF)

    w_gate, w_up, w_down = w_gate[0], w_up[0], w_down[0]
    weights = [w_gate, w_up, swap(w_gate), swap(w_up)]
    downs = [w_down, swap(w_down)]
    arrived = [along_z(outgoing(j), j) for j in range(2)]
    piece = after(jnp.concatenate(arrived, axis=0), *weights[2:], downs[1])

    lines = [(y + o + 4) % 4 for o in OFFSETS]
    place = [jnp.where(c == 0, j * 4 + lines[i], i * 4 + lines[j]) for i in range(4) for j in range(4)]
    scalars = jnp.stack(place + lines + [c] + [jnp.int32(0)] * 3).astype(jnp.int32)

    low = jnp.concatenate([piece, plane(piece, 0, 1)], axis=0)
    high = jnp.concatenate([plane(piece, 0, -1), plane(piece, 0, 2)], axis=0)
    below_low, above_high = plane(low, 1, 1), plane(high, 1, -1)
    below_high, above_low = plane(high, 1, 1), plane(low, 1, -1)
    far = [plane(below_low, 1, 1), plane(above_high, 1, -1)]
    rows_all = [low, high, below_low, below_high, above_low, above_high, *far]
    sums = gate_up(rows_all, weights, scalars)
    hidden, far_a, far_b = hidden_of(sums, swap(sums), *downs, scalars)
    below_a, below_b, above_a, above_b, own = down_of(hidden, *downs, scalars)

    from_below, from_above = plane(far_a, 0, 1), plane(far_b, 0, -1)
    got_high, got_low = plane(above_b, 0, 1), plane(below_a, 0, -1)
    got_low2 = plane(add(above_a, from_below), 0, 1)
    got_high2 = plane(add(below_b, from_above), 0, -1)
    mid = [add(own[i], got_low[i], got_low2[i]) for i in range(2)]
    mid += [add(own[2 + i], got_high[i], got_high2[i]) for i in range(2)]
    ends = [mid[0], plane(mid[1], 1, -1), plane(mid[2], 1, 1), plane(mid[3], 1, 2)]
    moved = []
    for step in range(0, -8, -1):
        [found] = [(i, j) for i in range(4) for j in range(2) if (ROUTES[i][j] - step) % 8 == 0]
        at = (2 * found[0] + found[1]) * CAP
        moved.append(add(*[e[at : at + CAP] for e in ends]))
    moved = jnp.concatenate(moved * 2, axis=0).reshape(2 * E, CAP, part)
    moved = lax.dynamic_slice_in_dim(moved, (E - z) % E, E, 0)
    table = lax.all_to_all(moved, "expert", 0, 0, tiled=True).reshape(E * CAP, part)

    share = jax.nn.sigmoid(logits - logits[:, ::-1])
    hit = jnp.arange(E * CAP, dtype=jnp.int32)[None, :, None] == target[:, None, :]
    mix = jnp.sum(jnp.where(hit, share[:, None, :], 0.0), axis=2)
    high_mix = mix.astype(BF)
    low_mix = (mix - high_mix.astype(F32)).astype(BF)
    return (dot(high_mix, table) + dot(low_mix, table)).astype(BF)


def solution(mesh):
    grid = Mesh(mesh.devices.reshape(4, 8, 4, 2), ("dp", "expert", "ty", "core"))
    tensor = ("ty", "core")
    placed = (
        P(("dp", "expert"), None),
        P(("dp", "expert"), None),
        P(("dp", "expert"), None),
        P("expert", None, ("dp",) + tensor),
        P("expert", None, ("dp",) + tensor),
        P("expert", ("dp",) + tensor, None),
    )
    return jax.shard_map(
        body, mesh=grid, in_specs=placed, out_specs=P(("dp", "expert"), tensor), check_vma=False
    )
```

time: 519 us -> 193 us (0.37)
  waiting for transfers between devices: 294 us -> 121 us
  blocking collectives: 98.8 us -> 0 us
  local copies, waits for them, and re-layouts: 58.2 us -> 6.35 us
  matrix products: 35 us -> 1.75 us
  starting transfers between devices: 11.9 us -> 36.5 us
  Pallas kernels: 0 us -> 22.2 us
  between operations: 13.5 us -> 0.4 us
    all_gather x1 -> x0, waiting for transfers between devices: 144 us -> none  [body(): piece = lax.all_gather(arrived, 'dp', axis=0, tiled=True)]
    reduce_scatter x1 -> x0, waiting for transfers between devices: 121 us -> none  [body(): lax.psum_scatter(jnp.einsum('rsef,efd->rsed', hidden, w_down, preferred_e...]
    ppermute x0 -> x24, waiting for transfers between devices: none -> 106 us  [the longest x18 82.5 us: plane(): return lax.ppermute(value, ('dp', 'ty', 'core'), pairs)]
    all_to_all x1 -> x0, blocking collectives: 98.8 us -> none  [body(): lax.all_to_all(outgoing, 'expert', split_axis=1, concat_axis=1, tiled=True)]
    dot_general x4, matrix products: 35 us -> 1.75 us  [dot(): return jnp.dot(p, q, preferred_element_type=F32)]
    ppermute x0 -> x24, starting transfers between devices: none -> 28.9 us  [the longest x18 19.5 us: plane(): return lax.ppermute(value, ('dp', 'ty', 'core'), pairs)]
    all_to_all x3 -> x0, local copies, waits for them, and re-layouts: 25.4 us -> none  [the longest x1 11.3 us: body(): lax.all_to_all(lax.all_to_all(summed, 'expert', split_axis=1, concat_axis...]
    pallas_call x0 -> x4, Pallas kernels: none -> 22.2 us  [the longest x1 12.8 us: gate_up(): pl.pallas_call(functools.partial(gate_up_kernel, len(rows)), in_specs=[SM...]
  transfers between devices with their start and end apart: 4 -> 25, of which waited for: 4 -> 19; matrix products, arithmetic and copies ran while one was open for 0% -> 2% of each run, Pallas kernels for 0% -> 3%
where the time goes in v1:
time: 193 us; the launch traced here: 192 us
  waiting for transfers between devices  121 us (63%)
  starting transfers between devices  36.5 us (19%)
  Pallas kernels  22.2 us (12%)
  local copies, waits for them, and re-layouts  6.35 us (3%)
  other arithmetic  4.27 us (2%)
    ppermute x18, waiting for transfers between devices, plane(): return lax.ppermute(value, ('dp', 'ty', 'core'), pairs)  82.5 us
    ppermute x18, starting transfers between devices, plane(): return lax.ppermute(value, ('dp', 'ty', 'core'), pairs)  19.5 us
    ppermute x2, waiting for transfers between devices, along_z(): return lax.ppermute(value, ('expert', 'ty'), pairs)  18.1 us
    all_to_all x1, waiting for transfers between devices, body(): lax.all_to_all(moved, 'expert', 0, 0, tiled=True).reshape(E * CAP, part)  15 us
    pallas_call x1, Pallas kernels, gate_up(): pl.pallas_call(functools.partial(gate_up_kernel, len(rows)), in_specs=[SM...  12.8 us
    ppermute x2, starting transfers between devices, along_z(): return lax.ppermute(value, ('expert', 'ty'), pairs)  8.74 us
    all_to_all x1, starting transfers between devices, body(): lax.all_to_all(moved, 'expert', 0, 0, tiled=True).reshape(E * CAP, part)  7.58 us
    pallas_call x1, Pallas kernels, down_of(): pl.pallas_call(down_kernel, in_specs=[SMEM, VMEM, HBM, HBM], out_specs=[V...  5.49 us
  transfers between devices with their start and end apart: 25, of which 19 were waited for; matrix products, arithmetic and copies ran while one was open for 2% of the time, Pallas kernels for 3%

profile of v1, /device:TPU:24, one launch (start us, length us, event | category | flops | bytes accessed | tf_op | source)
XLA Modules:
  0.0 192.0 jit_solution(9425856246989427845)
XLA Ops:
  0.0 0.5 collective-permute-start.2
  0.5 0.1 collective-permute-start.3
  0.6 0.8 copy.22
  1.4 0.1 eq.105
  1.5 0.1 eq.51
  1.7 0.6 reduce-window.6
  2.3 0.2 slice_reduce_fusion
  2.6 0.1 fusion.34
  2.6 0.1 reduce_sum.21
  2.9 0.7 multiply_add_fusion
  3.6 0.1 compare_reduce_fusion.1
  3.7 0.2 convolution_convert_fusion.1
  3.9 6.5 %collective-permute-start = (bf16[40,3072]{1,0:T(8,128)(2,1)S(1)}, bf16[40,3072]{1,0:T(8,128)(2,1)S(1)}, u32[]{:S(2)}, u32[]{:S(2)}) collective-permute-start(bf16[40,3072]{1,0:T(8,128)(2,1)S(1)} %convolution_convert_fusion.1), channel_id=1, source_target_pairs={{0,0},{2,10},{4,20},{6,30},{8,8},{10,18},{12,28},{14,38},{16,16},{... | collective-permute-start | bytes 737288 | tf_op jit(solution)/shard_map/ppermute | solution.py:46
  10.5 0.2 convolution_convert_fusion
  10.7 2.2 %collective-permute-start.1 = (bf16[40,3072]{1,0:T(8,128)(2,1)S(1)}, bf16[40,3072]{1,0:T(8,128)(2,1)S(1)}, u32[]{:S(2)}, u32[]{:S(2)}) collective-permute-start(bf16[40,3072]{1,0:T(8,128)(2,1)S(1)} %convolution_convert_fusion), channel_id=1, source_target_pairs={{0,32},{2,58},{4,52},{6,46},{8,40},{10,2},{12,60},{14,54},{16,48},... | collective-permute-start | bytes 737288 | tf_op jit(solution)/shard_map/ppermute | solution.py:46
  12.9 16.0 %collective-permute-done = bf16[40,3072]{1,0:T(8,128)(2,1)S(1)} collective-permute-done((bf16[40,3072]{1,0:T(8,128)(2,1)S(1)}, bf16[40,3072]{1,0:T(8,128)(2,1)S(1)}, u32[]{:S(2)}, u32[]{:S(2)}) %collective-permute-start) | collective-permute-done | bytes 245792 | tf_op jit(solution)/shard_map/ppermute | solution.py:46
  29.0 2.0 %collective-permute-done.1 = bf16[40,3072]{1,0:T(8,128)(2,1)S(1)} collective-permute-done((bf16[40,3072]{1,0:T(8,128)(2,1)S(1)}, bf16[40,3072]{1,0:T(8,128)(2,1)S(1)}, u32[]{:S(2)}, u32[]{:S(2)}) %collective-permute-start.1) | collective-permute-done | bytes 245792 | tf_op jit(solution)/shard_map/ppermute | solution.py:46
  31.1 2.8 %collective-permute-start.6 = (bf16[80,3072]{1,0:T(8,128)(2,1)S(1)}, bf16[80,3072]{1,0:T(8,128)(2,1)S(1)}, u32[]{:S(2)}, u32[]{:S(2)}) collective-permute-start(bf16[80,3072]{1,0:T(8,128)(2,1)S(1)} %shard_map.64), channel_id=1, source_target_pairs={{0,192},{1,7},{2,194},{3,1},{4,196},{5,3},{6,198},{7,5},{64,0},{65... | collective-permute-start | bytes 1474568 | tf_op jit(solution)/shard_map/ppermute | solution.py:41
  33.9 0.8 collective-permute-start.7
  34.7 0.9 collective-permute-start.5
  35.6 10.0 %collective-permute-done.6 = bf16[80,3072]{1,0:T(8,128)(2,1)S(1)} collective-permute-done((bf16[80,3072]{1,0:T(8,128)(2,1)S(1)}, bf16[80,3072]{1,0:T(8,128)(2,1)S(1)}, u32[]{:S(2)}, u32[]{:S(2)}) %collective-permute-start.6) | collective-permute-done | bytes 491552 | tf_op jit(solution)/shard_map/ppermute | solution.py:41
  45.7 0.1 collective-permute-start.11
  45.8 3.8 %collective-permute-done.5 = bf16[80,3072]{1,0:T(8,128)(2,1)S(1)} collective-permute-done((bf16[80,3072]{1,0:T(8,128)(2,1)S(1)}, bf16[80,3072]{1,0:T(8,128)(2,1)S(1)}, u32[]{:S(2)}, u32[]{:S(2)}) %collective-permute-start.5) | collective-permute-done | bytes 491552 | tf_op jit(solution)/shard_map/ppermute | solution.py:41
  49.5 0.1 pad_maximum_fusion.refs_0_
  49.6 0.1 collective-permute-start.8
  49.7 0.1 collective-permute-start.9
  49.8 2.0 %collective-permute-start.10 = (bf16[160,3072]{1,0:T(8,128)(2,1)S(1)}, bf16[160,3072]{1,0:T(8,128)(2,1)}, u32[]{:S(2)}, u32[]{:S(2)}) collective-permute-start(bf16[160,3072]{1,0:T(8,128)(2,1)S(1)} %pad_maximum_fusion.refs_0_), channel_id=1, source_target_pairs={{0,6},{1,193},{2,0},{3,195},{4,2},{5,197},{6,4},{7,199},{64,70},{6... | collective-permute-start | bytes 2949128 | tf_op jit(solution)/shard_map/ppermute | solution.py:41
  51.8 9.4 %collective-permute-done.11.refs_5_ = bf16[160,3072]{1,0:T(8,128)(2,1)} collective-permute-done((bf16[160,3072]{1,0:T(8,128)(2,1)S(1)}, bf16[160,3072]{1,0:T(8,128)(2,1)}, u32[]{:S(2)}, u32[]{:S(2)}) %collective-permute-start.11) | collective-permute-done | bytes 983072 | tf_op jit(solution)/shard_map/ppermute | solution.py:41
  61.2 2.7 %collective-permute-done.8.refs_2_ = bf16[160,3072]{1,0:T(8,128)(2,1)} collective-permute-done((bf16[160,3072]{1,0:T(8,128)(2,1)S(1)}, bf16[160,3072]{1,0:T(8,128)(2,1)}, u32[]{:S(2)}, u32[]{:S(2)}) %collective-permute-start.8) | collective-permute-done | bytes 983072 | tf_op jit(solution)/shard_map/ppermute | solution.py:41
  63.9 1.2 collective-permute-start.12
  65.1 0.1 stack.84.scalars
  65.2 9.2 %collective-permute-done.9.refs_3_ = bf16[160,3072]{1,0:T(8,128)(2,1)} collective-permute-done((bf16[160,3072]{1,0:T(8,128)(2,1)S(1)}, bf16[160,3072]{1,0:T(8,128)(2,1)}, u32[]{:S(2)}, u32[]{:S(2)}) %collective-permute-start.9) | collective-permute-done | bytes 983072 | tf_op jit(solution)/shard_map/ppermute | solution.py:41
  74.4 7.8 %collective-permute-done.13.refs_7_ = bf16[160,3072]{1,0:T(8,128)(2,1)} collective-permute-done((bf16[160,3072]{1,0:T(8,128)(2,1)}, bf16[160,3072]{1,0:T(8,128)(2,1)}, u32[]{:S(2)}, u32[]{:S(2)}) %collective-permute-start.13) | collective-permute-done | bytes 983072 | tf_op jit(solution)/shard_map/ppermute | solution.py:41
  82.2 2.7 %collective-permute-done.12.refs_6_ = bf16[160,3072]{1,0:T(8,128)(2,1)} collective-permute-done((bf16[160,3072]{1,0:T(8,128)(2,1)}, bf16[160,3072]{1,0:T(8,128)(2,1)}, u32[]{:S(2)}, u32[]{:S(2)}) %collective-permute-start.12) | collective-permute-done | bytes 983072 | tf_op jit(solution)/shard_map/ppermute | solution.py:41
  84.9 1.9 copy-done.2
  86.8 1.9 copy-done.3
  88.7 12.8 %shard_map.65.sums = bf16[16,80,1024]{2,1,0:T(8,128)(2,1)S(1)} custom-call(s32[24]{0:T(128)S(1)} %stack.84.scalars, bf16[160,3072]{1,0:T(8,128)(2,1)S(1)} %pad_maximum_fusion.refs_0_, bf16[160,3072]{1,0:T(8,128)(2,1)S(1)} %constant_dynamic-update-slice_fusion.refs_1_, bf16[160,3072]{1,0:T(8,128)(2,1)} %collective-permute-done.8.refs_2_, ...), custom_call_target="tpu_custom_call" | custom-call | flops 1048576 | bytes 1048576 | tf_op jit(solution)/shard_map/pallas_call | solution.py:99
  101.5 0.1 collective-permute-start.14
  101.6 4.9 %collective-permute-done.14.got = bf16[16,80,1024]{2,1,0:T(8,128)(2,1)S(1)} collective-permute-done((bf16[16,80,1024]{2,1,0:T(8,128)(2,1)S(1)}, bf16[16,80,1024]{2,1,0:T(8,128)(2,1)S(1)}, u32[]{:S(2)}, u32[]{:S(2)}) %collective-permute-start.14) | collective-permute-done | bytes 2621472 | tf_op jit(solution)/shard_map/ppermute | solution.py:50
  106.5 3.9 %shard_map.66 = (bf16[1280,512]{1,0:T(8,128)(2,1)S(1)}, bf16[2,320,768]{2,1,0:T(8,128)(2,1)S(1)}, bf16[2,320,768]{2,1,0:T(8,128)(2,1)S(1)}) custom-call(s32[24]{0:T(128)S(1)} %stack.84.scalars, bf16[16,80,1024]{2,1,0:T(8,128)(2,1)S(1)} %shard_map.65.sums, bf16[16,80,1024]{2,1,0:T(8,128)(2,1)S(1)} %collective-permute-done.14.got, ...), custom_call_target="tpu_custom_call" | custom-call | flops 1048576 | bytes 1048576 | tf_op jit(solution)/shard_map/pallas_call | solution.py:171
  110.4 1.0 collective-permute-start.20
  111.5 1.1 collective-permute-start.16
  112.5 5.5 %shard_map.67 = (bf16[2,320,768]{2,1,0:T(8,128)(2,1)S(1)}, bf16[2,320,768]{2,1,0:T(8,128)(2,1)S(1)}, bf16[2,320,768]{2,1,0:T(8,128)(2,1)S(1)}, bf16[2,320,768]{2,1,0:T(8,128)(2,1)S(1)}, bf16[4,320,768]{2,1,0:T(8,128)(2,1)S(1)}) custom-call(s32[24]{0:T(128)S(1)} %stack.84.scalars, bf16[1280,512]{1,0:T(8,128)(2,1)S(1)} %get-tuple-element.13.hidden, ...), custom_call_target="tpu_custom_call" | custom-call | flops 1048576 | bytes 1048576 | tf_op jit(solution)/shard_map/pallas_call | solution.py:215
  118.0 2.2 %collective-permute-start.15 = (bf16[2,320,768]{2,1,0:T(8,128)(2,1)S(1)}, bf16[2,320,768]{2,1,0:T(8,128)(2,1)S(1)}, u32[]{:S(2)}, u32[]{:S(2)}) collective-permute-start(bf16[2,320,768]{2,1,0:T(8,128)(2,1)S(1)} %get-tuple-element.15), channel_id=1, source_target_pairs={{0,192},{1,7},{2,194},{3,1},{4,196},{5,3},{6,198},{7,5},{64,0},{65... | collective-permute-start | bytes 2949128 | tf_op jit(solution)/shard_map/ppermute | solution.py:41
  120.3 4.3 %collective-permute-done.20 = bf16[2,320,768]{2,1,0:T(8,128)(2,1)S(1)} collective-permute-done((bf16[2,320,768]{2,1,0:T(8,128)(2,1)S(1)}, bf16[2,320,768]{2,1,0:T(8,128)(2,1)S(1)}, u32[]{:S(2)}, u32[]{:S(2)}) %collective-permute-start.20) | collective-permute-done | bytes 983072 | tf_op jit(solution)/shard_map/ppermute | solution.py:41
  124.6 0.3 add_convert_fusion
  124.9 2.2 %collective-permute-start.21 = (bf16[2,320,768]{2,1,0:T(8,128)(2,1)S(1)}, bf16[2,320,768]{2,1,0:T(8,128)(2,1)S(1)}, u32[]{:S(2)}, u32[]{:S(2)}) collective-permute-start(bf16[2,320,768]{2,1,0:T(8,128)(2,1)S(1)} %add_convert_fusion), channel_id=1, source_target_pairs={{0,192},{1,7},{2,194},{3,1},{4,196},{5,3},{6,198},{7,5},{64,0},{65... | collective-permute-start | bytes 2949128 | tf_op jit(solution)/shard_map/ppermute | solution.py:41
  127.1 0.3 add_convert_fusion.1
  127.4 0.1 collective-permute-start.17
  127.5 7.7 %collective-permute-done.15 = bf16[2,320,768]{2,1,0:T(8,128)(2,1)S(1)} collective-permute-done((bf16[2,320,768]{2,1,0:T(8,128)(2,1)S(1)}, bf16[2,320,768]{2,1,0:T(8,128)(2,1)S(1)}, u32[]{:S(2)}, u32[]{:S(2)}) %collective-permute-start.15) | collective-permute-done | bytes 983072 | tf_op jit(solution)/shard_map/ppermute | solution.py:41
  135.1 2.2 %collective-permute-done.19 = bf16[2,320,768]{2,1,0:T(8,128)(2,1)S(1)} collective-permute-done((bf16[2,320,768]{2,1,0:T(8,128)(2,1)S(1)}, bf16[2,320,768]{2,1,0:T(8,128)(2,1)S(1)}, u32[]{:S(2)}, u32[]{:S(2)}) %collective-permute-start.19) | collective-permute-done | bytes 983072 | tf_op jit(solution)/shard_map/ppermute | solution.py:41
  137.3 8.4 %collective-permute-done.21 = bf16[2,320,768]{2,1,0:T(8,128)(2,1)S(1)} collective-permute-done((bf16[2,320,768]{2,1,0:T(8,128)(2,1)S(1)}, bf16[2,320,768]{2,1,0:T(8,128)(2,1)S(1)}, u32[]{:S(2)}, u32[]{:S(2)}) %collective-permute-start.21) | collective-permute-done | bytes 983072 | tf_op jit(solution)/shard_map/ppermute | solution.py:41
  145.7 2.2 %collective-permute-done.17 = bf16[2,320,768]{2,1,0:T(8,128)(2,1)S(1)} collective-permute-done((bf16[2,320,768]{2,1,0:T(8,128)(2,1)S(1)}, bf16[2,320,768]{2,1,0:T(8,128)(2,1)S(1)}, u32[]{:S(2)}, u32[]{:S(2)}) %collective-permute-start.17) | collective-permute-done | bytes 983072 | tf_op jit(solution)/shard_map/ppermute | solution.py:41
  147.8 1.8 add_convert_fusion.5
  149.6 3.4 %collective-permute-start.22 = (bf16[320,768]{1,0:T(8,128)(2,1)}, bf16[320,768]{1,0:T(8,128)(2,1)S(1)}, u32[]{:S(2)}, u32[]{:S(2)}) collective-permute-start(bf16[320,768]{1,0:T(8,128)(2,1)} %get-tuple-element.44), channel_id=1, source_target_pairs={{0,2},{1,65},{2,4},{3,67},{4,6},{5,69},{6,0},{7,71},{64,66},{65,12... | collective-permute-start | bytes 1474568 | tf_op jit(solution)/shard_map/ppermute | solution.py:41
  153.0 1.5 collective-permute-start.23
  154.5 5.6 %collective-permute-done.18 = bf16[320,768]{1,0:T(8,128)(2,1)S(1)} collective-permute-done((bf16[320,768]{1,0:T(8,128)(2,1)}, bf16[320,768]{1,0:T(8,128)(2,1)S(1)}, u32[]{:S(2)}, u32[]{:S(2)}) %collective-permute-start.18) | collective-permute-done | bytes 491552 | tf_op jit(solution)/shard_map/ppermute | solution.py:41
  160.0 4.9 %collective-permute-done.22 = bf16[320,768]{1,0:T(8,128)(2,1)S(1)} collective-permute-done((bf16[320,768]{1,0:T(8,128)(2,1)}, bf16[320,768]{1,0:T(8,128)(2,1)S(1)}, u32[]{:S(2)}, u32[]{:S(2)}) %collective-permute-start.22) | collective-permute-done | bytes 491552 | tf_op jit(solution)/shard_map/ppermute | solution.py:41
  165.0 1.8 collective-permute-done.23
  167.2 0.8 constant_dynamic-slice_fusion
  168.1 7.6 %all-to-all-start = ((bf16[8,40,768]{2,1,0:T(8,128)(2,1)}), bf16[8,40,768]{2,1,0:T(8,128)(2,1)S(1)}, u32[]{:S(2)}, u32[]{:S(2)}) async-start(bf16[8,40,768]{2,1,0:T(8,128)(2,1)} %constant_dynamic-slice_fusion), calls=%async_computation | async-start | bytes 983040 | tf_op jit(solution)/shard_map/all_to_all | solution.py:282
  175.7 15.0 %all-to-all-done = bf16[8,40,768]{2,1,0:T(8,128)(2,1)S(1)} async-done(((bf16[8,40,768]{2,1,0:T(8,128)(2,1)}), bf16[8,40,768]{2,1,0:T(8,128)(2,1)S(1)}, u32[]{:S(2)}, u32[]{:S(2)}) %all-to-all-start) | async-done | bytes 491552 | tf_op jit(solution)/shard_map/all_to_all | solution.py:282
  190.8 0.3 fusion.31
  191.0 1.0 fusion
  (47 shorter events, 0.7 us)
Async XLA Ops:
  0.0 3.7 %copy-start = (bf16[128,6144]{1,0:T(8,128)(2,1)S(1)}, bf16[128,6144]{1,0:T(8,128)(2,1)}, u32[]{:S(2)}) copy-start(bf16[128,6144]{1,0:T(8,128)(2,1)} %param.6) | copy-start | bytes 4718596
  0.0 31.0 %collective-permute-start.4 = (bf16[256,6144]{1,0:T(8,128)(2,1)}, bf16[256,6144]{1,0:T(8,128)(2,1)}, u32[]{:S(2)}, u32[]{:S(2)}) collective-permute-start(bf16[256,6144]{1,0:T(8,128)(2,1)} %bitcast.91), channel_id=1, source_target_pairs={{0,1},{1,0},{2,3},{3,2},{4,5},{5,4},{6,7},{7,6},{8,9},{9,8},{10,11... | collective-permute-start | bytes 9437192 | tf_op jit(solution)/shard_map/ppermute | solution.py:50
  0.0 31.0 %collective-permute-start.2 = (bf16[6144,256]{1,0:T(8,128)(2,1)}, bf16[6144,256]{1,0:T(8,128)(2,1)}, u32[]{:S(2)}, u32[]{:S(2)}) collective-permute-start(bf16[6144,256]{1,0:T(8,128)(2,1)} %bitcast.94), channel_id=1, source_target_pairs={{0,1},{1,0},{2,3},{3,2},{4,5},{5,4},{6,7},{7,6},{8,9},{9,8},{10,11... | collective-permute-start | bytes 9437192 | tf_op jit(solution)/shard_map/ppermute | solution.py:50
  0.5 30.6 %collective-permute-start.3 = (bf16[6144,256]{1,0:T(8,128)(2,1)}, bf16[6144,256]{1,0:T(8,128)(2,1)}, u32[]{:S(2)}, u32[]{:S(2)}) collective-permute-start(bf16[6144,256]{1,0:T(8,128)(2,1)} %bitcast.96), channel_id=1, source_target_pairs={{0,1},{1,0},{2,3},{3,2},{4,5},{5,4},{6,7},{7,6},{8,9},{9,8},{10,11... | collective-permute-start | bytes 9437192 | tf_op jit(solution)/shard_map/ppermute | solution.py:50
  3.9 25.1 %collective-permute-start = (bf16[40,3072]{1,0:T(8,128)(2,1)S(1)}, bf16[40,3072]{1,0:T(8,128)(2,1)S(1)}, u32[]{:S(2)}, u32[]{:S(2)}) collective-permute-start(bf16[40,3072]{1,0:T(8,128)(2,1)S(1)} %convolution_convert_fusion.1), channel_id=1, source_target_pairs={{0,0},{2,10},{4,20},{6,30},{8,8},{10,18},{12,28},{14,38},{16,16},{... | collective-permute-start | bytes 737288 | tf_op jit(solution)/shard_map/ppermute | solution.py:46
  10.7 20.3 %collective-permute-start.1 = (bf16[40,3072]{1,0:T(8,128)(2,1)S(1)}, bf16[40,3072]{1,0:T(8,128)(2,1)S(1)}, u32[]{:S(2)}, u32[]{:S(2)}) collective-permute-start(bf16[40,3072]{1,0:T(8,128)(2,1)S(1)} %convolution_convert_fusion), channel_id=1, source_target_pairs={{0,32},{2,58},{4,52},{6,46},{8,40},{10,2},{12,60},{14,54},{16,48},... | collective-permute-start | bytes 737288 | tf_op jit(solution)/shard_map/ppermute | solution.py:46
  31.1 14.5 %collective-permute-start.6 = (bf16[80,3072]{1,0:T(8,128)(2,1)S(1)}, bf16[80,3072]{1,0:T(8,128)(2,1)S(1)}, u32[]{:S(2)}, u32[]{:S(2)}) collective-permute-start(bf16[80,3072]{1,0:T(8,128)(2,1)S(1)} %shard_map.64), channel_id=1, source_target_pairs={{0,192},{1,7},{2,194},{3,1},{4,196},{5,3},{6,198},{7,5},{64,0},{65... | collective-permute-start | bytes 1474568 | tf_op jit(solution)/shard_map/ppermute | solution.py:41
  33.9 11.7 %collective-permute-start.7 = (bf16[80,3072]{1,0:T(8,128)(2,1)S(1)}, bf16[80,3072]{1,0:T(8,128)(2,1)S(1)}, u32[]{:S(2)}, u32[]{:S(2)}) collective-permute-start(bf16[80,3072]{1,0:T(8,128)(2,1)S(1)} %shard_map.64), channel_id=1, source_target_pairs={{0,128},{1,5},{2,130},{3,7},{4,132},{5,1},{6,134},{7,3},{64,192},{... | collective-permute-start | bytes 1474568 | tf_op jit(solution)/shard_map/ppermute | solution.py:41
  34.7 14.8 %collective-permute-start.5 = (bf16[80,3072]{1,0:T(8,128)(2,1)S(1)}, bf16[80,3072]{1,0:T(8,128)(2,1)S(1)}, u32[]{:S(2)}, u32[]{:S(2)}) collective-permute-start(bf16[80,3072]{1,0:T(8,128)(2,1)S(1)} %shard_map.64), channel_id=1, source_target_pairs={{0,64},{1,3},{2,66},{3,5},{4,68},{5,7},{6,70},{7,1},{64,128},{65,6... | collective-permute-start | bytes 1474568 | tf_op jit(solution)/shard_map/ppermute | solution.py:41
  45.7 15.5 %collective-permute-start.11 = (bf16[160,3072]{1,0:T(8,128)(2,1)S(1)}, bf16[160,3072]{1,0:T(8,128)(2,1)}, u32[]{:S(2)}, u32[]{:S(2)}) collective-permute-start(bf16[160,3072]{1,0:T(8,128)(2,1)S(1)} %constant_dynamic-update-slice_fusion.refs_1_), channel_id=1, source_target_pairs={{0,6},{1,193},{2,0},{3,195},{4,2},{5,197},{6,4},{7,199},{64,70},{6... | collective-permute-start | bytes 2949128 | tf_op jit(solution)/shard_map/ppermute | solution.py:41
  49.6 14.3 %collective-permute-start.8 = (bf16[160,3072]{1,0:T(8,128)(2,1)S(1)}, bf16[160,3072]{1,0:T(8,128)(2,1)}, u32[]{:S(2)}, u32[]{:S(2)}) collective-permute-start(bf16[160,3072]{1,0:T(8,128)(2,1)S(1)} %pad_maximum_fusion.refs_0_), channel_id=1, source_target_pairs={{0,2},{1,65},{2,4},{3,67},{4,6},{5,69},{6,0},{7,71},{64,66},{65,12... | collective-permute-start | bytes 2949128 | tf_op jit(solution)/shard_map/ppermute | solution.py:41
  49.7 24.7 %collective-permute-start.9 = (bf16[160,3072]{1,0:T(8,128)(2,1)S(1)}, bf16[160,3072]{1,0:T(8,128)(2,1)}, u32[]{:S(2)}, u32[]{:S(2)}) collective-permute-start(bf16[160,3072]{1,0:T(8,128)(2,1)S(1)} %constant_dynamic-update-slice_fusion.refs_1_), channel_id=1, source_target_pairs={{0,2},{1,65},{2,4},{3,67},{4,6},{5,69},{6,0},{7,71},{64,66},{65,12... | collective-permute-start | bytes 2949128 | tf_op jit(solution)/shard_map/ppermute | solution.py:41
  49.8 24.6 %collective-permute-start.10 = (bf16[160,3072]{1,0:T(8,128)(2,1)S(1)}, bf16[160,3072]{1,0:T(8,128)(2,1)}, u32[]{:S(2)}, u32[]{:S(2)}) collective-permute-start(bf16[160,3072]{1,0:T(8,128)(2,1)S(1)} %pad_maximum_fusion.refs_0_), channel_id=1, source_target_pairs={{0,6},{1,193},{2,0},{3,195},{4,2},{5,197},{6,4},{7,199},{64,70},{6... | collective-permute-start | bytes 2949128 | tf_op jit(solution)/shard_map/ppermute | solution.py:41
  61.2 21.1 %collective-permute-start.13 = (bf16[160,3072]{1,0:T(8,128)(2,1)}, bf16[160,3072]{1,0:T(8,128)(2,1)}, u32[]{:S(2)}, u32[]{:S(2)}) collective-permute-start(bf16[160,3072]{1,0:T(8,128)(2,1)} %collective-permute-done.11.refs_5_), channel_id=1, source_target_pairs={{0,6},{1,193},{2,0},{3,195},{4,2},{5,197},{6,4},{7,199},{64,70},{6... | collective-permute-start | bytes 2949128 | tf_op jit(solution)/shard_map/ppermute | solution.py:41
  63.9 21.1 %collective-permute-start.12 = (bf16[160,3072]{1,0:T(8,128)(2,1)}, bf16[160,3072]{1,0:T(8,128)(2,1)}, u32[]{:S(2)}, u32[]{:S(2)}) collective-permute-start(bf16[160,3072]{1,0:T(8,128)(2,1)} %collective-permute-done.8.refs_2_), channel_id=1, source_target_pairs={{0,2},{1,65},{2,4},{3,67},{4,6},{5,69},{6,0},{7,71},{64,66},{65,12... | collective-permute-start | bytes 2949128 | tf_op jit(solution)/shard_map/ppermute | solution.py:41
  84.9 1.9 copy-start.2
  86.8 1.9 copy-start.3
  88.7 17.8 %copy-start.1 = (bf16[1,256,6144]{2,1,0:T(8,128)(2,1)S(1)}, bf16[1,256,6144]{2,1,0:T(8,128)(2,1)}, u32[]{:S(2)}) copy-start(bf16[1,256,6144]{2,1,0:T(8,128)(2,1)} %param.11) | copy-start | bytes 9437188
  101.5 5.0 %collective-permute-start.14 = (bf16[16,80,1024]{2,1,0:T(8,128)(2,1)S(1)}, bf16[16,80,1024]{2,1,0:T(8,128)(2,1)S(1)}, u32[]{:S(2)}, u32[]{:S(2)}) collective-permute-start(bf16[16,80,1024]{2,1,0:T(8,128)(2,1)S(1)} %shard_map.65.sums), channel_id=1, source_target_pairs={{0,1},{1,0},{2,3},{3,2},{4,5},{5,4},{6,7},{7,6},{8,9},{9,8},{10,11... | collective-permute-start | bytes 7864328 | tf_op jit(solution)/shard_map/ppermute | solution.py:50
  110.4 14.2 %collective-permute-start.20 = (bf16[2,320,768]{2,1,0:T(8,128)(2,1)S(1)}, bf16[2,320,768]{2,1,0:T(8,128)(2,1)S(1)}, u32[]{:S(2)}, u32[]{:S(2)}) collective-permute-start(bf16[2,320,768]{2,1,0:T(8,128)(2,1)S(1)} %get-tuple-element.20), channel_id=1, source_target_pairs={{0,192},{1,7},{2,194},{3,1},{4,196},{5,3},{6,198},{7,5},{64,0},{65... | collective-permute-start | bytes 2949128 | tf_op jit(solution)/shard_map/ppermute | solution.py:41
  111.5 15.7 %collective-permute-start.16 = (bf16[2,320,768]{2,1,0:T(8,128)(2,1)S(1)}, bf16[2,320,768]{2,1,0:T(8,128)(2,1)S(1)}, u32[]{:S(2)}, u32[]{:S(2)}) collective-permute-start(bf16[2,320,768]{2,1,0:T(8,128)(2,1)S(1)} %get-tuple-element.17), channel_id=1, source_target_pairs={{0,64},{1,3},{2,66},{3,5},{4,68},{5,7},{6,70},{7,1},{64,128},{65,6... | collective-permute-start | bytes 2949128 | tf_op jit(solution)/shard_map/ppermute | solution.py:41
  118.0 17.1 %collective-permute-start.15 = (bf16[2,320,768]{2,1,0:T(8,128)(2,1)S(1)}, bf16[2,320,768]{2,1,0:T(8,128)(2,1)S(1)}, u32[]{:S(2)}, u32[]{:S(2)}) collective-permute-start(bf16[2,320,768]{2,1,0:T(8,128)(2,1)S(1)} %get-tuple-element.15), channel_id=1, source_target_pairs={{0,192},{1,7},{2,194},{3,1},{4,196},{5,3},{6,198},{7,5},{64,0},{65... | collective-permute-start | bytes 2949128 | tf_op jit(solution)/shard_map/ppermute | solution.py:41
  120.3 17.0 %collective-permute-start.19 = (bf16[2,320,768]{2,1,0:T(8,128)(2,1)S(1)}, bf16[2,320,768]{2,1,0:T(8,128)(2,1)S(1)}, u32[]{:S(2)}, u32[]{:S(2)}) collective-permute-start(bf16[2,320,768]{2,1,0:T(8,128)(2,1)S(1)} %get-tuple-element.18), channel_id=1, source_target_pairs={{0,64},{1,3},{2,66},{3,5},{4,68},{5,7},{6,70},{7,1},{64,128},{65,6... | collective-permute-start | bytes 2949128 | tf_op jit(solution)/shard_map/ppermute | solution.py:41
  124.9 20.8 %collective-permute-start.21 = (bf16[2,320,768]{2,1,0:T(8,128)(2,1)S(1)}, bf16[2,320,768]{2,1,0:T(8,128)(2,1)S(1)}, u32[]{:S(2)}, u32[]{:S(2)}) collective-permute-start(bf16[2,320,768]{2,1,0:T(8,128)(2,1)S(1)} %add_convert_fusion), channel_id=1, source_target_pairs={{0,192},{1,7},{2,194},{3,1},{4,196},{5,3},{6,198},{7,5},{64,0},{65... | collective-permute-start | bytes 2949128 | tf_op jit(solution)/shard_map/ppermute | solution.py:41
  127.4 20.5 %collective-permute-start.17 = (bf16[2,320,768]{2,1,0:T(8,128)(2,1)S(1)}, bf16[2,320,768]{2,1,0:T(8,128)(2,1)S(1)}, u32[]{:S(2)}, u32[]{:S(2)}) collective-permute-start(bf16[2,320,768]{2,1,0:T(8,128)(2,1)S(1)} %add_convert_fusion.1), channel_id=1, source_target_pairs={{0,64},{1,3},{2,66},{3,5},{4,68},{5,7},{6,70},{7,1},{64,128},{65,6... | collective-permute-start | bytes 2949128 | tf_op jit(solution)/shard_map/ppermute | solution.py:41
  149.6 10.4 %collective-permute-start.18 = (bf16[320,768]{1,0:T(8,128)(2,1)}, bf16[320,768]{1,0:T(8,128)(2,1)S(1)}, u32[]{:S(2)}, u32[]{:S(2)}) collective-permute-start(bf16[320,768]{1,0:T(8,128)(2,1)} %get-tuple-element.40), channel_id=1, source_target_pairs={{0,6},{1,193},{2,0},{3,195},{4,2},{5,197},{6,4},{7,199},{64,70},{6... | collective-permute-start | bytes 1474568 | tf_op jit(solution)/shard_map/ppermute | solution.py:41
  149.6 15.3 %collective-permute-start.22 = (bf16[320,768]{1,0:T(8,128)(2,1)}, bf16[320,768]{1,0:T(8,128)(2,1)S(1)}, u32[]{:S(2)}, u32[]{:S(2)}) collective-permute-start(bf16[320,768]{1,0:T(8,128)(2,1)} %get-tuple-element.44), channel_id=1, source_target_pairs={{0,2},{1,65},{2,4},{3,67},{4,6},{5,69},{6,0},{7,71},{64,66},{65,12... | collective-permute-start | bytes 1474568 | tf_op jit(solution)/shard_map/ppermute | solution.py:41
  153.0 13.7 %collective-permute-start.23 = (bf16[320,768]{1,0:T(8,128)(2,1)}, bf16[320,768]{1,0:T(8,128)(2,1)S(1)}, u32[]{:S(2)}, u32[]{:S(2)}) collective-permute-start(bf16[320,768]{1,0:T(8,128)(2,1)} %get-tuple-element.43), channel_id=1, source_target_pairs={{0,4},{1,129},{2,6},{3,131},{4,0},{5,133},{6,2},{7,135},{64,68},{6... | collective-permute-start | bytes 1474568 | tf_op jit(solution)/shard_map/ppermute | solution.py:41
  167.0 8.7 %copy-start.4 = (f32[128,2]{0,1:T(2,128)S(1)}, f32[128,2]{0,1:T(2,128)}, u32[]{:S(2)}) copy-start(f32[128,2]{0,1:T(2,128)} %param.8) | copy-start | bytes 3076
  168.1 22.7 %all-to-all-start = ((bf16[8,40,768]{2,1,0:T(8,128)(2,1)}), bf16[8,40,768]{2,1,0:T(8,128)(2,1)S(1)}, u32[]{:S(2)}, u32[]{:S(2)}) async-start(bf16[8,40,768]{2,1,0:T(8,128)(2,1)} %constant_dynamic-slice_fusion), calls=%async_computation | async-start | bytes 983040 | tf_op jit(solution)/shard_map/all_to_all | solution.py:282

commit v2 on v1

--- a/solution.py
+++ b/solution.py
@@ -42,8 +42,13 @@
 
 
 def along_z(value, j):
-    pairs = [(z * 4 + y, (z + ROUTES[y][j]) % 8 * 4 + y) for z in range(8) for y in range(4)]
-    return lax.ppermute(value, ("expert", "ty"), pairs)
+    pairs = []
+    for z in range(8):
+        for y in range(4):
+            for c in range(2):
+                to = (z + ROUTES[-y % 4 if c else y][j]) % 8
+                pairs.append(((z * 4 + y) * 2 + c, (to * 4 + y) * 2 + c))
+    return lax.ppermute(value, ("expert", "ty", "core"), pairs)
 
 
 def swap(value):
@@ -62,21 +67,30 @@
     )(value, *others)
 
 
-def gate_up_kernel(pieces, scalars, *refs):
-    rows, weights = refs[:pieces], refs[pieces : pieces + 4]
-    out, held, weight, row_sems, sems = refs[-5:]
+def gate_up_kernel(places, merges, scalars, *refs):
+    pieces = len(places)
+    rows, weights, before = refs[:pieces], refs[pieces : pieces + 4], refs[pieces + 4 : -6]
+    out, held, weight, row_sems, sems, merge_sems = refs[-6:]
     depth, step = weight.shape[1:]
-    at, row_copies = 0, []
-    for i, ref in enumerate(rows):
+    block = out.shape[1]
+    start = pl.multiple_of(scalars[20] * depth, depth)
+    at, row_copies, order = 0, [], []
+    for i, (ref, place) in enumerate(zip(rows, places)):
         count = ref.shape[0]
         row_copies.append(pltpu.make_async_copy(ref, held.at[pl.ds(at, count)], row_sems.at[i]))
         at += count
-    start = pl.multiple_of(scalars[20] * depth, depth)
+        order += range(place, place + count // block)
     copies = [
         pltpu.make_async_copy(ref.at[pl.ds(start, depth)], weight.at[i], sems.at[i])
         for i, ref in enumerate(weights)
     ]
-    for copy in row_copies + copies:
+    merge_copies = [
+        pltpu.make_async_copy(
+            before[n].at[pl.ds(first, 2)], out.at[pl.ds(to, 2)], merge_sems.at[i]
+        )
+        for i, (n, first, to) in enumerate(merges)
+    ]
+    for copy in row_copies + copies + merge_copies:
         copy.start()
     for copy in row_copies:
         copy.wait()
@@ -86,30 +100,33 @@
         pltpu.make_async_copy(weights[0].at[pl.ds(start, depth)], weight.at[n], sems.at[n]).wait()
         value = dot(held[...], weight[n])
         column = pl.multiple_of(n * step, step)
-        for i in range(out.shape[0]):
-            block = value[i * out.shape[1] : (i + 1) * out.shape[1]]
-            out[i, :, pl.ds(column, step)] = block.astype(BF)
-
-
-def gate_up(rows, weights, scalars):
-    count = sum(r.shape[0] for r in rows)
+        for i, place in enumerate(order):
+            out[place, :, pl.ds(column, step)] = value[i * block : (i + 1) * block].astype(BF)
+
+    for copy in merge_copies:
+        copy.wait()
+
+
+def gate_up(rows, places, weights, scalars, before=(), merges=()):
+    count, block = sum(r.shape[0] for r in rows), 2 * CAP
     depth, step = weights[0].shape
     depth //= 2
-    block = 2 * CAP
-    return pl.pallas_call(
-        functools.partial(gate_up_kernel, len(rows)),
-        in_specs=[SMEM] + [ANY] * len(rows) + [HBM] * 4,
+    blocks = count // block + 2 * len(merges)
+    return pl.pallas_call(
+        functools.partial(gate_up_kernel, places, merges),
+        in_specs=[SMEM] + [ANY] * len(rows) + [HBM] * 4 + [ANY] * len(before),
         out_specs=VMEM,
-        out_shape=jax.ShapeDtypeStruct((count // block, block, 4 * step), BF),
+        out_shape=jax.ShapeDtypeStruct((blocks, block, 4 * step), BF),
         scratch_shapes=[
             pltpu.VMEM((count, depth), BF),
             pltpu.VMEM((4, depth, step), BF),
             pltpu.SemaphoreType.DMA((len(rows),)),
             pltpu.SemaphoreType.DMA((4,)),
+            pltpu.SemaphoreType.DMA((max(len(merges), 1),)),
         ],
-        compiler_params=pltpu.CompilerParams(vmem_limit_bytes=24 * MIB),
-        cost_estimate=COST,
-    )(scalars, *rows, *weights)
+        compiler_params=pltpu.CompilerParams(vmem_limit_bytes=20 * MIB),
+        cost_estimate=COST,
+    )(scalars, *rows, *weights, *before)
 
 
 def down_copies(scalars, mine, theirs, down, sems, count=4):
@@ -137,17 +154,15 @@
     units = hidden.shape[1] // 2
     rows = hidden.shape[0] // 4
     block = rows // 4
-    for i in range(4):
-        for j in range(4):
-            start = pl.multiple_of(scalars[4 * i + j] * block, 16)
-            here, there = sums[4 * i + j].astype(F32), got[4 * j + i].astype(F32)
-            for side in range(2):
-                at, other = 2 * units * side, 2 * units * (1 - side)
-                gate = here[:, at : at + units] + there[:, other : other + units]
-                upper = here[:, at + units : at + 2 * units]
-                upper = upper + there[:, other + units : other + 2 * units]
-                value = gate / (1.0 + jnp.exp(-gate)) * upper
-                hidden[pl.ds(start, block), side * units : (side + 1) * units] = value.astype(BF)
+    for i in range(16):
+        here, there = sums[scalars[i]].astype(F32), got[scalars[24 + i]].astype(F32)
+        for side in range(2):
+            at, other = 2 * units * side, 2 * units * (1 - side)
+            gate = here[:, at : at + units] + there[:, other : other + units]
+            upper = here[:, at + units : at + 2 * units]
+            upper = upper + there[:, other + units : other + 2 * units]
+            value = gate / (1.0 + jnp.exp(-gate)) * upper
+            hidden[i * block : (i + 1) * block, side * units : (side + 1) * units] = value.astype(BF)
     outs = (far_a.at[0], far_a.at[1], far_b.at[0], far_b.at[1])
     for copy in copies:
         copy.wait()
@@ -223,6 +238,44 @@
     )(scalars, hidden, mine, theirs)
 
 
+def mid_kernel(own, high, low, got_1, got_2, mid_1, mid_2):
+    for i, parts, out in ((1, (low.at[1], got_1), mid_1), (2, (high.at[0], got_2), mid_2)):
+        total = own[i].astype(F32)
+        for part in parts:
+            total = total + part[...].astype(F32)
+        out[...] = total.astype(BF)
+
+
+def mid_sums(*values):
+    piece = jax.ShapeDtypeStruct(values[-1].shape, BF)
+    return pl.pallas_call(
+        mid_kernel,
+        in_specs=[VMEM] * 5,
+        out_specs=[VMEM] * 2,
+        out_shape=[piece, piece],
+        compiler_params=pltpu.CompilerParams(vmem_limit_bytes=16 * MIB),
+        cost_estimate=COST,
+    )(*values)
+
+
+def last_kernel(places, a, b, c, d, out):
+    for i in range(E):
+        total = a[i].astype(F32) + b[i].astype(F32) + c[i].astype(F32) + d[i].astype(F32)
+        out[places[i]] = total.astype(BF)
+
+
+def last_sum(places, parts):
+    shape = (E, CAP, parts[0].shape[1])
+    return pl.pallas_call(
+        last_kernel,
+        in_specs=[SMEM] + [VMEM] * 4,
+        out_specs=VMEM,
+        out_shape=jax.ShapeDtypeStruct(shape, BF),
+        compiler_params=pltpu.CompilerParams(vmem_limit_bytes=16 * MIB),
+        cost_estimate=COST,
+    )(places, *[p.reshape(shape) for p in parts])
+
+
 def body(tokens, routes, logits, w_gate, w_up, w_down):
     rows, width = tokens.shape
     half = width // 2
@@ -236,11 +289,12 @@
     target = (expert_ids * CAP + slot_index).reshape(rows, 2)
     columns = lax.dynamic_slice_in_dim(tokens, c * half, half, 1)
     slots = jnp.arange(CAP, dtype=jnp.int32)
+    line = jnp.where(c == 0, y, -y % 4)
 
     def outgoing(j):
         step = jnp.int32(ROUTES[0][j])
-        for line in range(1, 4):
-            step = jnp.where(y == line, ROUTES[line][j], step)
+        for number in range(1, 4):
+            step = jnp.where(line == number, ROUTES[number][j], step)
         places = (z + step + 8) % 8 * CAP + slots
         hit = places[:, None, None] == target[None, :, :]
         return dot(jnp.any(hit, axis=2).astype(BF), columns).astype(BF)
@@ -252,34 +306,46 @@
     piece = after(jnp.concatenate(arrived, axis=0), *weights[2:], downs[1])
 
     lines = [(y + o + 4) % 4 for o in OFFSETS]
-    place = [jnp.where(c == 0, j * 4 + lines[i], i * 4 + lines[j]) for i in range(4) for j in range(4)]
-    scalars = jnp.stack(place + lines + [c] + [jnp.int32(0)] * 3).astype(jnp.int32)
+    at = lambda d: jnp.where(d == 0, 0, jnp.where(d == 3, 1, d + 1))
+    blocks = [
+        [4 * at((v - y + 4) % 4) + r for r in range(4) for v in range(4)],
+        [4 * r + at((8 - v - y) % 4) for r in range(4) for v in range(4)],
+    ]
+    here = [jnp.where(c == 0, p, q) for p, q in zip(*blocks)]
+    there = [jnp.where(c == 0, q, p) for p, q in zip(*blocks)]
+    scalars = jnp.stack(here + lines + [c] + [jnp.int32(0)] * 3 + there).astype(jnp.int32)
 
     low = jnp.concatenate([piece, plane(piece, 0, 1)], axis=0)
     high = jnp.concatenate([plane(piece, 0, -1), plane(piece, 0, 2)], axis=0)
     below_low, above_high = plane(low, 1, 1), plane(high, 1, -1)
     below_high, above_low = plane(high, 1, 1), plane(low, 1, -1)
-    far = [plane(below_low, 1, 1), plane(above_high, 1, -1)]
-    rows_all = [low, high, below_low, below_high, above_low, above_high, *far]
-    sums = gate_up(rows_all, weights, scalars)
+    own_sums = gate_up([low, high], (0, 2), weights, scalars)
+    far = [plane(after(below_low, own_sums), 1, 1), plane(above_high, 1, -1)]
+    near_sums = gate_up([below_low, above_high], (0, 2), weights, scalars)
+    sums = gate_up(
+        [below_high, above_low, *far],
+        (6, 8, 12, 14),
+        weights,
+        scalars,
+        [own_sums, near_sums],
+        ((0, 0, 0), (0, 2, 2), (1, 0, 4), (1, 2, 10)),
+    )
     hidden, far_a, far_b = hidden_of(sums, swap(sums), *downs, scalars)
     below_a, below_b, above_a, above_b, own = down_of(hidden, *downs, scalars)
 
     from_below, from_above = plane(far_a, 0, 1), plane(far_b, 0, -1)
     got_high, got_low = plane(above_b, 0, 1), plane(below_a, 0, -1)
-    got_low2 = plane(add(above_a, from_below), 0, 1)
-    got_high2 = plane(add(below_b, from_above), 0, -1)
-    mid = [add(own[i], got_low[i], got_low2[i]) for i in range(2)]
-    mid += [add(own[2 + i], got_high[i], got_high2[i]) for i in range(2)]
-    ends = [mid[0], plane(mid[1], 1, -1), plane(mid[2], 1, 1), plane(mid[3], 1, 2)]
-    moved = []
-    for step in range(0, -8, -1):
-        [found] = [(i, j) for i in range(4) for j in range(2) if (ROUTES[i][j] - step) % 8 == 0]
-        at = (2 * found[0] + found[1]) * CAP
-        moved.append(add(*[e[at : at + CAP] for e in ends]))
-    moved = jnp.concatenate(moved * 2, axis=0).reshape(2 * E, CAP, part)
-    moved = lax.dynamic_slice_in_dim(moved, (E - z) % E, E, 0)
-    table = lax.all_to_all(moved, "expert", 0, 0, tiled=True).reshape(E * CAP, part)
+    to_above = [add(above_a[i], from_below[i]) for i in range(2)]
+    to_below = [add(below_b[i], from_above[i]) for i in range(2)]
+    got_1, got_2 = plane(to_above[1], 0, 1), plane(to_below[0], 0, -1)
+    got_0, got_3 = plane(to_above[0], 0, 1), plane(to_below[1], 0, -1)
+    mid_1, mid_2 = mid_sums(own, got_high, got_low, got_1, got_2)
+    end_1, end_2 = plane(mid_1, 1, -1), plane(mid_2, 1, 1)
+    mid_0, mid_3 = add(own[0], got_low[0], got_0), add(own[3], got_high[1], got_3)
+    ends = [mid_0, end_1, end_2, plane(mid_3, 1, 2)]
+    places = jnp.stack([(z - step + 8) % 8 for pair in ROUTES for step in pair]).astype(jnp.int32)
+    table = lax.all_to_all(last_sum(places, ends), "expert", 0, 0, tiled=True)
+    table = table.reshape(E * CAP, part)
 
     share = jax.nn.sigmoid(logits - logits[:, ::-1])
     hit = jnp.arange(E * CAP, dtype=jnp.int32)[None, :, None] == target[:, None, :]

time: 193 us -> 173 us (0.90)
  waiting for transfers between devices: 121 us -> 83.4 us
  starting transfers between devices: 36.5 us -> 47.9 us
  Pallas kernels: 22.2 us -> 28.3 us
    ppermute x18 -> x20, waiting for transfers between devices: 82.5 us -> 55.4 us  [plane(): return lax.ppermute(value, ('dp', 'ty', 'core'), pairs)]
    ppermute x2, waiting for transfers between devices: 18.1 us -> 10.2 us  [along_z(): return lax.ppermute(value, ('expert', 'ty', 'core'), pairs)]
    ppermute x18 -> x20, starting transfers between devices: 19.5 us -> 27.3 us  [plane(): return lax.ppermute(value, ('dp', 'ty', 'core'), pairs)]
    pallas_call x1 -> x5, Pallas kernels: 12.8 us -> 19.8 us  [the longest x3 17 us: gate_up(): pl.pallas_call(functools.partial(gate_up_kernel, places, merges), in_spec...]
    all_to_all x1, starting transfers between devices: 7.58 us -> 11.2 us  [body(): table = lax.all_to_all(last_sum(places, ends), 'expert', 0, 0, tiled=True)]
    all_to_all x1, waiting for transfers between devices: 15 us -> 12.8 us  [body(): table = lax.all_to_all(last_sum(places, ends), 'expert', 0, 0, tiled=True)]
    unnamed x19 -> x14, local copies, waits for them, and re-layouts: 4.66 us -> 5.4 us
  transfers between devices with their start and end apart: 25 -> 27, of which waited for: 19 -> 19; matrix products, arithmetic and copies ran while one was open for 2% -> 4% of each run, Pallas kernels for 3% -> 9%
where the time goes in v2:
time: 173 us; the launch traced here: 172 us
  waiting for transfers between devices  83.4 us (48%)
  starting transfers between devices  47.9 us (28%)
  Pallas kernels  28.3 us (16%)
  local copies, waits for them, and re-layouts  7.15 us (4%)
  other arithmetic  3.34 us (2%)
  matrix products  1.75 us (1%)
    ppermute x20, waiting for transfers between devices, plane(): return lax.ppermute(value, ('dp', 'ty', 'core'), pairs)  55.4 us
    ppermute x20, starting transfers between devices, plane(): return lax.ppermute(value, ('dp', 'ty', 'core'), pairs)  27.3 us
    pallas_call x3, Pallas kernels, gate_up(): pl.pallas_call(functools.partial(gate_up_kernel, places, merges), in_spec...  17 us
    all_to_all x1, waiting for transfers between devices, body(): table = lax.all_to_all(last_sum(places, ends), 'expert', 0, 0, tiled=True)  12.8 us
    all_to_all x1, starting transfers between devices, body(): table = lax.all_to_all(last_sum(places, ends), 'expert', 0, 0, tiled=True)  11.2 us
    ppermute x2, waiting for transfers between devices, along_z(): return lax.ppermute(value, ('expert', 'ty', 'core'), pairs)  10.2 us
    ppermute x2, starting transfers between devices, along_z(): return lax.ppermute(value, ('expert', 'ty', 'core'), pairs)  8.74 us
    unnamed x14, local copies, waits for them, and re-layouts  5.4 us
  transfers between devices with their start and end apart: 27, of which 19 were waited for; matrix products, arithmetic and copies ran while one was open for 4% of the time, Pallas kernels for 9%

profile of v2, /device:TPU:24, one launch (start us, length us, event | category | flops | bytes accessed | tf_op | source)
XLA Modules:
  0.0 172.2 jit_solution(3860196047287913604)
XLA Ops:
  0.0 0.5 collective-permute-start.3
  0.5 0.1 collective-permute-start.4
  0.6 0.8 copy.23
  1.4 0.1 eq.115
  1.5 0.1 eq.111
  1.7 0.6 reduce-window.6
  2.3 0.2 slice_reduce_fusion
  2.6 0.1 reduce_sum.21
  2.9 0.7 multiply_add_fusion
  3.7 0.2 convolution_convert_fusion.1
  3.9 6.5 %collective-permute-start = (bf16[40,3072]{1,0:T(8,128)(2,1)S(1)}, bf16[40,3072]{1,0:T(8,128)(2,1)S(1)}, u32[]{:S(2)}, u32[]{:S(2)}) collective-permute-start(bf16[40,3072]{1,0:T(8,128)(2,1)S(1)} %convolution_convert_fusion.1), channel_id=1, source_target_pairs={{0,0},{1,1},{2,10},{3,27},{4,20},{5,21},{6,30},{7,15},{8,8},{9,9},... | collective-permute-start | bytes 737288 | tf_op jit(solution)/shard_map/ppermute | solution.py:51
  10.5 0.2 convolution_convert_fusion
  10.7 2.2 %collective-permute-start.1 = (bf16[40,3072]{1,0:T(8,128)(2,1)S(1)}, bf16[40,3072]{1,0:T(8,128)(2,1)S(1)}, u32[]{:S(2)}, u32[]{:S(2)}) collective-permute-start(bf16[40,3072]{1,0:T(8,128)(2,1)S(1)} %convolution_convert_fusion), channel_id=1, source_target_pairs={{0,32},{1,33},{2,58},{3,43},{4,52},{5,53},{6,46},{7,63},{8,40},{9,... | collective-permute-start | bytes 737288 | tf_op jit(solution)/shard_map/ppermute | solution.py:51
  12.9 9.7 %collective-permute-done = bf16[40,3072]{1,0:T(8,128)(2,1)S(1)} collective-permute-done((bf16[40,3072]{1,0:T(8,128)(2,1)S(1)}, bf16[40,3072]{1,0:T(8,128)(2,1)S(1)}, u32[]{:S(2)}, u32[]{:S(2)}) %collective-permute-start) | collective-permute-done | bytes 245792 | tf_op jit(solution)/shard_map/ppermute | solution.py:51
  22.7 0.5 collective-permute-done.1
  23.2 1.6 collective-permute-start.8
  24.8 1.7 %collective-permute-start.5 = (bf16[80,3072]{1,0:T(8,128)(2,1)S(1)}, bf16[80,3072]{1,0:T(8,128)(2,1)S(1)}, u32[]{:S(2)}, u32[]{:S(2)}) collective-permute-start(bf16[80,3072]{1,0:T(8,128)(2,1)S(1)} %shard_map.64), channel_id=1, source_target_pairs={{0,192},{1,7},{2,194},{3,1},{4,196},{5,3},{6,198},{7,5},{64,0},{65... | collective-permute-start | bytes 1474568 | tf_op jit(solution)/shard_map/ppermute | solution.py:41
  26.5 1.8 %collective-permute-start.6 = (bf16[80,3072]{1,0:T(8,128)(2,1)S(1)}, bf16[80,3072]{1,0:T(8,128)(2,1)S(1)}, u32[]{:S(2)}, u32[]{:S(2)}) collective-permute-start(bf16[80,3072]{1,0:T(8,128)(2,1)S(1)} %shard_map.64), channel_id=1, source_target_pairs={{0,128},{1,5},{2,130},{3,7},{4,132},{5,1},{6,134},{7,3},{64,192},{... | collective-permute-start | bytes 1474568 | tf_op jit(solution)/shard_map/ppermute | solution.py:41
  28.3 5.0 %collective-permute-done.8 = bf16[80,3072]{1,0:T(8,128)(2,1)S(1)} collective-permute-done((bf16[80,3072]{1,0:T(8,128)(2,1)S(1)}, bf16[80,3072]{1,0:T(8,128)(2,1)S(1)}, u32[]{:S(2)}, u32[]{:S(2)}) %collective-permute-start.8) | collective-permute-done | bytes 491552 | tf_op jit(solution)/shard_map/ppermute | solution.py:41
  33.5 4.7 %collective-permute-done.5 = bf16[80,3072]{1,0:T(8,128)(2,1)S(1)} collective-permute-done((bf16[80,3072]{1,0:T(8,128)(2,1)S(1)}, bf16[80,3072]{1,0:T(8,128)(2,1)S(1)}, u32[]{:S(2)}, u32[]{:S(2)}) %collective-permute-start.5) | collective-permute-done | bytes 491552 | tf_op jit(solution)/shard_map/ppermute | solution.py:41
  38.2 0.8 constant_dynamic-update-slice_fusion.1
  39.0 2.9 %collective-permute-done.6 = bf16[80,3072]{1,0:T(8,128)(2,1)S(1)} collective-permute-done((bf16[80,3072]{1,0:T(8,128)(2,1)S(1)}, bf16[80,3072]{1,0:T(8,128)(2,1)S(1)}, u32[]{:S(2)}, u32[]{:S(2)}) %collective-permute-start.6) | collective-permute-done | bytes 491552 | tf_op jit(solution)/shard_map/ppermute | solution.py:41
  41.9 0.8 constant_dynamic-update-slice_fusion.refs_1_
  42.7 0.7 collective-permute-start.12
  43.5 0.1 stack.187.scalars
  43.7 3.2 %collective-permute-start.7 = (bf16[160,3072]{1,0:T(8,128)(2,1)}, bf16[160,3072]{1,0:T(8,128)(2,1)S(1)}, u32[]{:S(2)}, u32[]{:S(2)}) collective-permute-start(bf16[160,3072]{1,0:T(8,128)(2,1)} %constant_dynamic-update-slice_fusion.refs_1_), channel_id=1, source_target_pairs={{0,2},{1,65},{2,4},{3,67},{4,6},{5,69},{6,0},{7,71},{64,66},{65,12... | collective-permute-start | bytes 2949128 | tf_op jit(solution)/shard_map/ppermute | solution.py:41
  46.9 1.9 %copy-done.1 = bf16[1,6144,256]{2,1,0:T(8,128)(2,1)S(1)} copy-done((bf16[1,6144,256]{2,1,0:T(8,128)(2,1)S(1)}, bf16[1,6144,256]{2,1,0:T(8,128)(2,1)}, u32[]{:S(2)}) %copy-start.1) | copy-done | bytes 3145752
  48.8 1.9 %copy-done.3 = bf16[1,6144,256]{2,1,0:T(8,128)(2,1)S(1)} copy-done((bf16[1,6144,256]{2,1,0:T(8,128)(2,1)S(1)}, bf16[1,6144,256]{2,1,0:T(8,128)(2,1)}, u32[]{:S(2)}) %copy-start.3) | copy-done | bytes 3145752
  50.7 4.9 %shard_map.65.refs_1_.refs_8_ = bf16[4,80,1024]{2,1,0:T(8,128)(2,1)S(1)} custom-call(s32[40]{0:T(128)S(1)} %stack.187.scalars, bf16[160,3072]{1,0:T(8,128)(2,1)S(1)} %pad_maximum_fusion.refs_0_, bf16[160,3072]{1,0:T(8,128)(2,1)} %constant_dynamic-update-slice_fusion.refs_1_, bf16[6144,256]{1,0:T(8,128)(2,1)S(1)} %bitcast.82, bf16[6144,256]{1,0:T(8,128)(2,1)S(1)} %bitcast.86, ...), custom_call_target="tpu_custom_call" | custom-call | flops 1048576 | bytes 1048576 | tf_op jit(solution)/shard_map/pallas_call | solution.py:115
  55.6 2.7 %collective-permute-done.12.refs_1_ = bf16[160,3072]{1,0:T(8,128)(2,1)} collective-permute-done((bf16[160,3072]{1,0:T(8,128)(2,1)}, bf16[160,3072]{1,0:T(8,128)(2,1)}, u32[]{:S(2)}, u32[]{:S(2)}) %collective-permute-start.12) | collective-permute-done | bytes 983072 | tf_op jit(solution)/shard_map/ppermute | solution.py:41
  58.4 4.8 %shard_map.67.refs_9_ = bf16[4,80,1024]{2,1,0:T(8,128)(2,1)S(1)} custom-call(s32[40]{0:T(128)S(1)} %stack.187.scalars, bf16[160,3072]{1,0:T(8,128)(2,1)S(1)} %collective-permute-done.10.refs_0_, bf16[160,3072]{1,0:T(8,128)(2,1)} %collective-permute-done.12.refs_1_, bf16[6144,256]{1,0:T(8,128)(2,1)S(1)} %bitcast.83, bf16[6144,256]{1,0:T(8,128)(2,1)S(1)} %bitcast.87, ...), custom_call_target="tpu_custom_call" | custom-call | flops 1048576 | bytes 1048576 | tf_op jit(solution)/shard_map/pallas_call | solution.py:115
  63.3 2.0 %collective-permute-start.13 = (bf16[160,3072]{1,0:T(8,128)(2,1)}, bf16[160,3072]{1,0:T(8,128)(2,1)S(1)}, u32[]{:S(2)}, u32[]{:S(2)}) collective-permute-start(bf16[160,3072]{1,0:T(8,128)(2,1)} %collective-permute-done.12.refs_1_), channel_id=1, source_target_pairs={{0,6},{1,193},{2,0},{3,195},{4,2},{5,197},{6,4},{7,199},{64,70},{6... | collective-permute-start | bytes 2949128 | tf_op jit(solution)/shard_map/ppermute | solution.py:41
  65.3 3.5 %collective-permute-done.9.refs_1_ = bf16[160,3072]{1,0:T(8,128)(2,1)S(1)} collective-permute-done((bf16[160,3072]{1,0:T(8,128)(2,1)S(1)}, bf16[160,3072]{1,0:T(8,128)(2,1)S(1)}, u32[]{:S(2)}, u32[]{:S(2)}) %collective-permute-start.9) | collective-permute-done | bytes 983072 | tf_op jit(solution)/shard_map/ppermute | solution.py:41
  68.8 8.6 %collective-permute-done.11.refs_2_ = bf16[160,3072]{1,0:T(8,128)(2,1)S(1)} collective-permute-done((bf16[160,3072]{1,0:T(8,128)(2,1)S(1)}, bf16[160,3072]{1,0:T(8,128)(2,1)S(1)}, u32[]{:S(2)}, u32[]{:S(2)}) %collective-permute-start.11) | collective-permute-done | bytes 983072 | tf_op jit(solution)/shard_map/ppermute | solution.py:41
  77.4 1.9 %collective-permute-done.13.refs_3_ = bf16[160,3072]{1,0:T(8,128)(2,1)S(1)} collective-permute-done((bf16[160,3072]{1,0:T(8,128)(2,1)}, bf16[160,3072]{1,0:T(8,128)(2,1)S(1)}, u32[]{:S(2)}, u32[]{:S(2)}) %collective-permute-start.13) | collective-permute-done | bytes 983072 | tf_op jit(solution)/shard_map/ppermute | solution.py:41
  79.3 7.2 %shard_map.68.sums = bf16[16,80,1024]{2,1,0:T(8,128)(2,1)S(1)} custom-call(s32[40]{0:T(128)S(1)} %stack.187.scalars, bf16[160,3072]{1,0:T(8,128)(2,1)S(1)} %collective-permute-done.7.refs_0_, bf16[160,3072]{1,0:T(8,128)(2,1)S(1)} %collective-permute-done.9.refs_1_, bf16[160,3072]{1,0:T(8,128)(2,1)S(1)} %collective-permute-done.11.refs_2_, ...), custom_call_target="tpu_custom_call" | custom-call | flops 1048576 | bytes 1048576 | tf_op jit(solution)/shard_map/pallas_call | solution.py:115
  86.6 0.1 collective-permute-start.14
  86.7 4.9 %collective-permute-done.14.got = bf16[16,80,1024]{2,1,0:T(8,128)(2,1)S(1)} collective-permute-done((bf16[16,80,1024]{2,1,0:T(8,128)(2,1)S(1)}, bf16[16,80,1024]{2,1,0:T(8,128)(2,1)S(1)}, u32[]{:S(2)}, u32[]{:S(2)}) %collective-permute-start.14) | collective-permute-done | bytes 2621472 | tf_op jit(solution)/shard_map/ppermute | solution.py:55
  91.6 3.2 %shard_map.69 = (bf16[1280,512]{1,0:T(8,128)(2,1)S(1)}, bf16[2,320,768]{2,1,0:T(8,128)(2,1)S(1)}, bf16[2,320,768]{2,1,0:T(8,128)(2,1)S(1)}) custom-call(s32[40]{0:T(128)S(1)} %stack.187.scalars, bf16[16,80,1024]{2,1,0:T(8,128)(2,1)S(1)} %shard_map.68.sums, bf16[16,80,1024]{2,1,0:T(8,128)(2,1)S(1)} %collective-permute-done.14.got, ...), custom_call_target="tpu_custom_call" | custom-call | flops 1048576 | bytes 1048576 | tf_op jit(solution)/shard_map/pallas_call | solution.py:186
  94.9 3.2 %collective-permute-start.20 = (bf16[2,320,768]{2,1,0:T(8,128)(2,1)S(1)}, bf16[2,320,768]{2,1,0:T(8,128)(2,1)S(1)}, u32[]{:S(2)}, u32[]{:S(2)}) collective-permute-start(bf16[2,320,768]{2,1,0:T(8,128)(2,1)S(1)} %get-tuple-element.22), channel_id=1, source_target_pairs={{0,192},{1,7},{2,194},{3,1},{4,196},{5,3},{6,198},{7,5},{64,0},{65... | collective-permute-start | bytes 2949128 | tf_op jit(solution)/shard_map/ppermute | solution.py:41
  98.1 5.3 %shard_map.70 = (bf16[2,320,768]{2,1,0:T(8,128)(2,1)S(1)}, bf16[2,320,768]{2,1,0:T(8,128)(2,1)S(1)}, bf16[2,320,768]{2,1,0:T(8,128)(2,1)S(1)}, bf16[2,320,768]{2,1,0:T(8,128)(2,1)S(1)}, bf16[4,320,768]{2,1,0:T(8,128)(2,1)S(1)}) custom-call(s32[40]{0:T(128)S(1)} %stack.187.scalars, bf16[1280,512]{1,0:T(8,128)(2,1)S(1)} %get-tuple-element.15.hidden, ...), custom_call_target="tpu_custom_call" | custom-call | flops 1048576 | bytes 1048576 | tf_op jit(solution)/shard_map/pallas_call | solution.py:230
  103.4 0.3 collective-permute-start.15
  103.7 2.0 %collective-permute-start.18 = (bf16[2,320,768]{2,1,0:T(8,128)(2,1)S(1)}, bf16[2,320,768]{2,1,0:T(8,128)(2,1)S(1)}, u32[]{:S(2)}, u32[]{:S(2)}) collective-permute-start(bf16[2,320,768]{2,1,0:T(8,128)(2,1)S(1)} %get-tuple-element.20), channel_id=1, source_target_pairs={{0,64},{1,3},{2,66},{3,5},{4,68},{5,7},{6,70},{7,1},{64,128},{65,6... | collective-permute-start | bytes 2949128 | tf_op jit(solution)/shard_map/ppermute | solution.py:41
  105.7 4.5 %collective-permute-done.16 = bf16[2,320,768]{2,1,0:T(8,128)(2,1)S(1)} collective-permute-done((bf16[2,320,768]{2,1,0:T(8,128)(2,1)S(1)}, bf16[2,320,768]{2,1,0:T(8,128)(2,1)S(1)}, u32[]{:S(2)}, u32[]{:S(2)}) %collective-permute-start.16) | collective-permute-done | bytes 983072 | tf_op jit(solution)/shard_map/ppermute | solution.py:41
  110.2 0.2 fusion.6
  110.5 0.2 fusion.8
  110.8 3.3 %collective-permute-start.21 = (bf16[320,768]{1,0:T(8,128)(2,1)S(1)}, bf16[320,768]{1,0:T(8,128)(2,1)S(1)}, u32[]{:S(2)}, u32[]{:S(2)}) collective-permute-start(bf16[320,768]{1,0:T(8,128)(2,1)S(1)} %get-tuple-element.30), channel_id=1, source_target_pairs={{0,192},{1,7},{2,194},{3,1},{4,196},{5,3},{6,198},{7,5},{64,0},{65... | collective-permute-start | bytes 1474568 | tf_op jit(solution)/shard_map/ppermute | solution.py:41
  114.1 6.2 %collective-permute-done.15.low = bf16[2,320,768]{2,1,0:T(8,128)(2,1)S(1)} collective-permute-done((bf16[2,320,768]{2,1,0:T(8,128)(2,1)S(1)}, bf16[2,320,768]{2,1,0:T(8,128)(2,1)S(1)}, u32[]{:S(2)}, u32[]{:S(2)}) %collective-permute-start.15) | collective-permute-done | bytes 983072 | tf_op jit(solution)/shard_map/ppermute | solution.py:41
  120.3 3.7 %collective-permute-start.24 = (bf16[320,768]{1,0:T(8,128)(2,1)S(1)}, bf16[320,768]{1,0:T(8,128)(2,1)S(1)}, u32[]{:S(2)}, u32[]{:S(2)}) collective-permute-start(bf16[320,768]{1,0:T(8,128)(2,1)S(1)} %get-tuple-element.29), channel_id=1, source_target_pairs={{0,192},{1,7},{2,194},{3,1},{4,196},{5,3},{6,198},{7,5},{64,0},{65... | collective-permute-start | bytes 1474568 | tf_op jit(solution)/shard_map/ppermute | solution.py:41
  124.0 2.0 %collective-permute-done.19.got_1 = bf16[320,768]{1,0:T(8,128)(2,1)S(1)} collective-permute-done((bf16[320,768]{1,0:T(8,128)(2,1)S(1)}, bf16[320,768]{1,0:T(8,128)(2,1)S(1)}, u32[]{:S(2)}, u32[]{:S(2)}) %collective-permute-start.19) | collective-permute-done | bytes 491552 | tf_op jit(solution)/shard_map/ppermute | solution.py:41
  126.0 1.3 shard_map.71
  127.3 0.3 collective-permute-start.22
  127.6 2.9 %collective-permute-start.23 = (bf16[320,768]{1,0:T(8,128)(2,1)}, bf16[320,768]{1,0:T(8,128)(2,1)S(1)}, u32[]{:S(2)}, u32[]{:S(2)}) collective-permute-start(bf16[320,768]{1,0:T(8,128)(2,1)} %get-tuple-element.24), channel_id=1, source_target_pairs={{0,2},{1,65},{2,4},{3,67},{4,6},{5,69},{6,0},{7,71},{64,66},{65,12... | collective-permute-start | bytes 1474568 | tf_op jit(solution)/shard_map/ppermute | solution.py:41
  130.5 0.8 collective-permute-done.17
  131.3 2.2 %collective-permute-done.24 = bf16[320,768]{1,0:T(8,128)(2,1)S(1)} collective-permute-done((bf16[320,768]{1,0:T(8,128)(2,1)S(1)}, bf16[320,768]{1,0:T(8,128)(2,1)S(1)}, u32[]{:S(2)}, u32[]{:S(2)}) %collective-permute-start.24) | collective-permute-done | bytes 491552 | tf_op jit(solution)/shard_map/ppermute | solution.py:41
  133.5 1.2 fusion.1
  134.7 2.8 %collective-permute-done.22 = bf16[320,768]{1,0:T(8,128)(2,1)S(1)} collective-permute-done((bf16[320,768]{1,0:T(8,128)(2,1)}, bf16[320,768]{1,0:T(8,128)(2,1)S(1)}, u32[]{:S(2)}, u32[]{:S(2)}) %collective-permute-start.22) | collective-permute-done | bytes 491552 | tf_op jit(solution)/shard_map/ppermute | solution.py:41
  137.5 4.9 %collective-permute-done.23 = bf16[320,768]{1,0:T(8,128)(2,1)S(1)} collective-permute-done((bf16[320,768]{1,0:T(8,128)(2,1)}, bf16[320,768]{1,0:T(8,128)(2,1)S(1)}, u32[]{:S(2)}, u32[]{:S(2)}) %collective-permute-start.23) | collective-permute-done | bytes 491552 | tf_op jit(solution)/shard_map/ppermute | solution.py:41
  142.4 2.8 %collective-permute-done.25 = bf16[320,768]{1,0:T(8,128)(2,1)S(1)} collective-permute-done((bf16[320,768]{1,0:T(8,128)(2,1)}, bf16[320,768]{1,0:T(8,128)(2,1)S(1)}, u32[]{:S(2)}, u32[]{:S(2)}) %collective-permute-start.25) | collective-permute-done | bytes 491552 | tf_op jit(solution)/shard_map/ppermute | solution.py:41
  145.2 1.6 shard_map.72
  146.8 11.2 %all-to-all-start = ((bf16[8,40,768]{2,1,0:T(8,128)(2,1)}), bf16[8,40,768]{2,1,0:T(8,128)(2,1)S(1)}, u32[]{:S(2)}, u32[]{:S(2)}) async-start(bf16[8,40,768]{2,1,0:T(8,128)(2,1)} %shard_map.72), calls=%async_computation | async-start | bytes 983040 | tf_op jit(solution)/shard_map/all_to_all | solution.py:347
  158.1 12.8 %all-to-all-done = bf16[8,40,768]{2,1,0:T(8,128)(2,1)S(1)} async-done(((bf16[8,40,768]{2,1,0:T(8,128)(2,1)}), bf16[8,40,768]{2,1,0:T(8,128)(2,1)S(1)}, u32[]{:S(2)}, u32[]{:S(2)}) %all-to-all-start) | async-done | bytes 491552 | tf_op jit(solution)/shard_map/all_to_all | solution.py:347
  170.9 0.3 fusion.9
  171.2 1.0 fusion
  (42 shorter events, 1.0 us)
Async XLA Ops:
  0.0 3.7 %copy-start = (bf16[128,6144]{1,0:T(8,128)(2,1)S(1)}, bf16[128,6144]{1,0:T(8,128)(2,1)}, u32[]{:S(2)}) copy-start(bf16[128,6144]{1,0:T(8,128)(2,1)} %param.6) | copy-start | bytes 4718596
  0.0 23.2 %collective-permute-start.2 = (bf16[6144,256]{1,0:T(8,128)(2,1)}, bf16[6144,256]{1,0:T(8,128)(2,1)}, u32[]{:S(2)}, u32[]{:S(2)}) collective-permute-start(bf16[6144,256]{1,0:T(8,128)(2,1)} %bitcast.81), channel_id=1, source_target_pairs={{0,1},{1,0},{2,3},{3,2},{4,5},{5,4},{6,7},{7,6},{8,9},{9,8},{10,11... | collective-permute-start | bytes 9437192 | tf_op jit(solution)/shard_map/ppermute | solution.py:55
  0.0 23.2 %collective-permute-start.3 = (bf16[6144,256]{1,0:T(8,128)(2,1)}, bf16[6144,256]{1,0:T(8,128)(2,1)}, u32[]{:S(2)}, u32[]{:S(2)}) collective-permute-start(bf16[6144,256]{1,0:T(8,128)(2,1)} %bitcast.85), channel_id=1, source_target_pairs={{0,1},{1,0},{2,3},{3,2},{4,5},{5,4},{6,7},{7,6},{8,9},{9,8},{10,11... | collective-permute-start | bytes 9437192 | tf_op jit(solution)/shard_map/ppermute | solution.py:55
  0.5 22.7 %collective-permute-start.4 = (bf16[256,6144]{1,0:T(8,128)(2,1)}, bf16[256,6144]{1,0:T(8,128)(2,1)}, u32[]{:S(2)}, u32[]{:S(2)}) collective-permute-start(bf16[256,6144]{1,0:T(8,128)(2,1)} %bitcast.89), channel_id=1, source_target_pairs={{0,1},{1,0},{2,3},{3,2},{4,5},{5,4},{6,7},{7,6},{8,9},{9,8},{10,11... | collective-permute-start | bytes 9437192 | tf_op jit(solution)/shard_map/ppermute | solution.py:55
  3.9 18.8 %collective-permute-start = (bf16[40,3072]{1,0:T(8,128)(2,1)S(1)}, bf16[40,3072]{1,0:T(8,128)(2,1)S(1)}, u32[]{:S(2)}, u32[]{:S(2)}) collective-permute-start(bf16[40,3072]{1,0:T(8,128)(2,1)S(1)} %convolution_convert_fusion.1), channel_id=1, source_target_pairs={{0,0},{1,1},{2,10},{3,27},{4,20},{5,21},{6,30},{7,15},{8,8},{9,9},... | collective-permute-start | bytes 737288 | tf_op jit(solution)/shard_map/ppermute | solution.py:51
  10.7 12.4 %collective-permute-start.1 = (bf16[40,3072]{1,0:T(8,128)(2,1)S(1)}, bf16[40,3072]{1,0:T(8,128)(2,1)S(1)}, u32[]{:S(2)}, u32[]{:S(2)}) collective-permute-start(bf16[40,3072]{1,0:T(8,128)(2,1)S(1)} %convolution_convert_fusion), channel_id=1, source_target_pairs={{0,32},{1,33},{2,58},{3,43},{4,52},{5,53},{6,46},{7,63},{8,40},{9,... | collective-permute-start | bytes 737288 | tf_op jit(solution)/shard_map/ppermute | solution.py:51
  23.2 10.1 %collective-permute-start.8 = (bf16[80,3072]{1,0:T(8,128)(2,1)S(1)}, bf16[80,3072]{1,0:T(8,128)(2,1)S(1)}, u32[]{:S(2)}, u32[]{:S(2)}) collective-permute-start(bf16[80,3072]{1,0:T(8,128)(2,1)S(1)} %shard_map.64), channel_id=1, source_target_pairs={{0,64},{1,3},{2,66},{3,5},{4,68},{5,7},{6,70},{7,1},{64,128},{65,6... | collective-permute-start | bytes 1474568 | tf_op jit(solution)/shard_map/ppermute | solution.py:41
  24.8 13.4 %collective-permute-start.5 = (bf16[80,3072]{1,0:T(8,128)(2,1)S(1)}, bf16[80,3072]{1,0:T(8,128)(2,1)S(1)}, u32[]{:S(2)}, u32[]{:S(2)}) collective-permute-start(bf16[80,3072]{1,0:T(8,128)(2,1)S(1)} %shard_map.64), channel_id=1, source_target_pairs={{0,192},{1,7},{2,194},{3,1},{4,196},{5,3},{6,198},{7,5},{64,0},{65... | collective-permute-start | bytes 1474568 | tf_op jit(solution)/shard_map/ppermute | solution.py:41
  26.5 15.4 %collective-permute-start.6 = (bf16[80,3072]{1,0:T(8,128)(2,1)S(1)}, bf16[80,3072]{1,0:T(8,128)(2,1)S(1)}, u32[]{:S(2)}, u32[]{:S(2)}) collective-permute-start(bf16[80,3072]{1,0:T(8,128)(2,1)S(1)} %shard_map.64), channel_id=1, source_target_pairs={{0,128},{1,5},{2,130},{3,7},{4,132},{5,1},{6,134},{7,3},{64,192},{... | collective-permute-start | bytes 1474568 | tf_op jit(solution)/shard_map/ppermute | solution.py:41
  33.4 22.2 %collective-permute-start.10 = (bf16[160,3072]{1,0:T(8,128)(2,1)S(1)}, bf16[160,3072]{1,0:T(8,128)(2,1)S(1)}, u32[]{:S(2)}, u32[]{:S(2)}) collective-permute-start(bf16[160,3072]{1,0:T(8,128)(2,1)S(1)} %pad_maximum_fusion.refs_0_), channel_id=1, source_target_pairs={{0,2},{1,65},{2,4},{3,67},{4,6},{5,69},{6,0},{7,71},{64,66},{65,12... | collective-permute-start | bytes 2949128 | tf_op jit(solution)/shard_map/ppermute | solution.py:41
  42.7 15.6 %collective-permute-start.12 = (bf16[160,3072]{1,0:T(8,128)(2,1)}, bf16[160,3072]{1,0:T(8,128)(2,1)}, u32[]{:S(2)}, u32[]{:S(2)}) collective-permute-start(bf16[160,3072]{1,0:T(8,128)(2,1)} %constant_dynamic-update-slice_fusion.refs_1_), channel_id=1, source_target_pairs={{0,6},{1,193},{2,0},{3,195},{4,2},{5,197},{6,4},{7,199},{64,70},{6... | collective-permute-start | bytes 2949128 | tf_op jit(solution)/shard_map/ppermute | solution.py:41
  43.6 25.2 %collective-permute-start.9 = (bf16[160,3072]{1,0:T(8,128)(2,1)S(1)}, bf16[160,3072]{1,0:T(8,128)(2,1)S(1)}, u32[]{:S(2)}, u32[]{:S(2)}) collective-permute-start(bf16[160,3072]{1,0:T(8,128)(2,1)S(1)} %pad_maximum_fusion.refs_0_), channel_id=1, source_target_pairs={{0,6},{1,193},{2,0},{3,195},{4,2},{5,197},{6,4},{7,199},{64,70},{6... | collective-permute-start | bytes 2949128 | tf_op jit(solution)/shard_map/ppermute | solution.py:41
  43.7 25.1 %collective-permute-start.7 = (bf16[160,3072]{1,0:T(8,128)(2,1)}, bf16[160,3072]{1,0:T(8,128)(2,1)S(1)}, u32[]{:S(2)}, u32[]{:S(2)}) collective-permute-start(bf16[160,3072]{1,0:T(8,128)(2,1)} %constant_dynamic-update-slice_fusion.refs_1_), channel_id=1, source_target_pairs={{0,2},{1,65},{2,4},{3,67},{4,6},{5,69},{6,0},{7,71},{64,66},{65,12... | collective-permute-start | bytes 2949128 | tf_op jit(solution)/shard_map/ppermute | solution.py:41
  46.9 1.9 %copy-start.1 = (bf16[1,6144,256]{2,1,0:T(8,128)(2,1)S(1)}, bf16[1,6144,256]{2,1,0:T(8,128)(2,1)}, u32[]{:S(2)}) copy-start(bf16[1,6144,256]{2,1,0:T(8,128)(2,1)} %param.9) | copy-start | bytes 9437188
  48.8 1.9 %copy-start.3 = (bf16[1,6144,256]{2,1,0:T(8,128)(2,1)S(1)}, bf16[1,6144,256]{2,1,0:T(8,128)(2,1)}, u32[]{:S(2)}) copy-start(bf16[1,6144,256]{2,1,0:T(8,128)(2,1)} %param.10) | copy-start | bytes 9437188
  50.7 7.7 %copy-start.2 = (bf16[1,6144,256]{2,1,0:T(8,128)(2,1)S(1)}, bf16[1,6144,256]{2,1,0:T(8,128)(2,1)}, u32[]{:S(2)}) copy-start(bf16[1,6144,256]{2,1,0:T(8,128)(2,1)} %param.9) | copy-start | bytes 9437188
  63.2 14.2 %collective-permute-start.11 = (bf16[160,3072]{1,0:T(8,128)(2,1)S(1)}, bf16[160,3072]{1,0:T(8,128)(2,1)S(1)}, u32[]{:S(2)}, u32[]{:S(2)}) collective-permute-start(bf16[160,3072]{1,0:T(8,128)(2,1)S(1)} %shard_map.66), channel_id=1, source_target_pairs={{0,2},{1,65},{2,4},{3,67},{4,6},{5,69},{6,0},{7,71},{64,66},{65,12... | collective-permute-start | bytes 2949128 | tf_op jit(solution)/shard_map/ppermute | solution.py:41
  63.3 16.0 %collective-permute-start.13 = (bf16[160,3072]{1,0:T(8,128)(2,1)}, bf16[160,3072]{1,0:T(8,128)(2,1)S(1)}, u32[]{:S(2)}, u32[]{:S(2)}) collective-permute-start(bf16[160,3072]{1,0:T(8,128)(2,1)} %collective-permute-done.12.refs_1_), channel_id=1, source_target_pairs={{0,6},{1,193},{2,0},{3,195},{4,2},{5,197},{6,4},{7,199},{64,70},{6... | collective-permute-start | bytes 2949128 | tf_op jit(solution)/shard_map/ppermute | solution.py:41
  79.3 12.2 %copy-start.4 = (bf16[1,256,6144]{2,1,0:T(8,128)(2,1)S(1)}, bf16[1,256,6144]{2,1,0:T(8,128)(2,1)}, u32[]{:S(2)}) copy-start(bf16[1,256,6144]{2,1,0:T(8,128)(2,1)} %param.11) | copy-start | bytes 9437188
  86.6 5.0 %collective-permute-start.14 = (bf16[16,80,1024]{2,1,0:T(8,128)(2,1)S(1)}, bf16[16,80,1024]{2,1,0:T(8,128)(2,1)S(1)}, u32[]{:S(2)}, u32[]{:S(2)}) collective-permute-start(bf16[16,80,1024]{2,1,0:T(8,128)(2,1)S(1)} %shard_map.68.sums), channel_id=1, source_target_pairs={{0,1},{1,0},{2,3},{3,2},{4,5},{5,4},{6,7},{7,6},{8,9},{9,8},{10,11... | collective-permute-start | bytes 7864328 | tf_op jit(solution)/shard_map/ppermute | solution.py:55
  94.8 15.4 %collective-permute-start.16 = (bf16[2,320,768]{2,1,0:T(8,128)(2,1)S(1)}, bf16[2,320,768]{2,1,0:T(8,128)(2,1)S(1)}, u32[]{:S(2)}, u32[]{:S(2)}) collective-permute-start(bf16[2,320,768]{2,1,0:T(8,128)(2,1)S(1)} %get-tuple-element.19), channel_id=1, source_target_pairs={{0,64},{1,3},{2,66},{3,5},{4,68},{5,7},{6,70},{7,1},{64,128},{65,6... | collective-permute-start | bytes 2949128 | tf_op jit(solution)/shard_map/ppermute | solution.py:41
  94.9 15.6 %collective-permute-start.20 = (bf16[2,320,768]{2,1,0:T(8,128)(2,1)S(1)}, bf16[2,320,768]{2,1,0:T(8,128)(2,1)S(1)}, u32[]{:S(2)}, u32[]{:S(2)}) collective-permute-start(bf16[2,320,768]{2,1,0:T(8,128)(2,1)S(1)} %get-tuple-element.22), channel_id=1, source_target_pairs={{0,192},{1,7},{2,194},{3,1},{4,196},{5,3},{6,198},{7,5},{64,0},{65... | collective-permute-start | bytes 2949128 | tf_op jit(solution)/shard_map/ppermute | solution.py:41
  103.4 16.9 %collective-permute-start.15 = (bf16[2,320,768]{2,1,0:T(8,128)(2,1)S(1)}, bf16[2,320,768]{2,1,0:T(8,128)(2,1)S(1)}, u32[]{:S(2)}, u32[]{:S(2)}) collective-permute-start(bf16[2,320,768]{2,1,0:T(8,128)(2,1)S(1)} %get-tuple-element.17), channel_id=1, source_target_pairs={{0,192},{1,7},{2,194},{3,1},{4,196},{5,3},{6,198},{7,5},{64,0},{65... | collective-permute-start | bytes 2949128 | tf_op jit(solution)/shard_map/ppermute | solution.py:41
  103.7 20.3 %collective-permute-start.18 = (bf16[2,320,768]{2,1,0:T(8,128)(2,1)S(1)}, bf16[2,320,768]{2,1,0:T(8,128)(2,1)S(1)}, u32[]{:S(2)}, u32[]{:S(2)}) collective-permute-start(bf16[2,320,768]{2,1,0:T(8,128)(2,1)S(1)} %get-tuple-element.20), channel_id=1, source_target_pairs={{0,64},{1,3},{2,66},{3,5},{4,68},{5,7},{6,70},{7,1},{64,128},{65,6... | collective-permute-start | bytes 2949128 | tf_op jit(solution)/shard_map/ppermute | solution.py:41
  110.4 15.6 %collective-permute-start.19 = (bf16[320,768]{1,0:T(8,128)(2,1)S(1)}, bf16[320,768]{1,0:T(8,128)(2,1)S(1)}, u32[]{:S(2)}, u32[]{:S(2)}) collective-permute-start(bf16[320,768]{1,0:T(8,128)(2,1)S(1)} %get-tuple-element.31), channel_id=1, source_target_pairs={{0,64},{1,3},{2,66},{3,5},{4,68},{5,7},{6,70},{7,1},{64,128},{65,6... | collective-permute-start | bytes 1474568 | tf_op jit(solution)/shard_map/ppermute | solution.py:41
  110.8 15.2 %collective-permute-start.21 = (bf16[320,768]{1,0:T(8,128)(2,1)S(1)}, bf16[320,768]{1,0:T(8,128)(2,1)S(1)}, u32[]{:S(2)}, u32[]{:S(2)}) collective-permute-start(bf16[320,768]{1,0:T(8,128)(2,1)S(1)} %get-tuple-element.30), channel_id=1, source_target_pairs={{0,192},{1,7},{2,194},{3,1},{4,196},{5,3},{6,198},{7,5},{64,0},{65... | collective-permute-start | bytes 1474568 | tf_op jit(solution)/shard_map/ppermute | solution.py:41
  114.1 17.2 %collective-permute-start.17 = (bf16[320,768]{1,0:T(8,128)(2,1)S(1)}, bf16[320,768]{1,0:T(8,128)(2,1)S(1)}, u32[]{:S(2)}, u32[]{:S(2)}) collective-permute-start(bf16[320,768]{1,0:T(8,128)(2,1)S(1)} %get-tuple-element.32), channel_id=1, source_target_pairs={{0,64},{1,3},{2,66},{3,5},{4,68},{5,7},{6,70},{7,1},{64,128},{65,6... | collective-permute-start | bytes 1474568 | tf_op jit(solution)/shard_map/ppermute | solution.py:41
  120.3 13.2 %collective-permute-start.24 = (bf16[320,768]{1,0:T(8,128)(2,1)S(1)}, bf16[320,768]{1,0:T(8,128)(2,1)S(1)}, u32[]{:S(2)}, u32[]{:S(2)}) collective-permute-start(bf16[320,768]{1,0:T(8,128)(2,1)S(1)} %get-tuple-element.29), channel_id=1, source_target_pairs={{0,192},{1,7},{2,194},{3,1},{4,196},{5,3},{6,198},{7,5},{64,0},{65... | collective-permute-start | bytes 1474568 | tf_op jit(solution)/shard_map/ppermute | solution.py:41
  127.3 10.3 %collective-permute-start.22 = (bf16[320,768]{1,0:T(8,128)(2,1)}, bf16[320,768]{1,0:T(8,128)(2,1)S(1)}, u32[]{:S(2)}, u32[]{:S(2)}) collective-permute-start(bf16[320,768]{1,0:T(8,128)(2,1)} %get-tuple-element.23), channel_id=1, source_target_pairs={{0,6},{1,193},{2,0},{3,195},{4,2},{5,197},{6,4},{7,199},{64,70},{6... | collective-permute-start | bytes 1474568 | tf_op jit(solution)/shard_map/ppermute | solution.py:41
  127.6 14.9 %collective-permute-start.23 = (bf16[320,768]{1,0:T(8,128)(2,1)}, bf16[320,768]{1,0:T(8,128)(2,1)S(1)}, u32[]{:S(2)}, u32[]{:S(2)}) collective-permute-start(bf16[320,768]{1,0:T(8,128)(2,1)} %get-tuple-element.24), channel_id=1, source_target_pairs={{0,2},{1,65},{2,4},{3,67},{4,6},{5,69},{6,0},{7,71},{64,66},{65,12... | collective-permute-start | bytes 1474568 | tf_op jit(solution)/shard_map/ppermute | solution.py:41
  134.7 23.3 %copy-start.5 = (f32[128,2]{0,1:T(2,128)S(1)}, f32[128,2]{0,1:T(2,128)}, u32[]{:S(2)}) copy-start(f32[128,2]{0,1:T(2,128)} %param.8) | copy-start | bytes 3076
  134.7 10.5 %collective-permute-start.25 = (bf16[320,768]{1,0:T(8,128)(2,1)}, bf16[320,768]{1,0:T(8,128)(2,1)S(1)}, u32[]{:S(2)}, u32[]{:S(2)}) collective-permute-start(bf16[320,768]{1,0:T(8,128)(2,1)} %get-tuple-element.27), channel_id=1, source_target_pairs={{0,4},{1,129},{2,6},{3,131},{4,0},{5,133},{6,2},{7,135},{64,68},{6... | collective-permute-start | bytes 1474568 | tf_op jit(solution)/shard_map/ppermute | solution.py:41
  146.8 24.1 %all-to-all-start = ((bf16[8,40,768]{2,1,0:T(8,128)(2,1)}), bf16[8,40,768]{2,1,0:T(8,128)(2,1)S(1)}, u32[]{:S(2)}, u32[]{:S(2)}) async-start(bf16[8,40,768]{2,1,0:T(8,128)(2,1)} %shard_map.72), calls=%async_computation | async-start | bytes 983040 | tf_op jit(solution)/shard_map/all_to_all | solution.py:347

commit v3 on v2

--- a/solution.py
+++ b/solution.py
@@ -238,8 +238,8 @@
     )(scalars, hidden, mine, theirs)
 
 
-def mid_kernel(own, high, low, got_1, got_2, mid_1, mid_2):
-    for i, parts, out in ((1, (low.at[1], got_1), mid_1), (2, (high.at[0], got_2), mid_2)):
+def mid_kernel(own, high, low, got_1, got_3, mid_1, mid_3):
+    for i, parts, out in ((1, (low.at[1], got_1), mid_1), (3, (high.at[1], got_3), mid_3)):
         total = own[i].astype(F32)
         for part in parts:
             total = total + part[...].astype(F32)
@@ -282,22 +282,23 @@
     part = half // 4
     y, c, z = lax.axis_index("ty"), lax.axis_index("core"), lax.axis_index("expert")
 
-    expert_ids = routes.reshape(-1)
-    onehot = (expert_ids[:, None] == jnp.arange(E, dtype=jnp.int32)[None, :]).astype(jnp.int32)
-    before = jnp.cumsum(onehot, axis=0) - onehot
-    slot_index = jnp.sum(before * onehot, axis=1)
-    target = (expert_ids * CAP + slot_index).reshape(rows, 2)
+    ids = jnp.arange(E, dtype=jnp.int32)[:, None]
+    named = (routes[:, 0][None, :] == ids) | (routes[:, 1][None, :] == ids)
+    numbers = jnp.arange(rows, dtype=jnp.int32)
+    earlier = (numbers[:, None] < numbers[None, :]).astype(BF)
+    before = dot(named.astype(BF), earlier)
     columns = lax.dynamic_slice_in_dim(tokens, c * half, half, 1)
-    slots = jnp.arange(CAP, dtype=jnp.int32)
+    slots = jnp.arange(CAP, dtype=jnp.int32).astype(F32)
     line = jnp.where(c == 0, y, -y % 4)
 
     def outgoing(j):
         step = jnp.int32(ROUTES[0][j])
         for number in range(1, 4):
             step = jnp.where(line == number, ROUTES[number][j], step)
-        places = (z + step + 8) % 8 * CAP + slots
-        hit = places[:, None, None] == target[None, :, :]
-        return dot(jnp.any(hit, axis=2).astype(BF), columns).astype(BF)
+        expert = (z + step + 8) % 8
+        row = lambda v: lax.dynamic_slice_in_dim(v, expert, 1, 0)
+        hit = row(named) & (row(before) == slots[:, None])
+        return dot(hit.astype(BF), columns).astype(BF)
 
     w_gate, w_up, w_down = w_gate[0], w_up[0], w_down[0]
     weights = [w_gate, w_up, swap(w_gate), swap(w_up)]
@@ -317,18 +318,18 @@
 
     low = jnp.concatenate([piece, plane(piece, 0, 1)], axis=0)
     high = jnp.concatenate([plane(piece, 0, -1), plane(piece, 0, 2)], axis=0)
-    below_low, above_high = plane(low, 1, 1), plane(high, 1, -1)
-    below_high, above_low = plane(high, 1, 1), plane(low, 1, -1)
+    below_low, above_low = plane(low, 1, 1), plane(low, 1, -1)
+    below_high, above_high = plane(high, 1, 1), plane(high, 1, -1)
     own_sums = gate_up([low, high], (0, 2), weights, scalars)
     far = [plane(after(below_low, own_sums), 1, 1), plane(above_high, 1, -1)]
-    near_sums = gate_up([below_low, above_high], (0, 2), weights, scalars)
+    near_sums = gate_up([below_low, above_low], (0, 2), weights, scalars)
     sums = gate_up(
-        [below_high, above_low, *far],
-        (6, 8, 12, 14),
+        [below_high, above_high, *far],
+        (6, 10, 12, 14),
         weights,
         scalars,
         [own_sums, near_sums],
-        ((0, 0, 0), (0, 2, 2), (1, 0, 4), (1, 2, 10)),
+        ((0, 0, 0), (0, 2, 2), (1, 0, 4), (1, 2, 8)),
     )
     hidden, far_a, far_b = hidden_of(sums, swap(sums), *downs, scalars)
     below_a, below_b, above_a, above_b, own = down_of(hidden, *downs, scalars)
@@ -337,22 +338,24 @@
     got_high, got_low = plane(above_b, 0, 1), plane(below_a, 0, -1)
     to_above = [add(above_a[i], from_below[i]) for i in range(2)]
     to_below = [add(below_b[i], from_above[i]) for i in range(2)]
-    got_1, got_2 = plane(to_above[1], 0, 1), plane(to_below[0], 0, -1)
-    got_0, got_3 = plane(to_above[0], 0, 1), plane(to_below[1], 0, -1)
-    mid_1, mid_2 = mid_sums(own, got_high, got_low, got_1, got_2)
-    end_1, end_2 = plane(mid_1, 1, -1), plane(mid_2, 1, 1)
-    mid_0, mid_3 = add(own[0], got_low[0], got_0), add(own[3], got_high[1], got_3)
-    ends = [mid_0, end_1, end_2, plane(mid_3, 1, 2)]
+    got_1, got_3 = plane(to_above[1], 0, 1), plane(to_below[1], 0, -1)
+    got_0, got_2 = plane(to_above[0], 0, 1), plane(to_below[0], 0, -1)
+    mid_1, mid_3 = mid_sums(own, got_high, got_low, got_1, got_3)
+    end_3, end_1 = plane(mid_3, 1, 2), plane(mid_1, 1, -1)
+    mid_0, mid_2 = add(own[0], got_low[0], got_0), add(own[2], got_high[0], got_2)
+    ends = [mid_0, end_1, plane(mid_2, 1, 1), end_3]
     places = jnp.stack([(z - step + 8) % 8 for pair in ROUTES for step in pair]).astype(jnp.int32)
     table = lax.all_to_all(last_sum(places, ends), "expert", 0, 0, tiled=True)
     table = table.reshape(E * CAP, part)
 
     share = jax.nn.sigmoid(logits - logits[:, ::-1])
-    hit = jnp.arange(E * CAP, dtype=jnp.int32)[None, :, None] == target[:, None, :]
-    mix = jnp.sum(jnp.where(hit, share[:, None, :], 0.0), axis=2)
+    shares = [jnp.where(routes[:, k][None, :] == ids, share[:, k][None, :], 0.0) for k in range(2)]
+    hit = named[:, None, :] & (before[:, None, :] == slots[None, :, None])
+    mix = jnp.where(hit, (shares[0] + shares[1])[:, None, :], 0.0).reshape(E * CAP, rows)
     high_mix = mix.astype(BF)
     low_mix = (mix - high_mix.astype(F32)).astype(BF)
-    return (dot(high_mix, table) + dot(low_mix, table)).astype(BF)
+    back = lambda m: lax.dot_general(m, table, (((0,), (0,)), ((), ())), preferred_element_type=F32)
+    return (back(high_mix) + back(low_mix)).astype(BF)
 
 
 def solution(mesh):

time: 173 us -> 170 us (0.983)
  waiting for transfers between devices: 83.4 us -> 80.7 us
    ppermute x20, waiting for transfers between devices: 55.4 us -> 51.4 us  [plane(): return lax.ppermute(value, ('dp', 'ty', 'core'), pairs)]
    unnamed x14 -> x15, local copies, waits for them, and re-layouts: 5.4 us -> 4.96 us
  transfers between devices with their start and end apart: 27 -> 27, of which waited for: 19 -> 16; matrix products, arithmetic and copies ran while one was open for 4% -> 5% of each run, Pallas kernels for 9% -> 10%
where the time goes in v3:
time: 170 us; the launch traced here: 169 us
  waiting for transfers between devices  80.7 us (47%)
  starting transfers between devices  46.5 us (27%)
  Pallas kernels  28.2 us (17%)
  local copies, waits for them, and re-layouts  8.59 us (5%)
  other arithmetic  3.05 us (2%)
  matrix products  2.12 us (1%)
    ppermute x20, waiting for transfers between devices, plane(): return lax.ppermute(value, ('dp', 'ty', 'core'), pairs)  51.4 us
    ppermute x20, starting transfers between devices, plane(): return lax.ppermute(value, ('dp', 'ty', 'core'), pairs)  26.7 us
    pallas_call x3, Pallas kernels, gate_up(): pl.pallas_call(functools.partial(gate_up_kernel, places, merges), in_spec...  16.9 us
    all_to_all x1, waiting for transfers between devices, body(): table = lax.all_to_all(last_sum(places, ends), 'expert', 0, 0, tiled=True)  14.2 us
    all_to_all x1, starting transfers between devices, body(): table = lax.all_to_all(last_sum(places, ends), 'expert', 0, 0, tiled=True)  10.4 us
    ppermute x2, waiting for transfers between devices, along_z(): return lax.ppermute(value, ('expert', 'ty', 'core'), pairs)  10.2 us
    ppermute x2, starting transfers between devices, along_z(): return lax.ppermute(value, ('expert', 'ty', 'core'), pairs)  8.74 us
    pallas_call x1, Pallas kernels, down_of(): pl.pallas_call(down_kernel, in_specs=[SMEM, VMEM, HBM, HBM], out_specs=[V...  5.27 us
  transfers between devices with their start and end apart: 27, of which 16 were waited for; matrix products, arithmetic and copies ran while one was open for 5% of the time, Pallas kernels for 10%

profile of v3, /device:TPU:24, one launch (start us, length us, event | category | flops | bytes accessed | tf_op | source)
XLA Modules:
  0.0 169.4 jit_solution(9285883864010170773)
XLA Ops:
  0.0 0.5 collective-permute-start.3
  0.5 0.1 collective-permute-start.4
  0.6 0.8 slice_bitcast_fusion.3
  1.4 0.1 fusion.22
  1.5 0.3 copy-done.5
  1.9 0.3 convolution_convert_fusion.1
  2.2 6.5 %collective-permute-start = (bf16[40,3072]{1,0:T(8,128)(2,1)S(1)}, bf16[40,3072]{1,0:T(8,128)(2,1)S(1)}, u32[]{:S(2)}, u32[]{:S(2)}) collective-permute-start(bf16[40,3072]{1,0:T(8,128)(2,1)S(1)} %convolution_convert_fusion.1), channel_id=1, source_target_pairs={{0,0},{1,1},{2,10},{3,27},{4,20},{5,21},{6,30},{7,15},{8,8},{9,9},... | collective-permute-start | bytes 737288 | tf_op jit(solution)/shard_map/ppermute | solution.py:51
  8.7 0.3 convolution_convert_fusion
  9.0 2.2 %collective-permute-start.1 = (bf16[40,3072]{1,0:T(8,128)(2,1)S(1)}, bf16[40,3072]{1,0:T(8,128)(2,1)S(1)}, u32[]{:S(2)}, u32[]{:S(2)}) collective-permute-start(bf16[40,3072]{1,0:T(8,128)(2,1)S(1)} %convolution_convert_fusion), channel_id=1, source_target_pairs={{0,32},{1,33},{2,58},{3,43},{4,52},{5,53},{6,46},{7,63},{8,40},{9,... | collective-permute-start | bytes 737288 | tf_op jit(solution)/shard_map/ppermute | solution.py:51
  11.2 9.7 %collective-permute-done = bf16[40,3072]{1,0:T(8,128)(2,1)S(1)} collective-permute-done((bf16[40,3072]{1,0:T(8,128)(2,1)S(1)}, bf16[40,3072]{1,0:T(8,128)(2,1)S(1)}, u32[]{:S(2)}, u32[]{:S(2)}) %collective-permute-start) | collective-permute-done | bytes 245792 | tf_op jit(solution)/shard_map/ppermute | solution.py:51
  20.9 0.5 collective-permute-done.1
  21.5 1.6 collective-permute-start.9
  23.1 1.7 %collective-permute-start.5 = (bf16[80,3072]{1,0:T(8,128)(2,1)S(1)}, bf16[80,3072]{1,0:T(8,128)(2,1)S(1)}, u32[]{:S(2)}, u32[]{:S(2)}) collective-permute-start(bf16[80,3072]{1,0:T(8,128)(2,1)S(1)} %shard_map.64), channel_id=1, source_target_pairs={{0,192},{1,7},{2,194},{3,1},{4,196},{5,3},{6,198},{7,5},{64,0},{65... | collective-permute-start | bytes 1474568 | tf_op jit(solution)/shard_map/ppermute | solution.py:41
  24.8 1.8 %collective-permute-start.6 = (bf16[80,3072]{1,0:T(8,128)(2,1)S(1)}, bf16[80,3072]{1,0:T(8,128)(2,1)S(1)}, u32[]{:S(2)}, u32[]{:S(2)}) collective-permute-start(bf16[80,3072]{1,0:T(8,128)(2,1)S(1)} %shard_map.64), channel_id=1, source_target_pairs={{0,128},{1,5},{2,130},{3,7},{4,132},{5,1},{6,134},{7,3},{64,192},{... | collective-permute-start | bytes 1474568 | tf_op jit(solution)/shard_map/ppermute | solution.py:41
  26.6 5.0 %collective-permute-done.9 = bf16[80,3072]{1,0:T(8,128)(2,1)S(1)} collective-permute-done((bf16[80,3072]{1,0:T(8,128)(2,1)S(1)}, bf16[80,3072]{1,0:T(8,128)(2,1)S(1)}, u32[]{:S(2)}, u32[]{:S(2)}) %collective-permute-start.9) | collective-permute-done | bytes 491552 | tf_op jit(solution)/shard_map/ppermute | solution.py:41
  31.8 3.1 %collective-permute-start.13 = (bf16[160,3072]{1,0:T(8,128)(2,1)S(1)}, bf16[160,3072]{1,0:T(8,128)(2,1)}, u32[]{:S(2)}, u32[]{:S(2)}) collective-permute-start(bf16[160,3072]{1,0:T(8,128)(2,1)S(1)} %pad_maximum_fusion.refs_0_), channel_id=1, source_target_pairs={{0,6},{1,193},{2,0},{3,195},{4,2},{5,197},{6,4},{7,199},{64,70},{6... | collective-permute-start | bytes 2949128 | tf_op jit(solution)/shard_map/ppermute | solution.py:41
  34.9 0.8 constant_dynamic-update-slice_fusion.1
  35.8 4.4 %collective-permute-done.6 = bf16[80,3072]{1,0:T(8,128)(2,1)S(1)} collective-permute-done((bf16[80,3072]{1,0:T(8,128)(2,1)S(1)}, bf16[80,3072]{1,0:T(8,128)(2,1)S(1)}, u32[]{:S(2)}, u32[]{:S(2)}) %collective-permute-start.6) | collective-permute-done | bytes 491552 | tf_op jit(solution)/shard_map/ppermute | solution.py:41
  40.2 0.9 constant_dynamic-update-slice_fusion.refs_1_
  41.1 0.7 collective-permute-start.8
  41.8 0.5 broadcast.94
  42.3 0.7 stack.187.scalars
  43.0 2.6 %collective-permute-start.7 = (bf16[160,3072]{1,0:T(8,128)(2,1)}, bf16[160,3072]{1,0:T(8,128)(2,1)S(1)}, u32[]{:S(2)}, u32[]{:S(2)}) collective-permute-start(bf16[160,3072]{1,0:T(8,128)(2,1)} %constant_dynamic-update-slice_fusion.refs_1_), channel_id=1, source_target_pairs={{0,2},{1,65},{2,4},{3,67},{4,6},{5,69},{6,0},{7,71},{64,66},{65,12... | collective-permute-start | bytes 2949128 | tf_op jit(solution)/shard_map/ppermute | solution.py:41
  45.6 1.9 %copy-done.1 = bf16[1,6144,256]{2,1,0:T(8,128)(2,1)S(1)} copy-done((bf16[1,6144,256]{2,1,0:T(8,128)(2,1)S(1)}, bf16[1,6144,256]{2,1,0:T(8,128)(2,1)}, u32[]{:S(2)}) %copy-start.1) | copy-done | bytes 3145752
  47.5 1.9 %copy-done.3 = bf16[1,6144,256]{2,1,0:T(8,128)(2,1)S(1)} copy-done((bf16[1,6144,256]{2,1,0:T(8,128)(2,1)S(1)}, bf16[1,6144,256]{2,1,0:T(8,128)(2,1)}, u32[]{:S(2)}) %copy-start.3) | copy-done | bytes 3145752
  49.4 5.0 %shard_map.65.refs_1_.refs_8_ = bf16[4,80,1024]{2,1,0:T(8,128)(2,1)S(1)} custom-call(s32[40]{0:T(128)S(1)} %stack.187.scalars, bf16[160,3072]{1,0:T(8,128)(2,1)S(1)} %pad_maximum_fusion.refs_0_, bf16[160,3072]{1,0:T(8,128)(2,1)} %constant_dynamic-update-slice_fusion.refs_1_, bf16[6144,256]{1,0:T(8,128)(2,1)S(1)} %bitcast.95, bf16[6144,256]{1,0:T(8,128)(2,1)S(1)} %bitcast.99, ...), custom_call_target="tpu_custom_call" | custom-call | flops 1048576 | bytes 1048576 | tf_op jit(solution)/shard_map/pallas_call | solution.py:115
  54.4 4.9 %shard_map.67.refs_9_ = bf16[4,80,1024]{2,1,0:T(8,128)(2,1)S(1)} custom-call(s32[40]{0:T(128)S(1)} %stack.187.scalars, bf16[160,3072]{1,0:T(8,128)(2,1)S(1)} %collective-permute-done.10.refs_0_, bf16[160,3072]{1,0:T(8,128)(2,1)} %collective-permute-done.13.refs_1_, bf16[6144,256]{1,0:T(8,128)(2,1)S(1)} %bitcast.96, bf16[6144,256]{1,0:T(8,128)(2,1)S(1)} %bitcast.100, ...), custom_call_target="tpu_custom_call" | custom-call | flops 1048576 | bytes 1048576 | tf_op jit(solution)/shard_map/pallas_call | solution.py:115
  59.3 0.1 collective-permute-start.11
  59.4 2.0 %collective-permute-start.12 = (bf16[160,3072]{1,0:T(8,128)(2,1)}, bf16[160,3072]{1,0:T(8,128)(2,1)S(1)}, u32[]{:S(2)}, u32[]{:S(2)}) collective-permute-start(bf16[160,3072]{1,0:T(8,128)(2,1)} %collective-permute-done.8.refs_1_), channel_id=1, source_target_pairs={{0,6},{1,193},{2,0},{3,195},{4,2},{5,197},{6,4},{7,199},{64,70},{6... | collective-permute-start | bytes 2949128 | tf_op jit(solution)/shard_map/ppermute | solution.py:41
  61.4 12.1 %collective-permute-done.11.refs_2_ = bf16[160,3072]{1,0:T(8,128)(2,1)S(1)} collective-permute-done((bf16[160,3072]{1,0:T(8,128)(2,1)S(1)}, bf16[160,3072]{1,0:T(8,128)(2,1)S(1)}, u32[]{:S(2)}, u32[]{:S(2)}) %collective-permute-start.11) | collective-permute-done | bytes 983072 | tf_op jit(solution)/shard_map/ppermute | solution.py:41
  73.4 1.7 %collective-permute-done.12.refs_3_ = bf16[160,3072]{1,0:T(8,128)(2,1)S(1)} collective-permute-done((bf16[160,3072]{1,0:T(8,128)(2,1)}, bf16[160,3072]{1,0:T(8,128)(2,1)S(1)}, u32[]{:S(2)}, u32[]{:S(2)}) %collective-permute-start.12) | collective-permute-done | bytes 983072 | tf_op jit(solution)/shard_map/ppermute | solution.py:41
  75.2 7.0 %shard_map.68.sums = bf16[16,80,1024]{2,1,0:T(8,128)(2,1)S(1)} custom-call(s32[40]{0:T(128)S(1)} %stack.187.scalars, bf16[160,3072]{1,0:T(8,128)(2,1)S(1)} %collective-permute-done.7.refs_0_, bf16[160,3072]{1,0:T(8,128)(2,1)} %collective-permute-done.8.refs_1_, bf16[160,3072]{1,0:T(8,128)(2,1)S(1)} %collective-permute-done.11.refs_2_, ...), custom_call_target="tpu_custom_call" | custom-call | flops 1048576 | bytes 1048576 | tf_op jit(solution)/shard_map/pallas_call | solution.py:115
  82.2 0.1 collective-permute-start.14
  82.3 4.9 %collective-permute-done.14.got = bf16[16,80,1024]{2,1,0:T(8,128)(2,1)S(1)} collective-permute-done((bf16[16,80,1024]{2,1,0:T(8,128)(2,1)S(1)}, bf16[16,80,1024]{2,1,0:T(8,128)(2,1)S(1)}, u32[]{:S(2)}, u32[]{:S(2)}) %collective-permute-start.14) | collective-permute-done | bytes 2621472 | tf_op jit(solution)/shard_map/ppermute | solution.py:55
  87.2 3.2 %shard_map.69 = (bf16[1280,512]{1,0:T(8,128)(2,1)S(1)}, bf16[2,320,768]{2,1,0:T(8,128)(2,1)S(1)}, bf16[2,320,768]{2,1,0:T(8,128)(2,1)S(1)}) custom-call(s32[40]{0:T(128)S(1)} %stack.187.scalars, bf16[16,80,1024]{2,1,0:T(8,128)(2,1)S(1)} %shard_map.68.sums, bf16[16,80,1024]{2,1,0:T(8,128)(2,1)S(1)} %collective-permute-done.14.got, ...), custom_call_target="tpu_custom_call" | custom-call | flops 1048576 | bytes 1048576 | tf_op jit(solution)/shard_map/pallas_call | solution.py:186
  90.4 1.8 %collective-permute-start.16 = (bf16[2,320,768]{2,1,0:T(8,128)(2,1)S(1)}, bf16[2,320,768]{2,1,0:T(8,128)(2,1)S(1)}, u32[]{:S(2)}, u32[]{:S(2)}) collective-permute-start(bf16[2,320,768]{2,1,0:T(8,128)(2,1)S(1)} %get-tuple-element.19), channel_id=1, source_target_pairs={{0,64},{1,3},{2,66},{3,5},{4,68},{5,7},{6,70},{7,1},{64,128},{65,6... | collective-permute-start | bytes 2949128 | tf_op jit(solution)/shard_map/ppermute | solution.py:41
  92.2 1.5 collective-permute-start.20
  93.7 5.3 %shard_map.70 = (bf16[2,320,768]{2,1,0:T(8,128)(2,1)S(1)}, bf16[2,320,768]{2,1,0:T(8,128)(2,1)S(1)}, bf16[2,320,768]{2,1,0:T(8,128)(2,1)S(1)}, bf16[2,320,768]{2,1,0:T(8,128)(2,1)S(1)}, bf16[4,320,768]{2,1,0:T(8,128)(2,1)S(1)}) custom-call(s32[40]{0:T(128)S(1)} %stack.187.scalars, bf16[1280,512]{1,0:T(8,128)(2,1)S(1)} %get-tuple-element.15.hidden, ...), custom_call_target="tpu_custom_call" | custom-call | flops 1048576 | bytes 1048576 | tf_op jit(solution)/shard_map/pallas_call | solution.py:230
  99.0 1.4 collective-permute-start.15
  100.5 0.9 collective-permute-start.18
  101.3 4.5 %collective-permute-done.16 = bf16[2,320,768]{2,1,0:T(8,128)(2,1)S(1)} collective-permute-done((bf16[2,320,768]{2,1,0:T(8,128)(2,1)S(1)}, bf16[2,320,768]{2,1,0:T(8,128)(2,1)S(1)}, u32[]{:S(2)}, u32[]{:S(2)}) %collective-permute-start.16) | collective-permute-done | bytes 983072 | tf_op jit(solution)/shard_map/ppermute | solution.py:41
  105.8 0.2 fusion.7
  106.1 0.6 collective-permute-start.19
  106.6 0.2 fusion.9
  106.9 2.8 %collective-permute-start.21 = (bf16[320,768]{1,0:T(8,128)(2,1)S(1)}, bf16[320,768]{1,0:T(8,128)(2,1)S(1)}, u32[]{:S(2)}, u32[]{:S(2)}) collective-permute-start(bf16[320,768]{1,0:T(8,128)(2,1)S(1)} %get-tuple-element.28), channel_id=1, source_target_pairs={{0,192},{1,7},{2,194},{3,1},{4,196},{5,3},{6,198},{7,5},{64,0},{65... | collective-permute-start | bytes 1474568 | tf_op jit(solution)/shard_map/ppermute | solution.py:41
  109.7 7.1 %collective-permute-done.15.low = bf16[2,320,768]{2,1,0:T(8,128)(2,1)S(1)} collective-permute-done((bf16[2,320,768]{2,1,0:T(8,128)(2,1)S(1)}, bf16[2,320,768]{2,1,0:T(8,128)(2,1)S(1)}, u32[]{:S(2)}, u32[]{:S(2)}) %collective-permute-start.15) | collective-permute-done | bytes 983072 | tf_op jit(solution)/shard_map/ppermute | solution.py:41
  116.8 2.7 %collective-permute-start.23 = (bf16[320,768]{1,0:T(8,128)(2,1)S(1)}, bf16[320,768]{1,0:T(8,128)(2,1)S(1)}, u32[]{:S(2)}, u32[]{:S(2)}) collective-permute-start(bf16[320,768]{1,0:T(8,128)(2,1)S(1)} %get-tuple-element.27), channel_id=1, source_target_pairs={{0,192},{1,7},{2,194},{3,1},{4,196},{5,3},{6,198},{7,5},{64,0},{65... | collective-permute-start | bytes 1474568 | tf_op jit(solution)/shard_map/ppermute | solution.py:41
  119.6 2.0 %collective-permute-done.19.got_1 = bf16[320,768]{1,0:T(8,128)(2,1)S(1)} collective-permute-done((bf16[320,768]{1,0:T(8,128)(2,1)S(1)}, bf16[320,768]{1,0:T(8,128)(2,1)S(1)}, u32[]{:S(2)}, u32[]{:S(2)}) %collective-permute-start.19) | collective-permute-done | bytes 491552 | tf_op jit(solution)/shard_map/ppermute | solution.py:41
  121.6 0.5 collective-permute-done.21.got_3
  122.1 1.3 shard_map.71
  123.4 1.0 collective-permute-start.22
  124.5 2.4 %collective-permute-done.17 = bf16[320,768]{1,0:T(8,128)(2,1)S(1)} collective-permute-done((bf16[320,768]{1,0:T(8,128)(2,1)S(1)}, bf16[320,768]{1,0:T(8,128)(2,1)S(1)}, u32[]{:S(2)}, u32[]{:S(2)}) %collective-permute-start.17) | collective-permute-done | bytes 491552 | tf_op jit(solution)/shard_map/ppermute | solution.py:41
  126.9 2.7 %collective-permute-done.23 = bf16[320,768]{1,0:T(8,128)(2,1)S(1)} collective-permute-done((bf16[320,768]{1,0:T(8,128)(2,1)S(1)}, bf16[320,768]{1,0:T(8,128)(2,1)S(1)}, u32[]{:S(2)}, u32[]{:S(2)}) %collective-permute-start.23) | collective-permute-done | bytes 491552 | tf_op jit(solution)/shard_map/ppermute | solution.py:41
  129.6 1.1 fusion.2
  130.8 8.1 %collective-permute-done.22 = bf16[320,768]{1,0:T(8,128)(2,1)S(1)} collective-permute-done((bf16[320,768]{1,0:T(8,128)(2,1)}, bf16[320,768]{1,0:T(8,128)(2,1)S(1)}, u32[]{:S(2)}, u32[]{:S(2)}) %collective-permute-start.22) | collective-permute-done | bytes 491552 | tf_op jit(solution)/shard_map/ppermute | solution.py:41
  138.9 0.9 collective-permute-done.24
  139.8 1.5 shard_map.72
  141.3 10.4 %all-to-all-start = ((bf16[8,40,768]{2,1,0:T(8,128)(2,1)}), bf16[8,40,768]{2,1,0:T(8,128)(2,1)S(1)}, u32[]{:S(2)}, u32[]{:S(2)}) async-start(bf16[8,40,768]{2,1,0:T(8,128)(2,1)} %shard_map.72), calls=%async_computation | async-start | bytes 983040 | tf_op jit(solution)/shard_map/all_to_all | solution.py:348
  151.7 0.7 rev.3
  152.4 0.7 add_divide_fusion
  153.1 0.6 select_add_fusion
  153.7 14.2 %all-to-all-done = bf16[8,40,768]{2,1,0:T(8,128)(2,1)S(1)} async-done(((bf16[8,40,768]{2,1,0:T(8,128)(2,1)}), bf16[8,40,768]{2,1,0:T(8,128)(2,1)S(1)}, u32[]{:S(2)}, u32[]{:S(2)}) %all-to-all-start) | async-done | bytes 491552 | tf_op jit(solution)/shard_map/all_to_all | solution.py:348
  167.9 0.4 convolution_bitcast_fusion
  168.3 1.0 fusion.1
  (37 shorter events, 0.4 us)
Async XLA Ops:
  0.0 1.9 %copy-start = (bf16[128,6144]{1,0:T(8,128)(2,1)S(1)}, bf16[128,6144]{1,0:T(8,128)(2,1)}, u32[]{:S(2)}) copy-start(bf16[128,6144]{1,0:T(8,128)(2,1)} %param.6) | copy-start | bytes 4718596
  0.0 21.5 %collective-permute-start.2 = (bf16[6144,256]{1,0:T(8,128)(2,1)}, bf16[6144,256]{1,0:T(8,128)(2,1)}, u32[]{:S(2)}, u32[]{:S(2)}) collective-permute-start(bf16[6144,256]{1,0:T(8,128)(2,1)} %bitcast.94), channel_id=1, source_target_pairs={{0,1},{1,0},{2,3},{3,2},{4,5},{5,4},{6,7},{7,6},{8,9},{9,8},{10,11... | collective-permute-start | bytes 9437192 | tf_op jit(solution)/shard_map/ppermute | solution.py:55
  0.0 21.5 %collective-permute-start.3 = (bf16[6144,256]{1,0:T(8,128)(2,1)}, bf16[6144,256]{1,0:T(8,128)(2,1)}, u32[]{:S(2)}, u32[]{:S(2)}) collective-permute-start(bf16[6144,256]{1,0:T(8,128)(2,1)} %bitcast.98), channel_id=1, source_target_pairs={{0,1},{1,0},{2,3},{3,2},{4,5},{5,4},{6,7},{7,6},{8,9},{9,8},{10,11... | collective-permute-start | bytes 9437192 | tf_op jit(solution)/shard_map/ppermute | solution.py:55
  0.5 21.0 %collective-permute-start.4 = (bf16[256,6144]{1,0:T(8,128)(2,1)}, bf16[256,6144]{1,0:T(8,128)(2,1)}, u32[]{:S(2)}, u32[]{:S(2)}) collective-permute-start(bf16[256,6144]{1,0:T(8,128)(2,1)} %bitcast.102), channel_id=1, source_target_pairs={{0,1},{1,0},{2,3},{3,2},{4,5},{5,4},{6,7},{7,6},{8,9},{9,8},{10,11... | collective-permute-start | bytes 9437192 | tf_op jit(solution)/shard_map/ppermute | solution.py:55
  1.4 0.5 copy-start.5
  1.4 0.5 copy-start.6
  2.2 18.8 %collective-permute-start = (bf16[40,3072]{1,0:T(8,128)(2,1)S(1)}, bf16[40,3072]{1,0:T(8,128)(2,1)S(1)}, u32[]{:S(2)}, u32[]{:S(2)}) collective-permute-start(bf16[40,3072]{1,0:T(8,128)(2,1)S(1)} %convolution_convert_fusion.1), channel_id=1, source_target_pairs={{0,0},{1,1},{2,10},{3,27},{4,20},{5,21},{6,30},{7,15},{8,8},{9,9},... | collective-permute-start | bytes 737288 | tf_op jit(solution)/shard_map/ppermute | solution.py:51
  9.0 12.4 %collective-permute-start.1 = (bf16[40,3072]{1,0:T(8,128)(2,1)S(1)}, bf16[40,3072]{1,0:T(8,128)(2,1)S(1)}, u32[]{:S(2)}, u32[]{:S(2)}) collective-permute-start(bf16[40,3072]{1,0:T(8,128)(2,1)S(1)} %convolution_convert_fusion), channel_id=1, source_target_pairs={{0,32},{1,33},{2,58},{3,43},{4,52},{5,53},{6,46},{7,63},{8,40},{9,... | collective-permute-start | bytes 737288 | tf_op jit(solution)/shard_map/ppermute | solution.py:51
  21.5 10.1 %collective-permute-start.9 = (bf16[80,3072]{1,0:T(8,128)(2,1)S(1)}, bf16[80,3072]{1,0:T(8,128)(2,1)S(1)}, u32[]{:S(2)}, u32[]{:S(2)}) collective-permute-start(bf16[80,3072]{1,0:T(8,128)(2,1)S(1)} %shard_map.64), channel_id=1, source_target_pairs={{0,64},{1,3},{2,66},{3,5},{4,68},{5,7},{6,70},{7,1},{64,128},{65,6... | collective-permute-start | bytes 1474568 | tf_op jit(solution)/shard_map/ppermute | solution.py:41
  23.1 11.9 %collective-permute-start.5 = (bf16[80,3072]{1,0:T(8,128)(2,1)S(1)}, bf16[80,3072]{1,0:T(8,128)(2,1)S(1)}, u32[]{:S(2)}, u32[]{:S(2)}) collective-permute-start(bf16[80,3072]{1,0:T(8,128)(2,1)S(1)} %shard_map.64), channel_id=1, source_target_pairs={{0,192},{1,7},{2,194},{3,1},{4,196},{5,3},{6,198},{7,5},{64,0},{65... | collective-permute-start | bytes 1474568 | tf_op jit(solution)/shard_map/ppermute | solution.py:41
  24.8 15.4 %collective-permute-start.6 = (bf16[80,3072]{1,0:T(8,128)(2,1)S(1)}, bf16[80,3072]{1,0:T(8,128)(2,1)S(1)}, u32[]{:S(2)}, u32[]{:S(2)}) collective-permute-start(bf16[80,3072]{1,0:T(8,128)(2,1)S(1)} %shard_map.64), channel_id=1, source_target_pairs={{0,128},{1,5},{2,130},{3,7},{4,132},{5,1},{6,134},{7,3},{64,192},{... | collective-permute-start | bytes 1474568 | tf_op jit(solution)/shard_map/ppermute | solution.py:41
  31.7 22.6 %collective-permute-start.10 = (bf16[160,3072]{1,0:T(8,128)(2,1)S(1)}, bf16[160,3072]{1,0:T(8,128)(2,1)S(1)}, u32[]{:S(2)}, u32[]{:S(2)}) collective-permute-start(bf16[160,3072]{1,0:T(8,128)(2,1)S(1)} %pad_maximum_fusion.refs_0_), channel_id=1, source_target_pairs={{0,2},{1,65},{2,4},{3,67},{4,6},{5,69},{6,0},{7,71},{64,66},{65,12... | collective-permute-start | bytes 2949128 | tf_op jit(solution)/shard_map/ppermute | solution.py:41
  31.8 22.6 %collective-permute-start.13 = (bf16[160,3072]{1,0:T(8,128)(2,1)S(1)}, bf16[160,3072]{1,0:T(8,128)(2,1)}, u32[]{:S(2)}, u32[]{:S(2)}) collective-permute-start(bf16[160,3072]{1,0:T(8,128)(2,1)S(1)} %pad_maximum_fusion.refs_0_), channel_id=1, source_target_pairs={{0,6},{1,193},{2,0},{3,195},{4,2},{5,197},{6,4},{7,199},{64,70},{6... | collective-permute-start | bytes 2949128 | tf_op jit(solution)/shard_map/ppermute | solution.py:41
  41.1 18.3 %collective-permute-start.8 = (bf16[160,3072]{1,0:T(8,128)(2,1)}, bf16[160,3072]{1,0:T(8,128)(2,1)}, u32[]{:S(2)}, u32[]{:S(2)}) collective-permute-start(bf16[160,3072]{1,0:T(8,128)(2,1)} %constant_dynamic-update-slice_fusion.refs_1_), channel_id=1, source_target_pairs={{0,6},{1,193},{2,0},{3,195},{4,2},{5,197},{6,4},{7,199},{64,70},{6... | collective-permute-start | bytes 2949128 | tf_op jit(solution)/shard_map/ppermute | solution.py:41
  43.0 18.4 %collective-permute-start.7 = (bf16[160,3072]{1,0:T(8,128)(2,1)}, bf16[160,3072]{1,0:T(8,128)(2,1)S(1)}, u32[]{:S(2)}, u32[]{:S(2)}) collective-permute-start(bf16[160,3072]{1,0:T(8,128)(2,1)} %constant_dynamic-update-slice_fusion.refs_1_), channel_id=1, source_target_pairs={{0,2},{1,65},{2,4},{3,67},{4,6},{5,69},{6,0},{7,71},{64,66},{65,12... | collective-permute-start | bytes 2949128 | tf_op jit(solution)/shard_map/ppermute | solution.py:41
  45.6 1.9 %copy-start.1 = (bf16[1,6144,256]{2,1,0:T(8,128)(2,1)S(1)}, bf16[1,6144,256]{2,1,0:T(8,128)(2,1)}, u32[]{:S(2)}) copy-start(bf16[1,6144,256]{2,1,0:T(8,128)(2,1)} %param.9) | copy-start | bytes 9437188
  47.5 1.9 %copy-start.3 = (bf16[1,6144,256]{2,1,0:T(8,128)(2,1)S(1)}, bf16[1,6144,256]{2,1,0:T(8,128)(2,1)}, u32[]{:S(2)}) copy-start(bf16[1,6144,256]{2,1,0:T(8,128)(2,1)} %param.10) | copy-start | bytes 9437188
  49.4 5.0 %copy-start.2 = (bf16[1,6144,256]{2,1,0:T(8,128)(2,1)S(1)}, bf16[1,6144,256]{2,1,0:T(8,128)(2,1)}, u32[]{:S(2)}) copy-start(bf16[1,6144,256]{2,1,0:T(8,128)(2,1)} %param.9) | copy-start | bytes 9437188
  59.3 14.2 %collective-permute-start.11 = (bf16[160,3072]{1,0:T(8,128)(2,1)S(1)}, bf16[160,3072]{1,0:T(8,128)(2,1)S(1)}, u32[]{:S(2)}, u32[]{:S(2)}) collective-permute-start(bf16[160,3072]{1,0:T(8,128)(2,1)S(1)} %shard_map.66), channel_id=1, source_target_pairs={{0,2},{1,65},{2,4},{3,67},{4,6},{5,69},{6,0},{7,71},{64,66},{65,12... | collective-permute-start | bytes 2949128 | tf_op jit(solution)/shard_map/ppermute | solution.py:41
  59.4 15.8 %collective-permute-start.12 = (bf16[160,3072]{1,0:T(8,128)(2,1)}, bf16[160,3072]{1,0:T(8,128)(2,1)S(1)}, u32[]{:S(2)}, u32[]{:S(2)}) collective-permute-start(bf16[160,3072]{1,0:T(8,128)(2,1)} %collective-permute-done.8.refs_1_), channel_id=1, source_target_pairs={{0,6},{1,193},{2,0},{3,195},{4,2},{5,197},{6,4},{7,199},{64,70},{6... | collective-permute-start | bytes 2949128 | tf_op jit(solution)/shard_map/ppermute | solution.py:41
  75.1 12.0 %copy-start.4 = (bf16[1,256,6144]{2,1,0:T(8,128)(2,1)S(1)}, bf16[1,256,6144]{2,1,0:T(8,128)(2,1)}, u32[]{:S(2)}) copy-start(bf16[1,256,6144]{2,1,0:T(8,128)(2,1)} %param.11) | copy-start | bytes 9437188
  82.2 5.0 %collective-permute-start.14 = (bf16[16,80,1024]{2,1,0:T(8,128)(2,1)S(1)}, bf16[16,80,1024]{2,1,0:T(8,128)(2,1)S(1)}, u32[]{:S(2)}, u32[]{:S(2)}) collective-permute-start(bf16[16,80,1024]{2,1,0:T(8,128)(2,1)S(1)} %shard_map.68.sums), channel_id=1, source_target_pairs={{0,1},{1,0},{2,3},{3,2},{4,5},{5,4},{6,7},{7,6},{8,9},{9,8},{10,11... | collective-permute-start | bytes 7864328 | tf_op jit(solution)/shard_map/ppermute | solution.py:55
  90.4 15.4 %collective-permute-start.16 = (bf16[2,320,768]{2,1,0:T(8,128)(2,1)S(1)}, bf16[2,320,768]{2,1,0:T(8,128)(2,1)S(1)}, u32[]{:S(2)}, u32[]{:S(2)}) collective-permute-start(bf16[2,320,768]{2,1,0:T(8,128)(2,1)S(1)} %get-tuple-element.19), channel_id=1, source_target_pairs={{0,64},{1,3},{2,66},{3,5},{4,68},{5,7},{6,70},{7,1},{64,128},{65,6... | collective-permute-start | bytes 2949128 | tf_op jit(solution)/shard_map/ppermute | solution.py:41
  92.2 14.4 %collective-permute-start.20 = (bf16[2,320,768]{2,1,0:T(8,128)(2,1)S(1)}, bf16[2,320,768]{2,1,0:T(8,128)(2,1)S(1)}, u32[]{:S(2)}, u32[]{:S(2)}) collective-permute-start(bf16[2,320,768]{2,1,0:T(8,128)(2,1)S(1)} %get-tuple-element.22), channel_id=1, source_target_pairs={{0,192},{1,7},{2,194},{3,1},{4,196},{5,3},{6,198},{7,5},{64,0},{65... | collective-permute-start | bytes 2949128 | tf_op jit(solution)/shard_map/ppermute | solution.py:41
  99.0 17.8 %collective-permute-start.15 = (bf16[2,320,768]{2,1,0:T(8,128)(2,1)S(1)}, bf16[2,320,768]{2,1,0:T(8,128)(2,1)S(1)}, u32[]{:S(2)}, u32[]{:S(2)}) collective-permute-start(bf16[2,320,768]{2,1,0:T(8,128)(2,1)S(1)} %get-tuple-element.17), channel_id=1, source_target_pairs={{0,192},{1,7},{2,194},{3,1},{4,196},{5,3},{6,198},{7,5},{64,0},{65... | collective-permute-start | bytes 2949128 | tf_op jit(solution)/shard_map/ppermute | solution.py:41
  100.5 19.1 %collective-permute-start.18 = (bf16[2,320,768]{2,1,0:T(8,128)(2,1)S(1)}, bf16[2,320,768]{2,1,0:T(8,128)(2,1)S(1)}, u32[]{:S(2)}, u32[]{:S(2)}) collective-permute-start(bf16[2,320,768]{2,1,0:T(8,128)(2,1)S(1)} %get-tuple-element.20), channel_id=1, source_target_pairs={{0,64},{1,3},{2,66},{3,5},{4,68},{5,7},{6,70},{7,1},{64,128},{65,6... | collective-permute-start | bytes 2949128 | tf_op jit(solution)/shard_map/ppermute | solution.py:41
  106.1 15.6 %collective-permute-start.19 = (bf16[320,768]{1,0:T(8,128)(2,1)S(1)}, bf16[320,768]{1,0:T(8,128)(2,1)S(1)}, u32[]{:S(2)}, u32[]{:S(2)}) collective-permute-start(bf16[320,768]{1,0:T(8,128)(2,1)S(1)} %get-tuple-element.29), channel_id=1, source_target_pairs={{0,64},{1,3},{2,66},{3,5},{4,68},{5,7},{6,70},{7,1},{64,128},{65,6... | collective-permute-start | bytes 1474568 | tf_op jit(solution)/shard_map/ppermute | solution.py:41
  106.9 15.2 %collective-permute-start.21 = (bf16[320,768]{1,0:T(8,128)(2,1)S(1)}, bf16[320,768]{1,0:T(8,128)(2,1)S(1)}, u32[]{:S(2)}, u32[]{:S(2)}) collective-permute-start(bf16[320,768]{1,0:T(8,128)(2,1)S(1)} %get-tuple-element.28), channel_id=1, source_target_pairs={{0,192},{1,7},{2,194},{3,1},{4,196},{5,3},{6,198},{7,5},{64,0},{65... | collective-permute-start | bytes 1474568 | tf_op jit(solution)/shard_map/ppermute | solution.py:41
  109.7 17.2 %collective-permute-start.17 = (bf16[320,768]{1,0:T(8,128)(2,1)S(1)}, bf16[320,768]{1,0:T(8,128)(2,1)S(1)}, u32[]{:S(2)}, u32[]{:S(2)}) collective-permute-start(bf16[320,768]{1,0:T(8,128)(2,1)S(1)} %get-tuple-element.30), channel_id=1, source_target_pairs={{0,64},{1,3},{2,66},{3,5},{4,68},{5,7},{6,70},{7,1},{64,128},{65,6... | collective-permute-start | bytes 1474568 | tf_op jit(solution)/shard_map/ppermute | solution.py:41
  116.8 12.8 %collective-permute-start.23 = (bf16[320,768]{1,0:T(8,128)(2,1)S(1)}, bf16[320,768]{1,0:T(8,128)(2,1)S(1)}, u32[]{:S(2)}, u32[]{:S(2)}) collective-permute-start(bf16[320,768]{1,0:T(8,128)(2,1)S(1)} %get-tuple-element.27), channel_id=1, source_target_pairs={{0,192},{1,7},{2,194},{3,1},{4,196},{5,3},{6,198},{7,5},{64,0},{65... | collective-permute-start | bytes 1474568 | tf_op jit(solution)/shard_map/ppermute | solution.py:41
  123.4 15.5 %collective-permute-start.22 = (bf16[320,768]{1,0:T(8,128)(2,1)}, bf16[320,768]{1,0:T(8,128)(2,1)S(1)}, u32[]{:S(2)}, u32[]{:S(2)}) collective-permute-start(bf16[320,768]{1,0:T(8,128)(2,1)} %get-tuple-element.23), channel_id=1, source_target_pairs={{0,6},{1,193},{2,0},{3,195},{4,2},{5,197},{6,4},{7,199},{64,70},{6... | collective-permute-start | bytes 1474568 | tf_op jit(solution)/shard_map/ppermute | solution.py:41
  124.5 14.5 %collective-permute-start.25 = (bf16[320,768]{1,0:T(8,128)(2,1)}, bf16[320,768]{1,0:T(8,128)(2,1)S(1)}, u32[]{:S(2)}, u32[]{:S(2)}) collective-permute-start(bf16[320,768]{1,0:T(8,128)(2,1)} %get-tuple-element.24), channel_id=1, source_target_pairs={{0,4},{1,129},{2,6},{3,131},{4,0},{5,133},{6,2},{7,135},{64,68},{6... | collective-permute-start | bytes 1474568 | tf_op jit(solution)/shard_map/ppermute | solution.py:41
  130.7 9.0 %collective-permute-start.24 = (bf16[320,768]{1,0:T(8,128)(2,1)}, bf16[320,768]{1,0:T(8,128)(2,1)S(1)}, u32[]{:S(2)}, u32[]{:S(2)}) collective-permute-start(bf16[320,768]{1,0:T(8,128)(2,1)} %get-tuple-element.25), channel_id=1, source_target_pairs={{0,2},{1,65},{2,4},{3,67},{4,6},{5,69},{6,0},{7,71},{64,66},{65,12... | collective-permute-start | bytes 1474568 | tf_op jit(solution)/shard_map/ppermute | solution.py:41
  141.3 26.6 %all-to-all-start = ((bf16[8,40,768]{2,1,0:T(8,128)(2,1)}), bf16[8,40,768]{2,1,0:T(8,128)(2,1)S(1)}, u32[]{:S(2)}, u32[]{:S(2)}) async-start(bf16[8,40,768]{2,1,0:T(8,128)(2,1)} %shard_map.72), calls=%async_computation | async-start | bytes 983040 | tf_op jit(solution)/shard_map/all_to_all | solution.py:348

commit v4 on v3

--- a/solution.py
+++ b/solution.py
@@ -16,7 +16,6 @@
 ROUTES = ((0, 4), (1, -1), (2, -2), (3, -3))
 MIB = 2**20
 VMEM = pl.BlockSpec(memory_space=pltpu.VMEM)
-SMEM = pl.BlockSpec(memory_space=pltpu.SMEM)
 ANY = pl.BlockSpec(memory_space=pl.ANY)
 HBM = pl.BlockSpec(memory_space=pltpu.HBM)
 COST = pl.CostEstimate(flops=MIB, bytes_accessed=MIB, transcendentals=0)
@@ -67,13 +66,13 @@
     )(value, *others)
 
 
-def gate_up_kernel(places, merges, scalars, *refs):
+def gate_up_kernel(places, merges, *refs):
     pieces = len(places)
     rows, weights, before = refs[:pieces], refs[pieces : pieces + 4], refs[pieces + 4 : -6]
     out, held, weight, row_sems, sems, merge_sems = refs[-6:]
     depth, step = weight.shape[1:]
     block = out.shape[1]
-    start = pl.multiple_of(scalars[20] * depth, depth)
+    start = pl.multiple_of(lax.axis_index("core") * depth, depth)
     at, row_copies, order = 0, [], []
     for i, (ref, place) in enumerate(zip(rows, places)):
         count = ref.shape[0]
@@ -107,14 +106,14 @@
         copy.wait()
 
 
-def gate_up(rows, places, weights, scalars, before=(), merges=()):
+def gate_up(rows, places, weights, before=(), merges=()):
     count, block = sum(r.shape[0] for r in rows), 2 * CAP
     depth, step = weights[0].shape
     depth //= 2
     blocks = count // block + 2 * len(merges)
     return pl.pallas_call(
         functools.partial(gate_up_kernel, places, merges),
-        in_specs=[SMEM] + [ANY] * len(rows) + [HBM] * 4 + [ANY] * len(before),
+        in_specs=[ANY] * len(rows) + [HBM] * 4 + [ANY] * len(before),
         out_specs=VMEM,
         out_shape=jax.ShapeDtypeStruct((blocks, block, 4 * step), BF),
         scratch_shapes=[
@@ -126,14 +125,25 @@
         ],
         compiler_params=pltpu.CompilerParams(vmem_limit_bytes=20 * MIB),
         cost_estimate=COST,
-    )(scalars, *rows, *weights, *before)
-
-
-def down_copies(scalars, mine, theirs, down, sems, count=4):
+    )(*rows, *weights, *before)
+
+
+def line_at(offset, y):
+    return (y + offset + 4) & 3
+
+
+def block_at(core, y, r, v):
+    place = lambda d: jnp.where(d == 0, 0, jnp.where(d == 3, 1, d + 1))
+    first = 4 * place((v - y + 4) & 3) + r
+    return jnp.where(core == 0, first, 4 * r + place((8 - v - y) & 3))
+
+
+def down_copies(mine, theirs, down, sems, count=4):
     units, part = mine.shape[0], down.shape[2]
+    y, core = lax.axis_index("ty"), lax.axis_index("core")
     copies = []
     for k in range(count):
-        start = pl.multiple_of((2 * scalars[16 + k] + scalars[20]) * part, part)
+        start = pl.multiple_of((2 * line_at(OFFSETS[k], y) + core) * part, part)
         for side, ref in enumerate((mine, theirs)):
             copies.append(
                 pltpu.make_async_copy(
@@ -146,16 +156,18 @@
 
 
 def hidden_kernel(
-    scalars, sums, got, mine, theirs, hidden, far_a, far_b, down, sems
+    sums, got, mine, theirs, hidden, far_a, far_b, down, sems
 ):
-    copies = down_copies(scalars, mine, theirs, down, sems)
+    copies = down_copies(mine, theirs, down, sems)
     for copy in copies:
         copy.start()
     units = hidden.shape[1] // 2
     rows = hidden.shape[0] // 4
     block = rows // 4
+    y, core = lax.axis_index("ty"), lax.axis_index("core")
     for i in range(16):
-        here, there = sums[scalars[i]].astype(F32), got[scalars[24 + i]].astype(F32)
+        here = sums[block_at(core, y, i // 4, i % 4)].astype(F32)
+        there = got[block_at(1 - core, y, i // 4, i % 4)].astype(F32)
         for side in range(2):
             at, other = 2 * units * side, 2 * units * (1 - side)
             gate = here[:, at : at + units] + there[:, other : other + units]
@@ -167,37 +179,37 @@
     for copy in copies:
         copy.wait()
 
-    @pl.when(scalars[20] == 0)
+    @pl.when(lax.axis_index("core") == 0)
     def _():
         for k in range(4):
             outs[k][...] = dot(hidden[3 * rows :, :], down[k]).astype(BF)
 
-    @pl.when(scalars[20] == 1)
+    @pl.when(lax.axis_index("core") == 1)
     def _():
         value = dot(hidden[...], down[3]).astype(BF)
         for r in range(4):
             outs[r][...] = value[r * rows : (r + 1) * rows]
 
 
-def hidden_of(sums, got, mine, theirs, scalars):
+def hidden_of(sums, got, mine, theirs):
     rows, units = sums.shape[0] * sums.shape[1], 2 * mine.shape[0]
     part = mine.shape[1] // 8
     piece = jax.ShapeDtypeStruct((2, rows // 4, part), BF)
     return pl.pallas_call(
         hidden_kernel,
-        in_specs=[SMEM] + [VMEM] * 2 + [HBM] * 2,
+        in_specs=[VMEM] * 2 + [HBM] * 2,
         out_specs=[VMEM] * 3,
         out_shape=[jax.ShapeDtypeStruct((rows, units), BF), piece, piece],
         scratch_shapes=[pltpu.VMEM((4, units, part), BF), pltpu.SemaphoreType.DMA((8,))],
         compiler_params=pltpu.CompilerParams(vmem_limit_bytes=20 * MIB),
         cost_estimate=COST,
-    )(scalars, sums, got, mine, theirs)
+    )(sums, got, mine, theirs)
 
 
 def down_kernel(
-    scalars, hidden, mine, theirs, below_a, below_b, above_a, above_b, own, down, sems
+    hidden, mine, theirs, below_a, below_b, above_a, above_b, own, down, sems
 ):
-    copies = down_copies(scalars, mine, theirs, down, sems)
+    copies = down_copies(mine, theirs, down, sems)
     for copy in copies:
         copy.start()
     for copy in copies:
@@ -209,14 +221,14 @@
         (above_a.at[0], above_a.at[1], above_b.at[0], above_b.at[1]),
     )
 
-    @pl.when(scalars[20] == 0)
+    @pl.when(lax.axis_index("core") == 0)
     def _():
         for k in range(4):
             value = dot(hidden[: 3 * rows, :], down[k]).astype(BF)
             for r in range(3):
                 outs[r][k][...] = value[r * rows : (r + 1) * rows]
 
-    @pl.when(scalars[20] == 1)
+    @pl.when(lax.axis_index("core") == 1)
     def _():
         for k in range(3):
             value = dot(hidden[...], down[k]).astype(BF)
@@ -224,18 +236,18 @@
                 outs[k][r][...] = value[r * rows : (r + 1) * rows]
 
 
-def down_of(hidden, mine, theirs, scalars):
+def down_of(hidden, mine, theirs):
     rows, units = hidden.shape
     part = mine.shape[1] // 8
     return pl.pallas_call(
         down_kernel,
-        in_specs=[SMEM, VMEM, HBM, HBM],
+        in_specs=[VMEM, HBM, HBM],
         out_specs=[VMEM] * 5,
         out_shape=[jax.ShapeDtypeStruct((s, rows // 4, part), BF) for s in (2, 2, 2, 2, 4)],
         scratch_shapes=[pltpu.VMEM((4, units, part), BF), pltpu.SemaphoreType.DMA((8,))],
         compiler_params=pltpu.CompilerParams(vmem_limit_bytes=20 * MIB),
         cost_estimate=COST,
-    )(scalars, hidden, mine, theirs)
+    )(hidden, mine, theirs)
 
 
 def mid_kernel(own, high, low, got_1, got_3, mid_1, mid_3):
@@ -258,22 +270,23 @@
     )(*values)
 
 
-def last_kernel(places, a, b, c, d, out):
-    for i in range(E):
+def last_kernel(a, b, c, d, out):
+    z = lax.axis_index("expert")
+    for i, step in enumerate(sum(ROUTES, ())):
         total = a[i].astype(F32) + b[i].astype(F32) + c[i].astype(F32) + d[i].astype(F32)
-        out[places[i]] = total.astype(BF)
-
-
-def last_sum(places, parts):
+        out[(z - step + 8) & 7] = total.astype(BF)
+
+
+def last_sum(parts):
     shape = (E, CAP, parts[0].shape[1])
     return pl.pallas_call(
         last_kernel,
-        in_specs=[SMEM] + [VMEM] * 4,
+        in_specs=[VMEM] * 4,
         out_specs=VMEM,
         out_shape=jax.ShapeDtypeStruct(shape, BF),
         compiler_params=pltpu.CompilerParams(vmem_limit_bytes=16 * MIB),
         cost_estimate=COST,
-    )(places, *[p.reshape(shape) for p in parts])
+    )(*[p.reshape(shape) for p in parts])
 
 
 def body(tokens, routes, logits, w_gate, w_up, w_down):
@@ -306,33 +319,22 @@
     arrived = [along_z(outgoing(j), j) for j in range(2)]
     piece = after(jnp.concatenate(arrived, axis=0), *weights[2:], downs[1])
 
-    lines = [(y + o + 4) % 4 for o in OFFSETS]
-    at = lambda d: jnp.where(d == 0, 0, jnp.where(d == 3, 1, d + 1))
-    blocks = [
-        [4 * at((v - y + 4) % 4) + r for r in range(4) for v in range(4)],
-        [4 * r + at((8 - v - y) % 4) for r in range(4) for v in range(4)],
-    ]
-    here = [jnp.where(c == 0, p, q) for p, q in zip(*blocks)]
-    there = [jnp.where(c == 0, q, p) for p, q in zip(*blocks)]
-    scalars = jnp.stack(here + lines + [c] + [jnp.int32(0)] * 3 + there).astype(jnp.int32)
-
     low = jnp.concatenate([piece, plane(piece, 0, 1)], axis=0)
     high = jnp.concatenate([plane(piece, 0, -1), plane(piece, 0, 2)], axis=0)
     below_low, above_low = plane(low, 1, 1), plane(low, 1, -1)
     below_high, above_high = plane(high, 1, 1), plane(high, 1, -1)
-    own_sums = gate_up([low, high], (0, 2), weights, scalars)
+    own_sums = gate_up([low, high], (0, 2), weights)
     far = [plane(after(below_low, own_sums), 1, 1), plane(above_high, 1, -1)]
-    near_sums = gate_up([below_low, above_low], (0, 2), weights, scalars)
+    near_sums = gate_up([below_low, above_low], (0, 2), weights)
     sums = gate_up(
         [below_high, above_high, *far],
         (6, 10, 12, 14),
         weights,
-        scalars,
         [own_sums, near_sums],
         ((0, 0, 0), (0, 2, 2), (1, 0, 4), (1, 2, 8)),
     )
-    hidden, far_a, far_b = hidden_of(sums, swap(sums), *downs, scalars)
-    below_a, below_b, above_a, above_b, own = down_of(hidden, *downs, scalars)
+    hidden, far_a, far_b = hidden_of(sums, swap(sums), *downs)
+    below_a, below_b, above_a, above_b, own = down_of(hidden, *downs)
 
     from_below, from_above = plane(far_a, 0, 1), plane(far_b, 0, -1)
     got_high, got_low = plane(above_b, 0, 1), plane(below_a, 0, -1)
@@ -344,8 +346,7 @@
     end_3, end_1 = plane(mid_3, 1, 2), plane(mid_1, 1, -1)
     mid_0, mid_2 = add(own[0], got_low[0], got_0), add(own[2], got_high[0], got_2)
     ends = [mid_0, end_1, plane(mid_2, 1, 1), end_3]
-    places = jnp.stack([(z - step + 8) % 8 for pair in ROUTES for step in pair]).astype(jnp.int32)
-    table = lax.all_to_all(last_sum(places, ends), "expert", 0, 0, tiled=True)
+    table = lax.all_to_all(last_sum(ends), "expert", 0, 0, tiled=True)
     table = table.reshape(E * CAP, part)
 
     share = jax.nn.sigmoid(logits - logits[:, ::-1])

time: 170 us -> 164 us (0.965)
  waiting for transfers between devices: 80.7 us -> 91.4 us
  local copies, waits for them, and re-layouts: 8.59 us -> 0.9 us
  Pallas kernels: 28.2 us -> 22.7 us
  other arithmetic: 3.05 us -> 0.94 us
    ppermute x20, waiting for transfers between devices: 51.4 us -> 60.1 us  [plane(): return lax.ppermute(value, ('dp', 'ty', 'core'), pairs)]
    unnamed x15 -> x11, local copies, waits for them, and re-layouts: 4.96 us -> 0.06 us
    pallas_call x3, Pallas kernels: 16.9 us -> 14 us  [gate_up(): pl.pallas_call(functools.partial(gate_up_kernel, places, merges), in_spec...]
    all_to_all x1, starting transfers between devices: 10.4 us -> 7.74 us  [body(): table = lax.all_to_all(last_sum(ends), 'expert', 0, 0, tiled=True)]
    all_to_all x1, waiting for transfers between devices: 14.2 us -> 16.2 us  [body(): table = lax.all_to_all(last_sum(ends), 'expert', 0, 0, tiled=True)]
  transfers between devices with their start and end apart: 27 -> 27, of which waited for: 16 -> 19; matrix products, arithmetic and copies ran while one was open for 5% -> 2% of each run, Pallas kernels for 10% -> 8%
where the time goes in v4:
time: 164 us
  waiting for transfers between devices  91.4 us (56%)
  starting transfers between devices  45.4 us (28%)
  Pallas kernels  22.7 us (14%)
  matrix products  2.12 us (1%)
    ppermute x20, waiting for transfers between devices, plane(): return lax.ppermute(value, ('dp', 'ty', 'core'), pairs)  60.1 us
    ppermute x20, starting transfers between devices, plane(): return lax.ppermute(value, ('dp', 'ty', 'core'), pairs)  28.1 us
    all_to_all x1, waiting for transfers between devices, body(): table = lax.all_to_all(last_sum(ends), 'expert', 0, 0, tiled=True)  16.2 us
    pallas_call x3, Pallas kernels, gate_up(): pl.pallas_call(functools.partial(gate_up_kernel, places, merges), in_spec...  14 us
    ppermute x2, waiting for transfers between devices, along_z(): return lax.ppermute(value, ('expert', 'ty', 'core'), pairs)  10.2 us
    ppermute x2, starting transfers between devices, along_z(): return lax.ppermute(value, ('expert', 'ty', 'core'), pairs)  8.74 us
    all_to_all x1, starting transfers between devices, body(): table = lax.all_to_all(last_sum(ends), 'expert', 0, 0, tiled=True)  7.74 us
    ppermute x4, waiting for transfers between devices, swap(): return lax.ppermute(value, 'core', [(0, 1), (1, 0)])  4.9 us
  transfers between devices with their start and end apart: 27, of which 19 were waited for; matrix products, arithmetic and copies ran while one was open for 2% of the time, Pallas kernels for 8%

profile of v4, /device:TPU:24, one launch (start us, length us, event | category | flops | bytes accessed | tf_op | source)
XLA Modules:
  0.0 163.8 jit_solution(12952690954681375866)
XLA Ops:
  0.0 0.5 collective-permute-start.3
  0.5 0.1 collective-permute-start.4
  0.6 0.8 slice_bitcast_fusion.3
  1.4 0.1 fusion.22
  1.5 0.3 convolution_convert_fusion.1
  1.8 6.5 %collective-permute-start = (bf16[40,3072]{1,0:T(8,128)(2,1)S(1)}, bf16[40,3072]{1,0:T(8,128)(2,1)S(1)}, u32[]{:S(2)}, u32[]{:S(2)}) collective-permute-start(bf16[40,3072]{1,0:T(8,128)(2,1)S(1)} %convolution_convert_fusion.1), channel_id=1, source_target_pairs={{0,0},{1,1},{2,10},{3,27},{4,20},{5,21},{6,30},{7,15},{8,8},{9,9},... | collective-permute-start | bytes 737288 | tf_op jit(solution)/shard_map/ppermute | solution.py:50
  8.4 0.3 convolution_convert_fusion
  8.7 2.2 %collective-permute-start.1 = (bf16[40,3072]{1,0:T(8,128)(2,1)S(1)}, bf16[40,3072]{1,0:T(8,128)(2,1)S(1)}, u32[]{:S(2)}, u32[]{:S(2)}) collective-permute-start(bf16[40,3072]{1,0:T(8,128)(2,1)S(1)} %convolution_convert_fusion), channel_id=1, source_target_pairs={{0,32},{1,33},{2,58},{3,43},{4,52},{5,53},{6,46},{7,63},{8,40},{9,... | collective-permute-start | bytes 737288 | tf_op jit(solution)/shard_map/ppermute | solution.py:50
  10.9 9.7 %collective-permute-done = bf16[40,3072]{1,0:T(8,128)(2,1)S(1)} collective-permute-done((bf16[40,3072]{1,0:T(8,128)(2,1)S(1)}, bf16[40,3072]{1,0:T(8,128)(2,1)S(1)}, u32[]{:S(2)}, u32[]{:S(2)}) %collective-permute-start) | collective-permute-done | bytes 245792 | tf_op jit(solution)/shard_map/ppermute | solution.py:50
  20.6 0.5 collective-permute-done.1
  21.1 0.0 collective-permute-done.3.refs_2_.refs_5_.refs_7_
  21.2 0.0 copy-start.2
  21.2 0.0 copy-start.1
  21.2 1.6 collective-permute-start.9
  22.8 1.7 %collective-permute-start.5 = (bf16[80,3072]{1,0:T(8,128)(2,1)S(1)}, bf16[80,3072]{1,0:T(8,128)(2,1)S(1)}, u32[]{:S(2)}, u32[]{:S(2)}) collective-permute-start(bf16[80,3072]{1,0:T(8,128)(2,1)S(1)} %shard_map.64), channel_id=1, source_target_pairs={{0,192},{1,7},{2,194},{3,1},{4,196},{5,3},{6,198},{7,5},{64,0},{65... | collective-permute-start | bytes 1474568 | tf_op jit(solution)/shard_map/ppermute | solution.py:40
  24.5 1.8 %collective-permute-start.6 = (bf16[80,3072]{1,0:T(8,128)(2,1)S(1)}, bf16[80,3072]{1,0:T(8,128)(2,1)S(1)}, u32[]{:S(2)}, u32[]{:S(2)}) collective-permute-start(bf16[80,3072]{1,0:T(8,128)(2,1)S(1)} %shard_map.64), channel_id=1, source_target_pairs={{0,128},{1,5},{2,130},{3,7},{4,132},{5,1},{6,134},{7,3},{64,192},{... | collective-permute-start | bytes 1474568 | tf_op jit(solution)/shard_map/ppermute | solution.py:40
  26.3 5.0 %collective-permute-done.9 = bf16[80,3072]{1,0:T(8,128)(2,1)S(1)} collective-permute-done((bf16[80,3072]{1,0:T(8,128)(2,1)S(1)}, bf16[80,3072]{1,0:T(8,128)(2,1)S(1)}, u32[]{:S(2)}, u32[]{:S(2)}) %collective-permute-start.9) | collective-permute-done | bytes 491552 | tf_op jit(solution)/shard_map/ppermute | solution.py:40
  31.3 0.1 pad_maximum_fusion.refs_0_
  31.4 0.1 collective-permute-start.10
  31.5 3.1 %collective-permute-start.13 = (bf16[160,3072]{1,0:T(8,128)(2,1)S(1)}, bf16[160,3072]{1,0:T(8,128)(2,1)S(1)}, u32[]{:S(2)}, u32[]{:S(2)}) collective-permute-start(bf16[160,3072]{1,0:T(8,128)(2,1)S(1)} %pad_maximum_fusion.refs_0_), channel_id=1, source_target_pairs={{0,6},{1,193},{2,0},{3,195},{4,2},{5,197},{6,4},{7,199},{64,70},{6... | collective-permute-start | bytes 2949128 | tf_op jit(solution)/shard_map/ppermute | solution.py:40
  34.7 5.2 %collective-permute-done.6 = bf16[80,3072]{1,0:T(8,128)(2,1)S(1)} collective-permute-done((bf16[80,3072]{1,0:T(8,128)(2,1)S(1)}, bf16[80,3072]{1,0:T(8,128)(2,1)S(1)}, u32[]{:S(2)}, u32[]{:S(2)}) %collective-permute-start.6) | collective-permute-done | bytes 491552 | tf_op jit(solution)/shard_map/ppermute | solution.py:40
  39.9 0.8 collective-permute-start.8
  40.8 2.5 %collective-permute-start.7 = (bf16[160,3072]{1,0:T(8,128)(2,1)S(1)}, bf16[160,3072]{1,0:T(8,128)(2,1)S(1)}, u32[]{:S(2)}, u32[]{:S(2)}) collective-permute-start(bf16[160,3072]{1,0:T(8,128)(2,1)S(1)} %constant_dynamic-update-slice_fusion.refs_1_), channel_id=1, source_target_pairs={{0,2},{1,65},{2,4},{3,67},{4,6},{5,69},{6,0},{7,71},{64,66},{65,12... | collective-permute-start | bytes 2949128 | tf_op jit(solution)/shard_map/ppermute | solution.py:40
  43.3 3.6 %shard_map.65.refs_1_.refs_8_ = bf16[4,80,1024]{2,1,0:T(8,128)(2,1)S(1)} custom-call(bf16[160,3072]{1,0:T(8,128)(2,1)S(1)} %pad_maximum_fusion.refs_0_, bf16[160,3072]{1,0:T(8,128)(2,1)S(1)} %constant_dynamic-update-slice_fusion.refs_1_, bf16[6144,256]{1,0:T(8,128)(2,1)S(1)} %bitcast.50, bf16[6144,256]{1,0:T(8,128)(2,1)S(1)} %bitcast.54, ...), custom_call_target="tpu_custom_call" | custom-call | flops 1048576 | bytes 1048576 | tf_op jit(solution)/shard_map/pallas_call | solution.py:114
  46.9 0.8 collective-permute-done.13.refs_1_
  47.7 3.6 %shard_map.67.refs_9_ = bf16[4,80,1024]{2,1,0:T(8,128)(2,1)S(1)} custom-call(bf16[160,3072]{1,0:T(8,128)(2,1)S(1)} %collective-permute-done.10.refs_0_, bf16[160,3072]{1,0:T(8,128)(2,1)S(1)} %collective-permute-done.13.refs_1_, bf16[6144,256]{1,0:T(8,128)(2,1)S(1)} %bitcast.51, bf16[6144,256]{1,0:T(8,128)(2,1)S(1)} %bitcast.55, ...), custom_call_target="tpu_custom_call" | custom-call | flops 1048576 | bytes 1048576 | tf_op jit(solution)/shard_map/pallas_call | solution.py:114
  51.4 1.6 collective-permute-start.11
  53.0 5.3 %collective-permute-done.8.refs_1_ = bf16[160,3072]{1,0:T(8,128)(2,1)S(1)} collective-permute-done((bf16[160,3072]{1,0:T(8,128)(2,1)S(1)}, bf16[160,3072]{1,0:T(8,128)(2,1)S(1)}, u32[]{:S(2)}, u32[]{:S(2)}) %collective-permute-start.8) | collective-permute-done | bytes 983072 | tf_op jit(solution)/shard_map/ppermute | solution.py:40
  58.2 1.0 collective-permute-start.12
  59.3 8.4 %collective-permute-done.11.refs_2_ = bf16[160,3072]{1,0:T(8,128)(2,1)S(1)} collective-permute-done((bf16[160,3072]{1,0:T(8,128)(2,1)S(1)}, bf16[160,3072]{1,0:T(8,128)(2,1)S(1)}, u32[]{:S(2)}, u32[]{:S(2)}) %collective-permute-start.11) | collective-permute-done | bytes 983072 | tf_op jit(solution)/shard_map/ppermute | solution.py:40
  67.7 5.9 %collective-permute-done.12.refs_3_ = bf16[160,3072]{1,0:T(8,128)(2,1)S(1)} collective-permute-done((bf16[160,3072]{1,0:T(8,128)(2,1)S(1)}, bf16[160,3072]{1,0:T(8,128)(2,1)S(1)}, u32[]{:S(2)}, u32[]{:S(2)}) %collective-permute-start.12) | collective-permute-done | bytes 983072 | tf_op jit(solution)/shard_map/ppermute | solution.py:40
  73.5 6.7 %shard_map.68.sums = bf16[16,80,1024]{2,1,0:T(8,128)(2,1)S(1)} custom-call(bf16[160,3072]{1,0:T(8,128)(2,1)S(1)} %collective-permute-done.7.refs_0_, bf16[160,3072]{1,0:T(8,128)(2,1)S(1)} %collective-permute-done.8.refs_1_, bf16[160,3072]{1,0:T(8,128)(2,1)S(1)} %collective-permute-done.11.refs_2_, bf16[160,3072]{1,0:T(8,128)(2,1)S(1)} %collective-permute-done.12.refs_3_, ...), custom_call_target="tpu_custom_call" | custom-call | flops 1048576 | bytes 1048576 | tf_op jit(solution)/shard_map/pallas_call | solution.py:114
  80.2 0.3 collective-permute-start.14
  80.5 4.9 %collective-permute-done.14.got = bf16[16,80,1024]{2,1,0:T(8,128)(2,1)S(1)} collective-permute-done((bf16[16,80,1024]{2,1,0:T(8,128)(2,1)S(1)}, bf16[16,80,1024]{2,1,0:T(8,128)(2,1)S(1)}, u32[]{:S(2)}, u32[]{:S(2)}) %collective-permute-start.14) | collective-permute-done | bytes 2621472 | tf_op jit(solution)/shard_map/ppermute | solution.py:54
  85.4 2.7 %shard_map.69 = (bf16[1280,512]{1,0:T(8,128)(2,1)S(1)}, bf16[2,320,768]{2,1,0:T(8,128)(2,1)S(1)}, bf16[2,320,768]{2,1,0:T(8,128)(2,1)S(1)}) custom-call(bf16[16,80,1024]{2,1,0:T(8,128)(2,1)S(1)} %shard_map.68.sums, bf16[16,80,1024]{2,1,0:T(8,128)(2,1)S(1)} %collective-permute-done.14.got, bf16[256,6144]{1,0:T(8,128)(2,1)S(1)} %bitcast.58, ...), custom_call_target="tpu_custom_call" | custom-call | flops 1048576 | bytes 1048576 | tf_op jit(solution)/shard_map/pallas_call | solution.py:198
  88.1 1.6 collective-permute-start.16
  89.7 1.8 %collective-permute-start.20 = (bf16[2,320,768]{2,1,0:T(8,128)(2,1)S(1)}, bf16[2,320,768]{2,1,0:T(8,128)(2,1)S(1)}, u32[]{:S(2)}, u32[]{:S(2)}) collective-permute-start(bf16[2,320,768]{2,1,0:T(8,128)(2,1)S(1)} %get-tuple-element.22), channel_id=1, source_target_pairs={{0,192},{1,7},{2,194},{3,1},{4,196},{5,3},{6,198},{7,5},{64,0},{65... | collective-permute-start | bytes 2949128 | tf_op jit(solution)/shard_map/ppermute | solution.py:40
  91.4 4.7 %shard_map.70 = (bf16[2,320,768]{2,1,0:T(8,128)(2,1)S(1)}, bf16[2,320,768]{2,1,0:T(8,128)(2,1)S(1)}, bf16[2,320,768]{2,1,0:T(8,128)(2,1)S(1)}, bf16[2,320,768]{2,1,0:T(8,128)(2,1)S(1)}, bf16[4,320,768]{2,1,0:T(8,128)(2,1)S(1)}) custom-call(bf16[1280,512]{1,0:T(8,128)(2,1)S(1)} %get-tuple-element.15.hidden, bf16[256,6144]{1,0:T(8,128)(2,1)S(1)} %bitcast.59, ...), custom_call_target="tpu_custom_call" | custom-call | flops 1048576 | bytes 1048576 | tf_op jit(solution)/shard_map/pallas_call | solution.py:242
  96.2 1.6 collective-permute-start.15
  97.8 0.5 collective-permute-start.18
  98.3 5.2 %collective-permute-done.16 = bf16[2,320,768]{2,1,0:T(8,128)(2,1)S(1)} collective-permute-done((bf16[2,320,768]{2,1,0:T(8,128)(2,1)S(1)}, bf16[2,320,768]{2,1,0:T(8,128)(2,1)S(1)}, u32[]{:S(2)}, u32[]{:S(2)}) %collective-permute-start.16) | collective-permute-done | bytes 983072 | tf_op jit(solution)/shard_map/ppermute | solution.py:40
  103.5 0.2 fusion.7
  103.7 0.4 collective-permute-start.19
  104.1 0.2 fusion.9
  104.3 3.0 %collective-permute-start.21 = (bf16[320,768]{1,0:T(8,128)(2,1)S(1)}, bf16[320,768]{1,0:T(8,128)(2,1)S(1)}, u32[]{:S(2)}, u32[]{:S(2)}) collective-permute-start(bf16[320,768]{1,0:T(8,128)(2,1)S(1)} %get-tuple-element.28), channel_id=1, source_target_pairs={{0,192},{1,7},{2,194},{3,1},{4,196},{5,3},{6,198},{7,5},{64,0},{65... | collective-permute-start | bytes 1474568 | tf_op jit(solution)/shard_map/ppermute | solution.py:40
  107.4 6.9 %collective-permute-done.15.low = bf16[2,320,768]{2,1,0:T(8,128)(2,1)S(1)} collective-permute-done((bf16[2,320,768]{2,1,0:T(8,128)(2,1)S(1)}, bf16[2,320,768]{2,1,0:T(8,128)(2,1)S(1)}, u32[]{:S(2)}, u32[]{:S(2)}) %collective-permute-start.15) | collective-permute-done | bytes 983072 | tf_op jit(solution)/shard_map/ppermute | solution.py:40
  114.3 3.0 %collective-permute-start.23 = (bf16[320,768]{1,0:T(8,128)(2,1)S(1)}, bf16[320,768]{1,0:T(8,128)(2,1)S(1)}, u32[]{:S(2)}, u32[]{:S(2)}) collective-permute-start(bf16[320,768]{1,0:T(8,128)(2,1)S(1)} %get-tuple-element.27), channel_id=1, source_target_pairs={{0,192},{1,7},{2,194},{3,1},{4,196},{5,3},{6,198},{7,5},{64,0},{65... | collective-permute-start | bytes 1474568 | tf_op jit(solution)/shard_map/ppermute | solution.py:40
  117.3 2.0 %collective-permute-done.19.got_1 = bf16[320,768]{1,0:T(8,128)(2,1)S(1)} collective-permute-done((bf16[320,768]{1,0:T(8,128)(2,1)S(1)}, bf16[320,768]{1,0:T(8,128)(2,1)S(1)}, u32[]{:S(2)}, u32[]{:S(2)}) %collective-permute-start.19) | collective-permute-done | bytes 491552 | tf_op jit(solution)/shard_map/ppermute | solution.py:40
  119.3 0.3 collective-permute-done.21.got_3
  119.6 0.4 shard_map.71
  119.9 1.9 %collective-permute-start.22 = (bf16[320,768]{1,0:T(8,128)(2,1)S(1)}, bf16[320,768]{1,0:T(8,128)(2,1)S(1)}, u32[]{:S(2)}, u32[]{:S(2)}) collective-permute-start(bf16[320,768]{1,0:T(8,128)(2,1)S(1)} %get-tuple-element.23), channel_id=1, source_target_pairs={{0,6},{1,193},{2,0},{3,195},{4,2},{5,197},{6,4},{7,199},{64,70},{6... | collective-permute-start | bytes 1474568 | tf_op jit(solution)/shard_map/ppermute | solution.py:40
  121.9 2.7 %collective-permute-done.17 = bf16[320,768]{1,0:T(8,128)(2,1)S(1)} collective-permute-done((bf16[320,768]{1,0:T(8,128)(2,1)S(1)}, bf16[320,768]{1,0:T(8,128)(2,1)S(1)}, u32[]{:S(2)}, u32[]{:S(2)}) %collective-permute-start.17) | collective-permute-done | bytes 491552 | tf_op jit(solution)/shard_map/ppermute | solution.py:40
  124.6 3.4 %collective-permute-done.23 = bf16[320,768]{1,0:T(8,128)(2,1)S(1)} collective-permute-done((bf16[320,768]{1,0:T(8,128)(2,1)S(1)}, bf16[320,768]{1,0:T(8,128)(2,1)S(1)}, u32[]{:S(2)}, u32[]{:S(2)}) %collective-permute-start.23) | collective-permute-done | bytes 491552 | tf_op jit(solution)/shard_map/ppermute | solution.py:40
  127.9 0.4 fusion.2
  128.3 0.0 copy-start.4
  128.3 0.1 collective-permute-start.24
  128.4 1.7 %collective-permute-done.22 = bf16[320,768]{1,0:T(8,128)(2,1)S(1)} collective-permute-done((bf16[320,768]{1,0:T(8,128)(2,1)S(1)}, bf16[320,768]{1,0:T(8,128)(2,1)S(1)}, u32[]{:S(2)}, u32[]{:S(2)}) %collective-permute-start.22) | collective-permute-done | bytes 491552 | tf_op jit(solution)/shard_map/ppermute | solution.py:40
  130.1 5.3 %collective-permute-done.25 = bf16[320,768]{1,0:T(8,128)(2,1)S(1)} collective-permute-done((bf16[320,768]{1,0:T(8,128)(2,1)S(1)}, bf16[320,768]{1,0:T(8,128)(2,1)S(1)}, u32[]{:S(2)}, u32[]{:S(2)}) %collective-permute-start.25) | collective-permute-done | bytes 491552 | tf_op jit(solution)/shard_map/ppermute | solution.py:40
  135.3 2.0 %collective-permute-done.24 = bf16[320,768]{1,0:T(8,128)(2,1)S(1)} collective-permute-done((bf16[320,768]{1,0:T(8,128)(2,1)S(1)}, bf16[320,768]{1,0:T(8,128)(2,1)S(1)}, u32[]{:S(2)}, u32[]{:S(2)}) %collective-permute-start.24) | collective-permute-done | bytes 491552 | tf_op jit(solution)/shard_map/ppermute | solution.py:40
  137.3 1.0 shard_map.72
  138.3 7.7 %all-to-all-start = ((bf16[8,40,768]{2,1,0:T(8,128)(2,1)}), bf16[8,40,768]{2,1,0:T(8,128)(2,1)S(1)}, u32[]{:S(2)}, u32[]{:S(2)}) async-start(bf16[8,40,768]{2,1,0:T(8,128)(2,1)} %shard_map.72), calls=%async_computation | async-start | bytes 983040 | tf_op jit(solution)/shard_map/all_to_all | solution.py:349
  146.1 16.2 %all-to-all-done = bf16[8,40,768]{2,1,0:T(8,128)(2,1)S(1)} async-done(((bf16[8,40,768]{2,1,0:T(8,128)(2,1)}), bf16[8,40,768]{2,1,0:T(8,128)(2,1)S(1)}, u32[]{:S(2)}, u32[]{:S(2)}) %all-to-all-start) | async-done | bytes 491552 | tf_op jit(solution)/shard_map/all_to_all | solution.py:349
  162.4 0.4 convolution_bitcast_fusion
  162.7 1.0 fusion.1
  (30 shorter events, 0.2 us)
Async XLA Ops:
  0.0 1.5 copy-start
  0.0 21.1 %collective-permute-start.2 = (bf16[6144,256]{1,0:T(8,128)(2,1)}, bf16[6144,256]{1,0:T(8,128)(2,1)}, u32[]{:S(2)}, u32[]{:S(2)}) collective-permute-start(bf16[6144,256]{1,0:T(8,128)(2,1)} %bitcast.49), channel_id=1, source_target_pairs={{0,1},{1,0},{2,3},{3,2},{4,5},{5,4},{6,7},{7,6},{8,9},{9,8},{10,11... | collective-permute-start | bytes 9437192 | tf_op jit(solution)/shard_map/ppermute | solution.py:54
  0.0 21.1 %collective-permute-start.3 = (bf16[6144,256]{1,0:T(8,128)(2,1)}, bf16[6144,256]{1,0:T(8,128)(2,1)}, u32[]{:S(2)}, u32[]{:S(2)}) collective-permute-start(bf16[6144,256]{1,0:T(8,128)(2,1)} %bitcast.53), channel_id=1, source_target_pairs={{0,1},{1,0},{2,3},{3,2},{4,5},{5,4},{6,7},{7,6},{8,9},{9,8},{10,11... | collective-permute-start | bytes 9437192 | tf_op jit(solution)/shard_map/ppermute | solution.py:54
  0.5 20.6 %collective-permute-start.4 = (bf16[256,6144]{1,0:T(8,128)(2,1)}, bf16[256,6144]{1,0:T(8,128)(2,1)}, u32[]{:S(2)}, u32[]{:S(2)}) collective-permute-start(bf16[256,6144]{1,0:T(8,128)(2,1)} %bitcast.57), channel_id=1, source_target_pairs={{0,1},{1,0},{2,3},{3,2},{4,5},{5,4},{6,7},{7,6},{8,9},{9,8},{10,11... | collective-permute-start | bytes 9437192 | tf_op jit(solution)/shard_map/ppermute | solution.py:54
  1.8 18.8 %collective-permute-start = (bf16[40,3072]{1,0:T(8,128)(2,1)S(1)}, bf16[40,3072]{1,0:T(8,128)(2,1)S(1)}, u32[]{:S(2)}, u32[]{:S(2)}) collective-permute-start(bf16[40,3072]{1,0:T(8,128)(2,1)S(1)} %convolution_convert_fusion.1), channel_id=1, source_target_pairs={{0,0},{1,1},{2,10},{3,27},{4,20},{5,21},{6,30},{7,15},{8,8},{9,9},... | collective-permute-start | bytes 737288 | tf_op jit(solution)/shard_map/ppermute | solution.py:50
  8.7 12.4 %collective-permute-start.1 = (bf16[40,3072]{1,0:T(8,128)(2,1)S(1)}, bf16[40,3072]{1,0:T(8,128)(2,1)S(1)}, u32[]{:S(2)}, u32[]{:S(2)}) collective-permute-start(bf16[40,3072]{1,0:T(8,128)(2,1)S(1)} %convolution_convert_fusion), channel_id=1, source_target_pairs={{0,32},{1,33},{2,58},{3,43},{4,52},{5,53},{6,46},{7,63},{8,40},{9,... | collective-permute-start | bytes 737288 | tf_op jit(solution)/shard_map/ppermute | solution.py:50
  21.2 22.1 %copy-start.2 = (bf16[1,6144,256]{2,1,0:T(8,128)(2,1)S(1)}, bf16[1,6144,256]{2,1,0:T(8,128)(2,1)}, u32[]{:S(2)}) copy-start(bf16[1,6144,256]{2,1,0:T(8,128)(2,1)} %param.10) | copy-start | bytes 9437188
  21.2 22.1 %copy-start.1 = (bf16[1,6144,256]{2,1,0:T(8,128)(2,1)S(1)}, bf16[1,6144,256]{2,1,0:T(8,128)(2,1)}, u32[]{:S(2)}) copy-start(bf16[1,6144,256]{2,1,0:T(8,128)(2,1)} %param.9) | copy-start | bytes 9437188
  21.2 10.1 %collective-permute-start.9 = (bf16[80,3072]{1,0:T(8,128)(2,1)S(1)}, bf16[80,3072]{1,0:T(8,128)(2,1)S(1)}, u32[]{:S(2)}, u32[]{:S(2)}) collective-permute-start(bf16[80,3072]{1,0:T(8,128)(2,1)S(1)} %shard_map.64), channel_id=1, source_target_pairs={{0,64},{1,3},{2,66},{3,5},{4,68},{5,7},{6,70},{7,1},{64,128},{65,6... | collective-permute-start | bytes 1474568 | tf_op jit(solution)/shard_map/ppermute | solution.py:40
  22.8 11.9 %collective-permute-start.5 = (bf16[80,3072]{1,0:T(8,128)(2,1)S(1)}, bf16[80,3072]{1,0:T(8,128)(2,1)S(1)}, u32[]{:S(2)}, u32[]{:S(2)}) collective-permute-start(bf16[80,3072]{1,0:T(8,128)(2,1)S(1)} %shard_map.64), channel_id=1, source_target_pairs={{0,192},{1,7},{2,194},{3,1},{4,196},{5,3},{6,198},{7,5},{64,0},{65... | collective-permute-start | bytes 1474568 | tf_op jit(solution)/shard_map/ppermute | solution.py:40
  24.5 15.4 %collective-permute-start.6 = (bf16[80,3072]{1,0:T(8,128)(2,1)S(1)}, bf16[80,3072]{1,0:T(8,128)(2,1)S(1)}, u32[]{:S(2)}, u32[]{:S(2)}) collective-permute-start(bf16[80,3072]{1,0:T(8,128)(2,1)S(1)} %shard_map.64), channel_id=1, source_target_pairs={{0,128},{1,5},{2,130},{3,7},{4,132},{5,1},{6,134},{7,3},{64,192},{... | collective-permute-start | bytes 1474568 | tf_op jit(solution)/shard_map/ppermute | solution.py:40
  31.4 15.5 %collective-permute-start.10 = (bf16[160,3072]{1,0:T(8,128)(2,1)S(1)}, bf16[160,3072]{1,0:T(8,128)(2,1)S(1)}, u32[]{:S(2)}, u32[]{:S(2)}) collective-permute-start(bf16[160,3072]{1,0:T(8,128)(2,1)S(1)} %pad_maximum_fusion.refs_0_), channel_id=1, source_target_pairs={{0,2},{1,65},{2,4},{3,67},{4,6},{5,69},{6,0},{7,71},{64,66},{65,12... | collective-permute-start | bytes 2949128 | tf_op jit(solution)/shard_map/ppermute | solution.py:40
  31.5 16.2 %collective-permute-start.13 = (bf16[160,3072]{1,0:T(8,128)(2,1)S(1)}, bf16[160,3072]{1,0:T(8,128)(2,1)S(1)}, u32[]{:S(2)}, u32[]{:S(2)}) collective-permute-start(bf16[160,3072]{1,0:T(8,128)(2,1)S(1)} %pad_maximum_fusion.refs_0_), channel_id=1, source_target_pairs={{0,6},{1,193},{2,0},{3,195},{4,2},{5,197},{6,4},{7,199},{64,70},{6... | collective-permute-start | bytes 2949128 | tf_op jit(solution)/shard_map/ppermute | solution.py:40
  39.9 18.3 %collective-permute-start.8 = (bf16[160,3072]{1,0:T(8,128)(2,1)S(1)}, bf16[160,3072]{1,0:T(8,128)(2,1)S(1)}, u32[]{:S(2)}, u32[]{:S(2)}) collective-permute-start(bf16[160,3072]{1,0:T(8,128)(2,1)S(1)} %constant_dynamic-update-slice_fusion.refs_1_), channel_id=1, source_target_pairs={{0,6},{1,193},{2,0},{3,195},{4,2},{5,197},{6,4},{7,199},{64,70},{6... | collective-permute-start | bytes 2949128 | tf_op jit(solution)/shard_map/ppermute | solution.py:40
  40.8 18.5 %collective-permute-start.7 = (bf16[160,3072]{1,0:T(8,128)(2,1)S(1)}, bf16[160,3072]{1,0:T(8,128)(2,1)S(1)}, u32[]{:S(2)}, u32[]{:S(2)}) collective-permute-start(bf16[160,3072]{1,0:T(8,128)(2,1)S(1)} %constant_dynamic-update-slice_fusion.refs_1_), channel_id=1, source_target_pairs={{0,2},{1,65},{2,4},{3,67},{4,6},{5,69},{6,0},{7,71},{64,66},{65,12... | collective-permute-start | bytes 2949128 | tf_op jit(solution)/shard_map/ppermute | solution.py:40
  51.4 16.3 %collective-permute-start.11 = (bf16[160,3072]{1,0:T(8,128)(2,1)S(1)}, bf16[160,3072]{1,0:T(8,128)(2,1)S(1)}, u32[]{:S(2)}, u32[]{:S(2)}) collective-permute-start(bf16[160,3072]{1,0:T(8,128)(2,1)S(1)} %shard_map.66), channel_id=1, source_target_pairs={{0,2},{1,65},{2,4},{3,67},{4,6},{5,69},{6,0},{7,71},{64,66},{65,12... | collective-permute-start | bytes 2949128 | tf_op jit(solution)/shard_map/ppermute | solution.py:40
  58.2 15.3 %collective-permute-start.12 = (bf16[160,3072]{1,0:T(8,128)(2,1)S(1)}, bf16[160,3072]{1,0:T(8,128)(2,1)S(1)}, u32[]{:S(2)}, u32[]{:S(2)}) collective-permute-start(bf16[160,3072]{1,0:T(8,128)(2,1)S(1)} %collective-permute-done.8.refs_1_), channel_id=1, source_target_pairs={{0,6},{1,193},{2,0},{3,195},{4,2},{5,197},{6,4},{7,199},{64,70},{6... | collective-permute-start | bytes 2949128 | tf_op jit(solution)/shard_map/ppermute | solution.py:40
  73.5 11.9 %copy-start.3 = (bf16[1,256,6144]{2,1,0:T(8,128)(2,1)S(1)}, bf16[1,256,6144]{2,1,0:T(8,128)(2,1)}, u32[]{:S(2)}) copy-start(bf16[1,256,6144]{2,1,0:T(8,128)(2,1)} %param.11) | copy-start | bytes 9437188
  80.2 5.2 %collective-permute-start.14 = (bf16[16,80,1024]{2,1,0:T(8,128)(2,1)S(1)}, bf16[16,80,1024]{2,1,0:T(8,128)(2,1)S(1)}, u32[]{:S(2)}, u32[]{:S(2)}) collective-permute-start(bf16[16,80,1024]{2,1,0:T(8,128)(2,1)S(1)} %shard_map.68.sums), channel_id=1, source_target_pairs={{0,1},{1,0},{2,3},{3,2},{4,5},{5,4},{6,7},{7,6},{8,9},{9,8},{10,11... | collective-permute-start | bytes 7864328 | tf_op jit(solution)/shard_map/ppermute | solution.py:54
  88.1 15.4 %collective-permute-start.16 = (bf16[2,320,768]{2,1,0:T(8,128)(2,1)S(1)}, bf16[2,320,768]{2,1,0:T(8,128)(2,1)S(1)}, u32[]{:S(2)}, u32[]{:S(2)}) collective-permute-start(bf16[2,320,768]{2,1,0:T(8,128)(2,1)S(1)} %get-tuple-element.19), channel_id=1, source_target_pairs={{0,64},{1,3},{2,66},{3,5},{4,68},{5,7},{6,70},{7,1},{64,128},{65,6... | collective-permute-start | bytes 2949128 | tf_op jit(solution)/shard_map/ppermute | solution.py:40
  89.7 14.4 %collective-permute-start.20 = (bf16[2,320,768]{2,1,0:T(8,128)(2,1)S(1)}, bf16[2,320,768]{2,1,0:T(8,128)(2,1)S(1)}, u32[]{:S(2)}, u32[]{:S(2)}) collective-permute-start(bf16[2,320,768]{2,1,0:T(8,128)(2,1)S(1)} %get-tuple-element.22), channel_id=1, source_target_pairs={{0,192},{1,7},{2,194},{3,1},{4,196},{5,3},{6,198},{7,5},{64,0},{65... | collective-permute-start | bytes 2949128 | tf_op jit(solution)/shard_map/ppermute | solution.py:40
  96.2 18.2 %collective-permute-start.15 = (bf16[2,320,768]{2,1,0:T(8,128)(2,1)S(1)}, bf16[2,320,768]{2,1,0:T(8,128)(2,1)S(1)}, u32[]{:S(2)}, u32[]{:S(2)}) collective-permute-start(bf16[2,320,768]{2,1,0:T(8,128)(2,1)S(1)} %get-tuple-element.17), channel_id=1, source_target_pairs={{0,192},{1,7},{2,194},{3,1},{4,196},{5,3},{6,198},{7,5},{64,0},{65... | collective-permute-start | bytes 2949128 | tf_op jit(solution)/shard_map/ppermute | solution.py:40
  97.8 19.5 %collective-permute-start.18 = (bf16[2,320,768]{2,1,0:T(8,128)(2,1)S(1)}, bf16[2,320,768]{2,1,0:T(8,128)(2,1)S(1)}, u32[]{:S(2)}, u32[]{:S(2)}) collective-permute-start(bf16[2,320,768]{2,1,0:T(8,128)(2,1)S(1)} %get-tuple-element.20), channel_id=1, source_target_pairs={{0,64},{1,3},{2,66},{3,5},{4,68},{5,7},{6,70},{7,1},{64,128},{65,6... | collective-permute-start | bytes 2949128 | tf_op jit(solution)/shard_map/ppermute | solution.py:40
  103.7 15.6 %collective-permute-start.19 = (bf16[320,768]{1,0:T(8,128)(2,1)S(1)}, bf16[320,768]{1,0:T(8,128)(2,1)S(1)}, u32[]{:S(2)}, u32[]{:S(2)}) collective-permute-start(bf16[320,768]{1,0:T(8,128)(2,1)S(1)} %get-tuple-element.29), channel_id=1, source_target_pairs={{0,64},{1,3},{2,66},{3,5},{4,68},{5,7},{6,70},{7,1},{64,128},{65,6... | collective-permute-start | bytes 1474568 | tf_op jit(solution)/shard_map/ppermute | solution.py:40
  104.3 15.3 %collective-permute-start.21 = (bf16[320,768]{1,0:T(8,128)(2,1)S(1)}, bf16[320,768]{1,0:T(8,128)(2,1)S(1)}, u32[]{:S(2)}, u32[]{:S(2)}) collective-permute-start(bf16[320,768]{1,0:T(8,128)(2,1)S(1)} %get-tuple-element.28), channel_id=1, source_target_pairs={{0,192},{1,7},{2,194},{3,1},{4,196},{5,3},{6,198},{7,5},{64,0},{65... | collective-permute-start | bytes 1474568 | tf_op jit(solution)/shard_map/ppermute | solution.py:40
  107.4 17.2 %collective-permute-start.17 = (bf16[320,768]{1,0:T(8,128)(2,1)S(1)}, bf16[320,768]{1,0:T(8,128)(2,1)S(1)}, u32[]{:S(2)}, u32[]{:S(2)}) collective-permute-start(bf16[320,768]{1,0:T(8,128)(2,1)S(1)} %get-tuple-element.30), channel_id=1, source_target_pairs={{0,64},{1,3},{2,66},{3,5},{4,68},{5,7},{6,70},{7,1},{64,128},{65,6... | collective-permute-start | bytes 1474568 | tf_op jit(solution)/shard_map/ppermute | solution.py:40
  114.3 13.6 %collective-permute-start.23 = (bf16[320,768]{1,0:T(8,128)(2,1)S(1)}, bf16[320,768]{1,0:T(8,128)(2,1)S(1)}, u32[]{:S(2)}, u32[]{:S(2)}) collective-permute-start(bf16[320,768]{1,0:T(8,128)(2,1)S(1)} %get-tuple-element.27), channel_id=1, source_target_pairs={{0,192},{1,7},{2,194},{3,1},{4,196},{5,3},{6,198},{7,5},{64,0},{65... | collective-permute-start | bytes 1474568 | tf_op jit(solution)/shard_map/ppermute | solution.py:40
  119.9 10.1 %collective-permute-start.22 = (bf16[320,768]{1,0:T(8,128)(2,1)S(1)}, bf16[320,768]{1,0:T(8,128)(2,1)S(1)}, u32[]{:S(2)}, u32[]{:S(2)}) collective-permute-start(bf16[320,768]{1,0:T(8,128)(2,1)S(1)} %get-tuple-element.23), channel_id=1, source_target_pairs={{0,6},{1,193},{2,0},{3,195},{4,2},{5,197},{6,4},{7,199},{64,70},{6... | collective-permute-start | bytes 1474568 | tf_op jit(solution)/shard_map/ppermute | solution.py:40
  121.9 13.5 %collective-permute-start.25 = (bf16[320,768]{1,0:T(8,128)(2,1)S(1)}, bf16[320,768]{1,0:T(8,128)(2,1)S(1)}, u32[]{:S(2)}, u32[]{:S(2)}) collective-permute-start(bf16[320,768]{1,0:T(8,128)(2,1)S(1)} %get-tuple-element.24), channel_id=1, source_target_pairs={{0,4},{1,129},{2,6},{3,131},{4,0},{5,133},{6,2},{7,135},{64,68},{6... | collective-permute-start | bytes 1474568 | tf_op jit(solution)/shard_map/ppermute | solution.py:40
  128.3 17.8 %copy-start.4 = (f32[128,2]{0,1:T(2,128)S(1)}, f32[128,2]{0,1:T(2,128)}, u32[]{:S(2)}) copy-start(f32[128,2]{0,1:T(2,128)} %param.8) | copy-start | bytes 3076
  128.3 9.0 %collective-permute-start.24 = (bf16[320,768]{1,0:T(8,128)(2,1)S(1)}, bf16[320,768]{1,0:T(8,128)(2,1)S(1)}, u32[]{:S(2)}, u32[]{:S(2)}) collective-permute-start(bf16[320,768]{1,0:T(8,128)(2,1)S(1)} %get-tuple-element.25), channel_id=1, source_target_pairs={{0,2},{1,65},{2,4},{3,67},{4,6},{5,69},{6,0},{7,71},{64,66},{65,12... | collective-permute-start | bytes 1474568 | tf_op jit(solution)/shard_map/ppermute | solution.py:40
  138.3 24.0 %all-to-all-start = ((bf16[8,40,768]{2,1,0:T(8,128)(2,1)}), bf16[8,40,768]{2,1,0:T(8,128)(2,1)S(1)}, u32[]{:S(2)}, u32[]{:S(2)}) async-start(bf16[8,40,768]{2,1,0:T(8,128)(2,1)} %shard_map.72), calls=%async_computation | async-start | bytes 983040 | tf_op jit(solution)/shard_map/all_to_all | solution.py:349

commit v5 on v4

--- a/solution.py
+++ b/solution.py
@@ -296,7 +296,8 @@
     y, c, z = lax.axis_index("ty"), lax.axis_index("core"), lax.axis_index("expert")
 
     ids = jnp.arange(E, dtype=jnp.int32)[:, None]
-    named = (routes[:, 0][None, :] == ids) | (routes[:, 1][None, :] == ids)
+    chosen = routes.T[None, :, :] == ids[:, :, None]
+    named = jnp.any(chosen, axis=1)
     numbers = jnp.arange(rows, dtype=jnp.int32)
     earlier = (numbers[:, None] < numbers[None, :]).astype(BF)
     before = dot(named.astype(BF), earlier)
@@ -326,12 +327,13 @@
     own_sums = gate_up([low, high], (0, 2), weights)
     far = [plane(after(below_low, own_sums), 1, 1), plane(above_high, 1, -1)]
     near_sums = gate_up([below_low, above_low], (0, 2), weights)
+    more_sums = gate_up([below_high, above_high], (0, 2), weights)
     sums = gate_up(
-        [below_high, above_high, *far],
-        (6, 10, 12, 14),
+        far,
+        (12, 14),
         weights,
-        [own_sums, near_sums],
-        ((0, 0, 0), (0, 2, 2), (1, 0, 4), (1, 2, 8)),
+        [own_sums, near_sums, more_sums],
+        ((0, 0, 0), (0, 2, 2), (1, 0, 4), (1, 2, 8), (2, 0, 6), (2, 2, 10)),
     )
     hidden, far_a, far_b = hidden_of(sums, swap(sums), *downs)
     below_a, below_b, above_a, above_b, own = down_of(hidden, *downs)
@@ -350,9 +352,9 @@
     table = table.reshape(E * CAP, part)
 
     share = jax.nn.sigmoid(logits - logits[:, ::-1])
-    shares = [jnp.where(routes[:, k][None, :] == ids, share[:, k][None, :], 0.0) for k in range(2)]
+    shares = jnp.sum(jnp.where(chosen, share.T[None, :, :], 0.0), axis=1)
     hit = named[:, None, :] & (before[:, None, :] == slots[None, :, None])
-    mix = jnp.where(hit, (shares[0] + shares[1])[:, None, :], 0.0).reshape(E * CAP, rows)
+    mix = jnp.where(hit, shares[:, None, :], 0.0).reshape(E * CAP, rows)
     high_mix = mix.astype(BF)
     low_mix = (mix - high_mix.astype(F32)).astype(BF)
     back = lambda m: lax.dot_general(m, table, (((0,), (0,)), ((), ())), preferred_element_type=F32)

time: 164 us -> 161 us (0.982)
  waiting for transfers between devices: 91.4 us -> 88.5 us
    pallas_call x3 -> x4, Pallas kernels: 14 us -> 15.2 us  [gate_up(): pl.pallas_call(functools.partial(gate_up_kernel, places, merges), in_spec...]
  transfers between devices with their start and end apart: 27 -> 27, of which waited for: 19 -> 19; matrix products, arithmetic and copies ran while one was open for 2% -> 2% of each run, Pallas kernels for 8% -> 10%
where the time goes in v5:
time: 161 us
  waiting for transfers between devices  88.5 us (55%)
  starting transfers between devices  44.3 us (28%)
  Pallas kernels  24 us (15%)
  matrix products  2.12 us (1%)
  other arithmetic  1.61 us (1%)
    ppermute x20, waiting for transfers between devices, plane(): return lax.ppermute(value, ('dp', 'ty', 'core'), pairs)  58.7 us
    ppermute x20, starting transfers between devices, plane(): return lax.ppermute(value, ('dp', 'ty', 'core'), pairs)  26.5 us
    pallas_call x4, Pallas kernels, gate_up(): pl.pallas_call(functools.partial(gate_up_kernel, places, merges), in_spec...  15.2 us
    all_to_all x1, waiting for transfers between devices, body(): table = lax.all_to_all(last_sum(ends), 'expert', 0, 0, tiled=True)  14.7 us
    ppermute x2, waiting for transfers between devices, along_z(): return lax.ppermute(value, ('expert', 'ty', 'core'), pairs)  10.2 us
    ppermute x2, starting transfers between devices, along_z(): return lax.ppermute(value, ('expert', 'ty', 'core'), pairs)  8.74 us
    all_to_all x1, starting transfers between devices, body(): table = lax.all_to_all(last_sum(ends), 'expert', 0, 0, tiled=True)  8.33 us
    ppermute x4, waiting for transfers between devices, swap(): return lax.ppermute(value, 'core', [(0, 1), (1, 0)])  4.9 us
  transfers between devices with their start and end apart: 27, of which 19 were waited for; matrix products, arithmetic and copies ran while one was open for 2% of the time, Pallas kernels for 10%

profile of v5, /device:TPU:24, one launch (start us, length us, event | category | flops | bytes accessed | tf_op | source)
XLA Modules:
  0.0 160.9 jit_solution(9326671808441079759)
XLA Ops:
  0.0 0.5 collective-permute-start.3
  0.5 0.1 collective-permute-start.4
  0.6 0.7 fusion.33
  1.3 0.1 fusion.22
  1.5 0.3 convolution_convert_fusion.1
  1.8 6.5 %collective-permute-start = (bf16[40,3072]{1,0:T(8,128)(2,1)S(1)}, bf16[40,3072]{1,0:T(8,128)(2,1)S(1)}, u32[]{:S(2)}, u32[]{:S(2)}) collective-permute-start(bf16[40,3072]{1,0:T(8,128)(2,1)S(1)} %convolution_convert_fusion.1), channel_id=1, source_target_pairs={{0,0},{1,1},{2,10},{3,27},{4,20},{5,21},{6,30},{7,15},{8,8},{9,9},... | collective-permute-start | bytes 737288 | tf_op jit(solution)/shard_map/ppermute | solution.py:50
  8.3 0.3 convolution_convert_fusion
  8.6 2.2 %collective-permute-start.1 = (bf16[40,3072]{1,0:T(8,128)(2,1)S(1)}, bf16[40,3072]{1,0:T(8,128)(2,1)S(1)}, u32[]{:S(2)}, u32[]{:S(2)}) collective-permute-start(bf16[40,3072]{1,0:T(8,128)(2,1)S(1)} %convolution_convert_fusion), channel_id=1, source_target_pairs={{0,32},{1,33},{2,58},{3,43},{4,52},{5,53},{6,46},{7,63},{8,40},{9,... | collective-permute-start | bytes 737288 | tf_op jit(solution)/shard_map/ppermute | solution.py:50
  10.8 9.7 %collective-permute-done = bf16[40,3072]{1,0:T(8,128)(2,1)S(1)} collective-permute-done((bf16[40,3072]{1,0:T(8,128)(2,1)S(1)}, bf16[40,3072]{1,0:T(8,128)(2,1)S(1)}, u32[]{:S(2)}, u32[]{:S(2)}) %collective-permute-start) | collective-permute-done | bytes 245792 | tf_op jit(solution)/shard_map/ppermute | solution.py:50
  20.5 0.5 collective-permute-done.1
  21.1 0.0 copy-start.2
  21.1 1.6 collective-permute-start.5
  22.7 1.7 %collective-permute-start.7 = (bf16[80,3072]{1,0:T(8,128)(2,1)S(1)}, bf16[80,3072]{1,0:T(8,128)(2,1)S(1)}, u32[]{:S(2)}, u32[]{:S(2)}) collective-permute-start(bf16[80,3072]{1,0:T(8,128)(2,1)S(1)} %shard_map.64), channel_id=1, source_target_pairs={{0,192},{1,7},{2,194},{3,1},{4,196},{5,3},{6,198},{7,5},{64,0},{65... | collective-permute-start | bytes 1474568 | tf_op jit(solution)/shard_map/ppermute | solution.py:40
  24.4 1.8 %collective-permute-start.8 = (bf16[80,3072]{1,0:T(8,128)(2,1)S(1)}, bf16[80,3072]{1,0:T(8,128)(2,1)S(1)}, u32[]{:S(2)}, u32[]{:S(2)}) collective-permute-start(bf16[80,3072]{1,0:T(8,128)(2,1)S(1)} %shard_map.64), channel_id=1, source_target_pairs={{0,128},{1,5},{2,130},{3,7},{4,132},{5,1},{6,134},{7,3},{64,192},{... | collective-permute-start | bytes 1474568 | tf_op jit(solution)/shard_map/ppermute | solution.py:40
  26.2 5.0 %collective-permute-done.5 = bf16[80,3072]{1,0:T(8,128)(2,1)S(1)} collective-permute-done((bf16[80,3072]{1,0:T(8,128)(2,1)S(1)}, bf16[80,3072]{1,0:T(8,128)(2,1)S(1)}, u32[]{:S(2)}, u32[]{:S(2)}) %collective-permute-start.5) | collective-permute-done | bytes 491552 | tf_op jit(solution)/shard_map/ppermute | solution.py:40
  31.2 0.1 pad_maximum_fusion.refs_0_
  31.3 3.2 %collective-permute-start.12 = (bf16[160,3072]{1,0:T(8,128)(2,1)S(1)}, bf16[160,3072]{1,0:T(8,128)(2,1)S(1)}, u32[]{:S(2)}, u32[]{:S(2)}) collective-permute-start(bf16[160,3072]{1,0:T(8,128)(2,1)S(1)} %pad_maximum_fusion.refs_0_), channel_id=1, source_target_pairs={{0,6},{1,193},{2,0},{3,195},{4,2},{5,197},{6,4},{7,199},{64,70},{6... | collective-permute-start | bytes 2949128 | tf_op jit(solution)/shard_map/ppermute | solution.py:40
  34.4 0.2 collective-permute-start.6
  34.6 4.6 %collective-permute-done.8 = bf16[80,3072]{1,0:T(8,128)(2,1)S(1)} collective-permute-done((bf16[80,3072]{1,0:T(8,128)(2,1)S(1)}, bf16[80,3072]{1,0:T(8,128)(2,1)S(1)}, u32[]{:S(2)}, u32[]{:S(2)}) %collective-permute-start.8) | collective-permute-done | bytes 491552 | tf_op jit(solution)/shard_map/ppermute | solution.py:40
  39.3 1.4 collective-permute-start.10
  40.7 2.0 %collective-permute-start.13 = (bf16[160,3072]{1,0:T(8,128)(2,1)S(1)}, bf16[160,3072]{1,0:T(8,128)(2,1)S(1)}, u32[]{:S(2)}, u32[]{:S(2)}) collective-permute-start(bf16[160,3072]{1,0:T(8,128)(2,1)S(1)} %constant_dynamic-update-slice_fusion.refs_1_), channel_id=1, source_target_pairs={{0,2},{1,65},{2,4},{3,67},{4,6},{5,69},{6,0},{7,71},{64,66},{65,12... | collective-permute-start | bytes 2949128 | tf_op jit(solution)/shard_map/ppermute | solution.py:40
  42.6 3.6 %shard_map.65.refs_1_.refs_6_ = bf16[4,80,1024]{2,1,0:T(8,128)(2,1)S(1)} custom-call(bf16[160,3072]{1,0:T(8,128)(2,1)S(1)} %pad_maximum_fusion.refs_0_, bf16[160,3072]{1,0:T(8,128)(2,1)S(1)} %constant_dynamic-update-slice_fusion.refs_1_, bf16[6144,256]{1,0:T(8,128)(2,1)S(1)} %bitcast.46, bf16[6144,256]{1,0:T(8,128)(2,1)S(1)} %bitcast.51, ...), custom_call_target="tpu_custom_call" | custom-call | flops 1048576 | bytes 1048576 | tf_op jit(solution)/shard_map/pallas_call | solution.py:114
  46.3 2.1 %collective-permute-done.12.refs_1_ = bf16[160,3072]{1,0:T(8,128)(2,1)S(1)} collective-permute-done((bf16[160,3072]{1,0:T(8,128)(2,1)S(1)}, bf16[160,3072]{1,0:T(8,128)(2,1)S(1)}, u32[]{:S(2)}, u32[]{:S(2)}) %collective-permute-start.12) | collective-permute-done | bytes 983072 | tf_op jit(solution)/shard_map/ppermute | solution.py:40
  48.4 0.1 collective-permute-done.6.refs_0_
  48.5 3.6 %shard_map.67.refs_7_ = bf16[4,80,1024]{2,1,0:T(8,128)(2,1)S(1)} custom-call(bf16[160,3072]{1,0:T(8,128)(2,1)S(1)} %collective-permute-done.6.refs_0_, bf16[160,3072]{1,0:T(8,128)(2,1)S(1)} %collective-permute-done.12.refs_1_, bf16[6144,256]{1,0:T(8,128)(2,1)S(1)} %bitcast.47, bf16[6144,256]{1,0:T(8,128)(2,1)S(1)} %bitcast.52, ...), custom_call_target="tpu_custom_call" | custom-call | flops 1048576 | bytes 1048576 | tf_op jit(solution)/shard_map/pallas_call | solution.py:114
  52.2 1.5 collective-permute-start.9
  53.7 5.3 %collective-permute-done.10.refs_1_ = bf16[160,3072]{1,0:T(8,128)(2,1)S(1)} collective-permute-done((bf16[160,3072]{1,0:T(8,128)(2,1)S(1)}, bf16[160,3072]{1,0:T(8,128)(2,1)S(1)}, u32[]{:S(2)}, u32[]{:S(2)}) %collective-permute-start.10) | collective-permute-done | bytes 983072 | tf_op jit(solution)/shard_map/ppermute | solution.py:40
  59.0 0.1 collective-permute-start.11
  59.1 3.6 %shard_map.68.refs_8_ = bf16[4,80,1024]{2,1,0:T(8,128)(2,1)S(1)} custom-call(bf16[160,3072]{1,0:T(8,128)(2,1)S(1)} %collective-permute-done.13.refs_0_, bf16[160,3072]{1,0:T(8,128)(2,1)S(1)} %collective-permute-done.10.refs_1_, bf16[6144,256]{1,0:T(8,128)(2,1)S(1)} %bitcast.48, bf16[6144,256]{1,0:T(8,128)(2,1)S(1)} %bitcast.53, ...), custom_call_target="tpu_custom_call" | custom-call | flops 1048576 | bytes 1048576 | tf_op jit(solution)/shard_map/pallas_call | solution.py:114
  62.7 6.9 %collective-permute-done.9.refs_0_ = bf16[160,3072]{1,0:T(8,128)(2,1)S(1)} collective-permute-done((bf16[160,3072]{1,0:T(8,128)(2,1)S(1)}, bf16[160,3072]{1,0:T(8,128)(2,1)S(1)}, u32[]{:S(2)}, u32[]{:S(2)}) %collective-permute-start.9) | collective-permute-done | bytes 983072 | tf_op jit(solution)/shard_map/ppermute | solution.py:40
  69.6 4.7 %collective-permute-done.11.refs_1_ = bf16[160,3072]{1,0:T(8,128)(2,1)S(1)} collective-permute-done((bf16[160,3072]{1,0:T(8,128)(2,1)S(1)}, bf16[160,3072]{1,0:T(8,128)(2,1)S(1)}, u32[]{:S(2)}, u32[]{:S(2)}) %collective-permute-start.11) | collective-permute-done | bytes 983072 | tf_op jit(solution)/shard_map/ppermute | solution.py:40
  74.3 4.3 %shard_map.69.sums = bf16[16,80,1024]{2,1,0:T(8,128)(2,1)S(1)} custom-call(bf16[160,3072]{1,0:T(8,128)(2,1)S(1)} %collective-permute-done.9.refs_0_, bf16[160,3072]{1,0:T(8,128)(2,1)S(1)} %collective-permute-done.11.refs_1_, bf16[6144,256]{1,0:T(8,128)(2,1)S(1)} %bitcast.49, bf16[6144,256]{1,0:T(8,128)(2,1)S(1)} %bitcast.54, ...), custom_call_target="tpu_custom_call" | custom-call | flops 1048576 | bytes 1048576 | tf_op jit(solution)/shard_map/pallas_call | solution.py:114
  78.5 0.1 collective-permute-start.14
  78.6 4.9 %collective-permute-done.14.got = bf16[16,80,1024]{2,1,0:T(8,128)(2,1)S(1)} collective-permute-done((bf16[16,80,1024]{2,1,0:T(8,128)(2,1)S(1)}, bf16[16,80,1024]{2,1,0:T(8,128)(2,1)S(1)}, u32[]{:S(2)}, u32[]{:S(2)}) %collective-permute-start.14) | collective-permute-done | bytes 2621472 | tf_op jit(solution)/shard_map/ppermute | solution.py:54
  83.5 2.7 %shard_map.70 = (bf16[1280,512]{1,0:T(8,128)(2,1)S(1)}, bf16[2,320,768]{2,1,0:T(8,128)(2,1)S(1)}, bf16[2,320,768]{2,1,0:T(8,128)(2,1)S(1)}) custom-call(bf16[16,80,1024]{2,1,0:T(8,128)(2,1)S(1)} %shard_map.69.sums, bf16[16,80,1024]{2,1,0:T(8,128)(2,1)S(1)} %collective-permute-done.14.got, bf16[256,6144]{1,0:T(8,128)(2,1)S(1)} %bitcast.56, ...), custom_call_target="tpu_custom_call" | custom-call | flops 1048576 | bytes 1048576 | tf_op jit(solution)/shard_map/pallas_call | solution.py:198
  86.2 1.6 collective-permute-start.16
  87.8 1.7 %collective-permute-start.20 = (bf16[2,320,768]{2,1,0:T(8,128)(2,1)S(1)}, bf16[2,320,768]{2,1,0:T(8,128)(2,1)S(1)}, u32[]{:S(2)}, u32[]{:S(2)}) collective-permute-start(bf16[2,320,768]{2,1,0:T(8,128)(2,1)S(1)} %get-tuple-element.22), channel_id=1, source_target_pairs={{0,192},{1,7},{2,194},{3,1},{4,196},{5,3},{6,198},{7,5},{64,0},{65... | collective-permute-start | bytes 2949128 | tf_op jit(solution)/shard_map/ppermute | solution.py:40
  89.5 4.7 %shard_map.71 = (bf16[2,320,768]{2,1,0:T(8,128)(2,1)S(1)}, bf16[2,320,768]{2,1,0:T(8,128)(2,1)S(1)}, bf16[2,320,768]{2,1,0:T(8,128)(2,1)S(1)}, bf16[2,320,768]{2,1,0:T(8,128)(2,1)S(1)}, bf16[4,320,768]{2,1,0:T(8,128)(2,1)S(1)}) custom-call(bf16[1280,512]{1,0:T(8,128)(2,1)S(1)} %get-tuple-element.15.hidden, bf16[256,6144]{1,0:T(8,128)(2,1)S(1)} %bitcast.57, ...), custom_call_target="tpu_custom_call" | custom-call | flops 1048576 | bytes 1048576 | tf_op jit(solution)/shard_map/pallas_call | solution.py:242
  94.3 1.8 %collective-permute-start.15 = (bf16[2,320,768]{2,1,0:T(8,128)(2,1)S(1)}, bf16[2,320,768]{2,1,0:T(8,128)(2,1)S(1)}, u32[]{:S(2)}, u32[]{:S(2)}) collective-permute-start(bf16[2,320,768]{2,1,0:T(8,128)(2,1)S(1)} %get-tuple-element.17), channel_id=1, source_target_pairs={{0,192},{1,7},{2,194},{3,1},{4,196},{5,3},{6,198},{7,5},{64,0},{65... | collective-permute-start | bytes 2949128 | tf_op jit(solution)/shard_map/ppermute | solution.py:40
  96.1 0.5 collective-permute-start.18
  96.6 5.0 %collective-permute-done.16 = bf16[2,320,768]{2,1,0:T(8,128)(2,1)S(1)} collective-permute-done((bf16[2,320,768]{2,1,0:T(8,128)(2,1)S(1)}, bf16[2,320,768]{2,1,0:T(8,128)(2,1)S(1)}, u32[]{:S(2)}, u32[]{:S(2)}) %collective-permute-start.16) | collective-permute-done | bytes 983072 | tf_op jit(solution)/shard_map/ppermute | solution.py:40
  101.6 0.2 fusion.7
  101.8 0.4 collective-permute-start.19
  102.2 0.2 fusion.9
  102.4 3.0 %collective-permute-start.21 = (bf16[320,768]{1,0:T(8,128)(2,1)S(1)}, bf16[320,768]{1,0:T(8,128)(2,1)S(1)}, u32[]{:S(2)}, u32[]{:S(2)}) collective-permute-start(bf16[320,768]{1,0:T(8,128)(2,1)S(1)} %get-tuple-element.28), channel_id=1, source_target_pairs={{0,192},{1,7},{2,194},{3,1},{4,196},{5,3},{6,198},{7,5},{64,0},{65... | collective-permute-start | bytes 1474568 | tf_op jit(solution)/shard_map/ppermute | solution.py:40
  105.5 6.9 %collective-permute-done.15.low = bf16[2,320,768]{2,1,0:T(8,128)(2,1)S(1)} collective-permute-done((bf16[2,320,768]{2,1,0:T(8,128)(2,1)S(1)}, bf16[2,320,768]{2,1,0:T(8,128)(2,1)S(1)}, u32[]{:S(2)}, u32[]{:S(2)}) %collective-permute-start.15) | collective-permute-done | bytes 983072 | tf_op jit(solution)/shard_map/ppermute | solution.py:40
  112.4 3.0 %collective-permute-start.23 = (bf16[320,768]{1,0:T(8,128)(2,1)S(1)}, bf16[320,768]{1,0:T(8,128)(2,1)S(1)}, u32[]{:S(2)}, u32[]{:S(2)}) collective-permute-start(bf16[320,768]{1,0:T(8,128)(2,1)S(1)} %get-tuple-element.27), channel_id=1, source_target_pairs={{0,192},{1,7},{2,194},{3,1},{4,196},{5,3},{6,198},{7,5},{64,0},{65... | collective-permute-start | bytes 1474568 | tf_op jit(solution)/shard_map/ppermute | solution.py:40
  115.4 2.0 %collective-permute-done.19.got_1 = bf16[320,768]{1,0:T(8,128)(2,1)S(1)} collective-permute-done((bf16[320,768]{1,0:T(8,128)(2,1)S(1)}, bf16[320,768]{1,0:T(8,128)(2,1)S(1)}, u32[]{:S(2)}, u32[]{:S(2)}) %collective-permute-start.19) | collective-permute-done | bytes 491552 | tf_op jit(solution)/shard_map/ppermute | solution.py:40
  117.4 0.3 collective-permute-done.21.got_3
  117.7 0.4 shard_map.72
  118.0 0.9 collective-permute-start.22
  119.0 0.2 collective-permute-start.25
  119.1 3.5 %collective-permute-done.17 = bf16[320,768]{1,0:T(8,128)(2,1)S(1)} collective-permute-done((bf16[320,768]{1,0:T(8,128)(2,1)S(1)}, bf16[320,768]{1,0:T(8,128)(2,1)S(1)}, u32[]{:S(2)}, u32[]{:S(2)}) %collective-permute-start.17) | collective-permute-done | bytes 491552 | tf_op jit(solution)/shard_map/ppermute | solution.py:40
  122.7 3.4 %collective-permute-done.23 = bf16[320,768]{1,0:T(8,128)(2,1)S(1)} collective-permute-done((bf16[320,768]{1,0:T(8,128)(2,1)S(1)}, bf16[320,768]{1,0:T(8,128)(2,1)S(1)}, u32[]{:S(2)}, u32[]{:S(2)}) %collective-permute-start.23) | collective-permute-done | bytes 491552 | tf_op jit(solution)/shard_map/ppermute | solution.py:40
  126.0 0.4 fusion.2
  126.4 0.0 copy-start.5
  126.4 0.1 collective-permute-start.24
  126.5 6.9 %collective-permute-done.22 = bf16[320,768]{1,0:T(8,128)(2,1)S(1)} collective-permute-done((bf16[320,768]{1,0:T(8,128)(2,1)S(1)}, bf16[320,768]{1,0:T(8,128)(2,1)S(1)}, u32[]{:S(2)}, u32[]{:S(2)}) %collective-permute-start.22) | collective-permute-done | bytes 491552 | tf_op jit(solution)/shard_map/ppermute | solution.py:40
  133.4 1.9 %collective-permute-done.24 = bf16[320,768]{1,0:T(8,128)(2,1)S(1)} collective-permute-done((bf16[320,768]{1,0:T(8,128)(2,1)S(1)}, bf16[320,768]{1,0:T(8,128)(2,1)S(1)}, u32[]{:S(2)}, u32[]{:S(2)}) %collective-permute-start.24) | collective-permute-done | bytes 491552 | tf_op jit(solution)/shard_map/ppermute | solution.py:40
  135.3 1.0 shard_map.73
  136.3 8.3 %all-to-all-start = ((bf16[8,40,768]{2,1,0:T(8,128)(2,1)}), bf16[8,40,768]{2,1,0:T(8,128)(2,1)S(1)}, u32[]{:S(2)}, u32[]{:S(2)}) async-start(bf16[8,40,768]{2,1,0:T(8,128)(2,1)} %shard_map.73), calls=%async_computation | async-start | bytes 983040 | tf_op jit(solution)/shard_map/all_to_all | solution.py:351
  144.7 14.7 %all-to-all-done = bf16[8,40,768]{2,1,0:T(8,128)(2,1)S(1)} async-done(((bf16[8,40,768]{2,1,0:T(8,128)(2,1)}), bf16[8,40,768]{2,1,0:T(8,128)(2,1)S(1)}, u32[]{:S(2)}, u32[]{:S(2)}) %all-to-all-start) | async-done | bytes 491552 | tf_op jit(solution)/shard_map/all_to_all | solution.py:351
  159.5 0.4 convolution_bitcast_fusion
  159.8 1.0 fusion.1
  (31 shorter events, 0.2 us)
Async XLA Ops:
  0.0 1.5 copy-start
  0.0 21.0 %collective-permute-start.2 = (bf16[6144,256]{1,0:T(8,128)(2,1)}, bf16[6144,256]{1,0:T(8,128)(2,1)}, u32[]{:S(2)}, u32[]{:S(2)}) collective-permute-start(bf16[6144,256]{1,0:T(8,128)(2,1)} %bitcast.45), channel_id=1, source_target_pairs={{0,1},{1,0},{2,3},{3,2},{4,5},{5,4},{6,7},{7,6},{8,9},{9,8},{10,11... | collective-permute-start | bytes 9437192 | tf_op jit(solution)/shard_map/ppermute | solution.py:54
  0.0 21.0 %collective-permute-start.3 = (bf16[6144,256]{1,0:T(8,128)(2,1)}, bf16[6144,256]{1,0:T(8,128)(2,1)}, u32[]{:S(2)}, u32[]{:S(2)}) collective-permute-start(bf16[6144,256]{1,0:T(8,128)(2,1)} %bitcast.50), channel_id=1, source_target_pairs={{0,1},{1,0},{2,3},{3,2},{4,5},{5,4},{6,7},{7,6},{8,9},{9,8},{10,11... | collective-permute-start | bytes 9437192 | tf_op jit(solution)/shard_map/ppermute | solution.py:54
  0.5 20.5 %collective-permute-start.4 = (bf16[256,6144]{1,0:T(8,128)(2,1)}, bf16[256,6144]{1,0:T(8,128)(2,1)}, u32[]{:S(2)}, u32[]{:S(2)}) collective-permute-start(bf16[256,6144]{1,0:T(8,128)(2,1)} %bitcast.55), channel_id=1, source_target_pairs={{0,1},{1,0},{2,3},{3,2},{4,5},{5,4},{6,7},{7,6},{8,9},{9,8},{10,11... | collective-permute-start | bytes 9437192 | tf_op jit(solution)/shard_map/ppermute | solution.py:54
  1.8 18.8 %collective-permute-start = (bf16[40,3072]{1,0:T(8,128)(2,1)S(1)}, bf16[40,3072]{1,0:T(8,128)(2,1)S(1)}, u32[]{:S(2)}, u32[]{:S(2)}) collective-permute-start(bf16[40,3072]{1,0:T(8,128)(2,1)S(1)} %convolution_convert_fusion.1), channel_id=1, source_target_pairs={{0,0},{1,1},{2,10},{3,27},{4,20},{5,21},{6,30},{7,15},{8,8},{9,9},... | collective-permute-start | bytes 737288 | tf_op jit(solution)/shard_map/ppermute | solution.py:50
  8.6 12.4 %collective-permute-start.1 = (bf16[40,3072]{1,0:T(8,128)(2,1)S(1)}, bf16[40,3072]{1,0:T(8,128)(2,1)S(1)}, u32[]{:S(2)}, u32[]{:S(2)}) collective-permute-start(bf16[40,3072]{1,0:T(8,128)(2,1)S(1)} %convolution_convert_fusion), channel_id=1, source_target_pairs={{0,32},{1,33},{2,58},{3,43},{4,52},{5,53},{6,46},{7,63},{8,40},{9,... | collective-permute-start | bytes 737288 | tf_op jit(solution)/shard_map/ppermute | solution.py:50
  21.1 21.5 %copy-start.2 = (bf16[1,6144,256]{2,1,0:T(8,128)(2,1)S(1)}, bf16[1,6144,256]{2,1,0:T(8,128)(2,1)}, u32[]{:S(2)}) copy-start(bf16[1,6144,256]{2,1,0:T(8,128)(2,1)} %param.10) | copy-start | bytes 9437188
  21.1 21.5 %copy-start.1 = (bf16[1,6144,256]{2,1,0:T(8,128)(2,1)S(1)}, bf16[1,6144,256]{2,1,0:T(8,128)(2,1)}, u32[]{:S(2)}) copy-start(bf16[1,6144,256]{2,1,0:T(8,128)(2,1)} %param.9) | copy-start | bytes 9437188
  21.1 10.1 %collective-permute-start.5 = (bf16[80,3072]{1,0:T(8,128)(2,1)S(1)}, bf16[80,3072]{1,0:T(8,128)(2,1)S(1)}, u32[]{:S(2)}, u32[]{:S(2)}) collective-permute-start(bf16[80,3072]{1,0:T(8,128)(2,1)S(1)} %shard_map.64), channel_id=1, source_target_pairs={{0,64},{1,3},{2,66},{3,5},{4,68},{5,7},{6,70},{7,1},{64,128},{65,6... | collective-permute-start | bytes 1474568 | tf_op jit(solution)/shard_map/ppermute | solution.py:40
  22.7 11.9 %collective-permute-start.7 = (bf16[80,3072]{1,0:T(8,128)(2,1)S(1)}, bf16[80,3072]{1,0:T(8,128)(2,1)S(1)}, u32[]{:S(2)}, u32[]{:S(2)}) collective-permute-start(bf16[80,3072]{1,0:T(8,128)(2,1)S(1)} %shard_map.64), channel_id=1, source_target_pairs={{0,192},{1,7},{2,194},{3,1},{4,196},{5,3},{6,198},{7,5},{64,0},{65... | collective-permute-start | bytes 1474568 | tf_op jit(solution)/shard_map/ppermute | solution.py:40
  24.4 14.8 %collective-permute-start.8 = (bf16[80,3072]{1,0:T(8,128)(2,1)S(1)}, bf16[80,3072]{1,0:T(8,128)(2,1)S(1)}, u32[]{:S(2)}, u32[]{:S(2)}) collective-permute-start(bf16[80,3072]{1,0:T(8,128)(2,1)S(1)} %shard_map.64), channel_id=1, source_target_pairs={{0,128},{1,5},{2,130},{3,7},{4,132},{5,1},{6,134},{7,3},{64,192},{... | collective-permute-start | bytes 1474568 | tf_op jit(solution)/shard_map/ppermute | solution.py:40
  31.3 17.1 %collective-permute-start.12 = (bf16[160,3072]{1,0:T(8,128)(2,1)S(1)}, bf16[160,3072]{1,0:T(8,128)(2,1)S(1)}, u32[]{:S(2)}, u32[]{:S(2)}) collective-permute-start(bf16[160,3072]{1,0:T(8,128)(2,1)S(1)} %pad_maximum_fusion.refs_0_), channel_id=1, source_target_pairs={{0,6},{1,193},{2,0},{3,195},{4,2},{5,197},{6,4},{7,199},{64,70},{6... | collective-permute-start | bytes 2949128 | tf_op jit(solution)/shard_map/ppermute | solution.py:40
  34.4 14.1 %collective-permute-start.6 = (bf16[160,3072]{1,0:T(8,128)(2,1)S(1)}, bf16[160,3072]{1,0:T(8,128)(2,1)S(1)}, u32[]{:S(2)}, u32[]{:S(2)}) collective-permute-start(bf16[160,3072]{1,0:T(8,128)(2,1)S(1)} %pad_maximum_fusion.refs_0_), channel_id=1, source_target_pairs={{0,2},{1,65},{2,4},{3,67},{4,6},{5,69},{6,0},{7,71},{64,66},{65,12... | collective-permute-start | bytes 2949128 | tf_op jit(solution)/shard_map/ppermute | solution.py:40
  39.3 19.6 %collective-permute-start.10 = (bf16[160,3072]{1,0:T(8,128)(2,1)S(1)}, bf16[160,3072]{1,0:T(8,128)(2,1)S(1)}, u32[]{:S(2)}, u32[]{:S(2)}) collective-permute-start(bf16[160,3072]{1,0:T(8,128)(2,1)S(1)} %constant_dynamic-update-slice_fusion.refs_1_), channel_id=1, source_target_pairs={{0,6},{1,193},{2,0},{3,195},{4,2},{5,197},{6,4},{7,199},{64,70},{6... | collective-permute-start | bytes 2949128 | tf_op jit(solution)/shard_map/ppermute | solution.py:40
  40.7 18.4 %collective-permute-start.13 = (bf16[160,3072]{1,0:T(8,128)(2,1)S(1)}, bf16[160,3072]{1,0:T(8,128)(2,1)S(1)}, u32[]{:S(2)}, u32[]{:S(2)}) collective-permute-start(bf16[160,3072]{1,0:T(8,128)(2,1)S(1)} %constant_dynamic-update-slice_fusion.refs_1_), channel_id=1, source_target_pairs={{0,2},{1,65},{2,4},{3,67},{4,6},{5,69},{6,0},{7,71},{64,66},{65,12... | collective-permute-start | bytes 2949128 | tf_op jit(solution)/shard_map/ppermute | solution.py:40
  52.2 17.4 %collective-permute-start.9 = (bf16[160,3072]{1,0:T(8,128)(2,1)S(1)}, bf16[160,3072]{1,0:T(8,128)(2,1)S(1)}, u32[]{:S(2)}, u32[]{:S(2)}) collective-permute-start(bf16[160,3072]{1,0:T(8,128)(2,1)S(1)} %shard_map.66), channel_id=1, source_target_pairs={{0,2},{1,65},{2,4},{3,67},{4,6},{5,69},{6,0},{7,71},{64,66},{65,12... | collective-permute-start | bytes 2949128 | tf_op jit(solution)/shard_map/ppermute | solution.py:40
  59.0 15.3 %collective-permute-start.11 = (bf16[160,3072]{1,0:T(8,128)(2,1)S(1)}, bf16[160,3072]{1,0:T(8,128)(2,1)S(1)}, u32[]{:S(2)}, u32[]{:S(2)}) collective-permute-start(bf16[160,3072]{1,0:T(8,128)(2,1)S(1)} %collective-permute-done.10.refs_1_), channel_id=1, source_target_pairs={{0,6},{1,193},{2,0},{3,195},{4,2},{5,197},{6,4},{7,199},{64,70},{6... | collective-permute-start | bytes 2949128 | tf_op jit(solution)/shard_map/ppermute | solution.py:40
  74.3 9.3 %copy-start.3 = (bf16[1,256,6144]{2,1,0:T(8,128)(2,1)S(1)}, bf16[1,256,6144]{2,1,0:T(8,128)(2,1)}, u32[]{:S(2)}) copy-start(bf16[1,256,6144]{2,1,0:T(8,128)(2,1)} %param.11) | copy-start | bytes 9437188
  78.5 5.0 %collective-permute-start.14 = (bf16[16,80,1024]{2,1,0:T(8,128)(2,1)S(1)}, bf16[16,80,1024]{2,1,0:T(8,128)(2,1)S(1)}, u32[]{:S(2)}, u32[]{:S(2)}) collective-permute-start(bf16[16,80,1024]{2,1,0:T(8,128)(2,1)S(1)} %shard_map.69.sums), channel_id=1, source_target_pairs={{0,1},{1,0},{2,3},{3,2},{4,5},{5,4},{6,7},{7,6},{8,9},{9,8},{10,11... | collective-permute-start | bytes 7864328 | tf_op jit(solution)/shard_map/ppermute | solution.py:54
  86.2 15.4 %collective-permute-start.16 = (bf16[2,320,768]{2,1,0:T(8,128)(2,1)S(1)}, bf16[2,320,768]{2,1,0:T(8,128)(2,1)S(1)}, u32[]{:S(2)}, u32[]{:S(2)}) collective-permute-start(bf16[2,320,768]{2,1,0:T(8,128)(2,1)S(1)} %get-tuple-element.19), channel_id=1, source_target_pairs={{0,64},{1,3},{2,66},{3,5},{4,68},{5,7},{6,70},{7,1},{64,128},{65,6... | collective-permute-start | bytes 2949128 | tf_op jit(solution)/shard_map/ppermute | solution.py:40
  87.8 14.4 %collective-permute-start.20 = (bf16[2,320,768]{2,1,0:T(8,128)(2,1)S(1)}, bf16[2,320,768]{2,1,0:T(8,128)(2,1)S(1)}, u32[]{:S(2)}, u32[]{:S(2)}) collective-permute-start(bf16[2,320,768]{2,1,0:T(8,128)(2,1)S(1)} %get-tuple-element.22), channel_id=1, source_target_pairs={{0,192},{1,7},{2,194},{3,1},{4,196},{5,3},{6,198},{7,5},{64,0},{65... | collective-permute-start | bytes 2949128 | tf_op jit(solution)/shard_map/ppermute | solution.py:40
  94.3 18.2 %collective-permute-start.15 = (bf16[2,320,768]{2,1,0:T(8,128)(2,1)S(1)}, bf16[2,320,768]{2,1,0:T(8,128)(2,1)S(1)}, u32[]{:S(2)}, u32[]{:S(2)}) collective-permute-start(bf16[2,320,768]{2,1,0:T(8,128)(2,1)S(1)} %get-tuple-element.17), channel_id=1, source_target_pairs={{0,192},{1,7},{2,194},{3,1},{4,196},{5,3},{6,198},{7,5},{64,0},{65... | collective-permute-start | bytes 2949128 | tf_op jit(solution)/shard_map/ppermute | solution.py:40
  96.1 19.3 %collective-permute-start.18 = (bf16[2,320,768]{2,1,0:T(8,128)(2,1)S(1)}, bf16[2,320,768]{2,1,0:T(8,128)(2,1)S(1)}, u32[]{:S(2)}, u32[]{:S(2)}) collective-permute-start(bf16[2,320,768]{2,1,0:T(8,128)(2,1)S(1)} %get-tuple-element.20), channel_id=1, source_target_pairs={{0,64},{1,3},{2,66},{3,5},{4,68},{5,7},{6,70},{7,1},{64,128},{65,6... | collective-permute-start | bytes 2949128 | tf_op jit(solution)/shard_map/ppermute | solution.py:40
  101.8 15.6 %collective-permute-start.19 = (bf16[320,768]{1,0:T(8,128)(2,1)S(1)}, bf16[320,768]{1,0:T(8,128)(2,1)S(1)}, u32[]{:S(2)}, u32[]{:S(2)}) collective-permute-start(bf16[320,768]{1,0:T(8,128)(2,1)S(1)} %get-tuple-element.29), channel_id=1, source_target_pairs={{0,64},{1,3},{2,66},{3,5},{4,68},{5,7},{6,70},{7,1},{64,128},{65,6... | collective-permute-start | bytes 1474568 | tf_op jit(solution)/shard_map/ppermute | solution.py:40
  102.4 15.3 %collective-permute-start.21 = (bf16[320,768]{1,0:T(8,128)(2,1)S(1)}, bf16[320,768]{1,0:T(8,128)(2,1)S(1)}, u32[]{:S(2)}, u32[]{:S(2)}) collective-permute-start(bf16[320,768]{1,0:T(8,128)(2,1)S(1)} %get-tuple-element.28), channel_id=1, source_target_pairs={{0,192},{1,7},{2,194},{3,1},{4,196},{5,3},{6,198},{7,5},{64,0},{65... | collective-permute-start | bytes 1474568 | tf_op jit(solution)/shard_map/ppermute | solution.py:40
  105.5 17.2 %collective-permute-start.17 = (bf16[320,768]{1,0:T(8,128)(2,1)S(1)}, bf16[320,768]{1,0:T(8,128)(2,1)S(1)}, u32[]{:S(2)}, u32[]{:S(2)}) collective-permute-start(bf16[320,768]{1,0:T(8,128)(2,1)S(1)} %get-tuple-element.30), channel_id=1, source_target_pairs={{0,64},{1,3},{2,66},{3,5},{4,68},{5,7},{6,70},{7,1},{64,128},{65,6... | collective-permute-start | bytes 1474568 | tf_op jit(solution)/shard_map/ppermute | solution.py:40
  112.4 13.6 %collective-permute-start.23 = (bf16[320,768]{1,0:T(8,128)(2,1)S(1)}, bf16[320,768]{1,0:T(8,128)(2,1)S(1)}, u32[]{:S(2)}, u32[]{:S(2)}) collective-permute-start(bf16[320,768]{1,0:T(8,128)(2,1)S(1)} %get-tuple-element.27), channel_id=1, source_target_pairs={{0,192},{1,7},{2,194},{3,1},{4,196},{5,3},{6,198},{7,5},{64,0},{65... | collective-permute-start | bytes 1474568 | tf_op jit(solution)/shard_map/ppermute | solution.py:40
  118.0 15.4 %collective-permute-start.22 = (bf16[320,768]{1,0:T(8,128)(2,1)S(1)}, bf16[320,768]{1,0:T(8,128)(2,1)S(1)}, u32[]{:S(2)}, u32[]{:S(2)}) collective-permute-start(bf16[320,768]{1,0:T(8,128)(2,1)S(1)} %get-tuple-element.23), channel_id=1, source_target_pairs={{0,6},{1,193},{2,0},{3,195},{4,2},{5,197},{6,4},{7,199},{64,70},{6... | collective-permute-start | bytes 1474568 | tf_op jit(solution)/shard_map/ppermute | solution.py:40
  119.0 14.5 %collective-permute-start.25 = (bf16[320,768]{1,0:T(8,128)(2,1)S(1)}, bf16[320,768]{1,0:T(8,128)(2,1)S(1)}, u32[]{:S(2)}, u32[]{:S(2)}) collective-permute-start(bf16[320,768]{1,0:T(8,128)(2,1)S(1)} %get-tuple-element.24), channel_id=1, source_target_pairs={{0,4},{1,129},{2,6},{3,131},{4,0},{5,133},{6,2},{7,135},{64,68},{6... | collective-permute-start | bytes 1474568 | tf_op jit(solution)/shard_map/ppermute | solution.py:40
  126.4 18.3 %copy-start.4 = (f32[128,2]{0,1:T(2,128)S(1)}, f32[128,2]{0,1:T(2,128)}, u32[]{:S(2)}) copy-start(f32[128,2]{0,1:T(2,128)} %param.8) | copy-start | bytes 3076
  126.4 18.3 %copy-start.5 = (s32[128,2]{0,1:T(2,128)S(1)}, s32[128,2]{0,1:T(2,128)}, u32[]{:S(2)}) copy-start(s32[128,2]{0,1:T(2,128)} %param.7) | copy-start | bytes 3076
  126.4 8.9 %collective-permute-start.24 = (bf16[320,768]{1,0:T(8,128)(2,1)S(1)}, bf16[320,768]{1,0:T(8,128)(2,1)S(1)}, u32[]{:S(2)}, u32[]{:S(2)}) collective-permute-start(bf16[320,768]{1,0:T(8,128)(2,1)S(1)} %get-tuple-element.25), channel_id=1, source_target_pairs={{0,2},{1,65},{2,4},{3,67},{4,6},{5,69},{6,0},{7,71},{64,66},{65,12... | collective-permute-start | bytes 1474568 | tf_op jit(solution)/shard_map/ppermute | solution.py:40
  136.3 23.1 %all-to-all-start = ((bf16[8,40,768]{2,1,0:T(8,128)(2,1)}), bf16[8,40,768]{2,1,0:T(8,128)(2,1)S(1)}, u32[]{:S(2)}, u32[]{:S(2)}) async-start(bf16[8,40,768]{2,1,0:T(8,128)(2,1)} %shard_map.73), calls=%async_computation | async-start | bytes 983040 | tf_op jit(solution)/shard_map/all_to_all | solution.py:351
